TPU v7x, 32 devices: a whole 2x2x4 slice. The times are simulated.
32 devices in a mesh: row: 8 (over z, core), col: 4 (over y, x).
Axes of the slice: x: 2, y: 2, z: 4, core: 2. Of those that a mesh axis runs over, the one named last changes fastest.
Arguments:
- rhs: float32 [16, 64, 128], P('col'), may hold values from -6 to 6
- diag_inv: float32 [16, 128, 128], P('col'), as said below
- panel: bfloat16 [16, 16, 128, 128], P('row', 'col'), may hold values from -0.09375 to 0.09375
- offdiag: bfloat16 [512, 16, 128, 128], P('row', 'col'), may hold values from -0.0234375 to 0.0234375
- known: bfloat16 [64, 64, 128], P(('row', 'col')), may hold values from -6 to 6
- row_index: int32 [512], P('row'), may hold values from 0 to 7
Outputs:
- solution: bfloat16 [16, 64, 128], P('col')
Inputs may be any that keep to these rules, and one draw needn't show every extreme that they name: Each block of diag_inv is lower triangular (the inverse of a lower triangular diagonal block).
All inputs are finite; a program needn't handle non-finite values.
Results may differ from a plain program's by a relative error of at most 0.015.
Values may be sent and summed in bfloat16 or wider, within the bound.
No kernel may reach another device: no remote copies, remote signals or barrier semaphores. Data moves between devices by JAX's collectives and lax.ppermute only.
A program may use at most 64 MiB of HBM per device.

v0:
```python
import jax
import jax.numpy as jnp
from jax import lax
from jax.sharding import PartitionSpec as P

NB = 16


def spread(array, axis, root):
    mine = lax.axis_index(axis) == root
    return lax.psum(jnp.where(mine, array, jnp.zeros_like(array)), axis)


def finish_block(total, inverse, turn_block, root, solved):
    local = jnp.dot(
        total, inverse, precision=lax.Precision.HIGHEST, preferred_element_type=jnp.float32
    ).astype(jnp.bfloat16)
    block = spread(local, "col", root)
    solved = lax.dynamic_update_index_in_dim(solved, block, turn_block, 0)
    return (block, solved)


def body(rhs, diag_inv, panel, offdiag, known, row_index):
    rows_count = lax.axis_size("row")
    cols_count = lax.axis_size("col")
    row_id = lax.axis_index("row")
    col_id = lax.axis_index("col")
    col_slots = NB // cols_count
    known_row = lax.all_gather(known, "col", axis=0, tiled=True)
    picked = jnp.take(known_row, row_index, axis=0)
    off_part = jnp.einsum("pqi,pbia->bqa", picked, offdiag, preferred_element_type=jnp.float32)
    off_sum = lax.psum(off_part, "row")
    update = rhs - off_sum
    col_global = jnp.arange(col_slots) * cols_count + col_id
    accum = jnp.zeros(update.shape, jnp.float32)
    solved = jnp.zeros((NB,) + update.shape[1:], jnp.bfloat16)

    def step_reduced(turn, carry):
        sums, result = carry
        block_id = NB - 1 - turn
        slot = block_id // cols_count
        partial_value = lax.dynamic_index_in_dim(sums, slot, 0, keepdims=False)
        summed = lax.psum(partial_value.astype(jnp.bfloat16), "row").astype(jnp.float32)
        total = lax.dynamic_index_in_dim(update, slot, 0, keepdims=False) - summed
        inverse = lax.dynamic_index_in_dim(diag_inv, slot, 0, keepdims=False)
        block, result = finish_block(total, inverse, block_id, block_id % cols_count, result)
        tiles = lax.dynamic_index_in_dim(panel, block_id // rows_count, 0, keepdims=False)
        contrib = jnp.einsum("qi,bia->bqa", block, tiles, preferred_element_type=jnp.float32)
        keep = (col_global < block_id) & (block_id % rows_count == row_id)
        return (sums + jnp.where(keep[:, None, None], contrib, 0.0), result)

    accum, solved = lax.fori_loop(0, NB, step_reduced, (accum, solved))
    return jnp.take(solved, col_global, axis=0)


def solution(mesh):
    placed = (
        P("col", None, None),
        P("col", None, None),
        P("row", "col", None, None),
        P("row", "col", None, None),
        P(("row", "col"), None, None),
        P("row"),
    )
    return jax.shard_map(
        body, mesh=mesh, in_specs=placed, out_specs=P("col", None, None), check_vma=False
    )
```

profile of v0, /device:TPU:0, one launch (start us, length us, event | category | flops | bytes accessed | tf_op | source)
XLA Modules:
  0.0 758.1 jit_solution(1539131164149741869)
XLA Ops:
  6.5 0.7 compare_select_fusion.1
  7.2 0.7 compare_and_fusion.1
  7.9 10.1 %all_gather.3 = bf16[8,64,128]{2,1,0:T(8,128)(2,1)S(1)} all-gather(bf16[2,64,128]{2,1,0:T(8,128)(2,1)} %param.12), channel_id=1, replica_groups=mesh['row'=8,'col'=4] {'col'}, dimensions={0}, use_global_device_ids=true | all-gather | bytes 163840 | tf_op jit(solution)/shard_map/all_gather | solution.py:29
  18.0 0.7 gather_fusion
  18.8 5.7 convolution_bitcast_fusion
  24.5 54.5 %all-reduce.2.cloned.1.call-done = f32[4,64,128]{2,1,0:T(8,128)} async-done(((f32[4,64,128]{2,1,0:T(8,128)}), f32[4,64,128]{2,1,0:T(8,128)}) %all-reduce.2.cloned.1.call-update) | async-done | bytes 131088 | tf_op jit(solution)/shard_map/psum | solution.py:32
  79.1 0.9 sub.36
  80.1 669.9 %while.19 = (s32[]{:T(128)}, f32[4,64,128]{2,1,0:T(8,128)S(1)}, bf16[16,64,128]{2,1,0:T(8,128)(2,1)S(1)}, s32[]{:T(128)}, bf16[2,4,128,128]{3,2,1,0:T(8,128)(2,1...) while((s32[]{:T(128)}, f32[4,64,128]{2,1,0:T(8,128)S(1)}, ...), condition=%wide.region_4.5_spmd.clone, body=%wide.region_1.0_spmd.clone.sunk | while | flops 21119040 | bytes 936614 | solution.py:52
  80.1 25.9 %psum.42 = bf16[64,128]{1,0:T(8,128)(2,1)S(1)} all-reduce(bf16[64,128]{1,0:T(8,128)(2,1)S(1)} %fusion.31), channel_id=1, replica_groups=mesh['row'=8,'col'=4] {'row'}, use_global_device_ids=true, to_apply=%region_2.2 | all-reduce | flops 8192 | bytes 32768 | tf_op jit(solution)/shard_map/while/body/eval_jaxpr/psum | solution.py:43
  106.1 1.0 fusion.32
  107.1 16.0 %psum.43 = bf16[64,128]{1,0:T(8,128)(2,1)S(1)} all-reduce(bf16[64,128]{1,0:T(8,128)(2,1)S(1)} %fusion.32), channel_id=1, replica_groups=mesh['row'=8,'col'=4] {'col'}, use_global_device_ids=true, to_apply=%region_3.3 | all-reduce | flops 8192 | bytes 32768 | tf_op jit(solution)/shard_map/while/body/eval_jaxpr/psum | solution.py:11
  123.1 0.2 fusion.33
  123.4 25.9 %psum.42 = bf16[64,128]{1,0:T(8,128)(2,1)S(1)} all-reduce(bf16[64,128]{1,0:T(8,128)(2,1)S(1)} %fusion.31), channel_id=1, replica_groups=mesh['row'=8,'col'=4] {'row'}, use_global_device_ids=true, to_apply=%region_2.2 | all-reduce | flops 8192 | bytes 32768 | tf_op jit(solution)/shard_map/while/body/eval_jaxpr/psum | solution.py:43
  149.3 1.0 fusion.32
  150.3 13.7 %psum.43 = bf16[64,128]{1,0:T(8,128)(2,1)S(1)} all-reduce(bf16[64,128]{1,0:T(8,128)(2,1)S(1)} %fusion.32), channel_id=1, replica_groups=mesh['row'=8,'col'=4] {'col'}, use_global_device_ids=true, to_apply=%region_3.3 | all-reduce | flops 8192 | bytes 32768 | tf_op jit(solution)/shard_map/while/body/eval_jaxpr/psum | solution.py:11
  164.4 25.9 %psum.42 = bf16[64,128]{1,0:T(8,128)(2,1)S(1)} all-reduce(bf16[64,128]{1,0:T(8,128)(2,1)S(1)} %fusion.31), channel_id=1, replica_groups=mesh['row'=8,'col'=4] {'row'}, use_global_device_ids=true, to_apply=%region_2.2 | all-reduce | flops 8192 | bytes 32768 | tf_op jit(solution)/shard_map/while/body/eval_jaxpr/psum | solution.py:43
  190.3 1.0 fusion.32
  191.3 15.4 %psum.43 = bf16[64,128]{1,0:T(8,128)(2,1)S(1)} all-reduce(bf16[64,128]{1,0:T(8,128)(2,1)S(1)} %fusion.32), channel_id=1, replica_groups=mesh['row'=8,'col'=4] {'col'}, use_global_device_ids=true, to_apply=%region_3.3 | all-reduce | flops 8192 | bytes 32768 | tf_op jit(solution)/shard_map/while/body/eval_jaxpr/psum | solution.py:11
  206.8 0.2 fusion.33
  207.0 25.9 %psum.42 = bf16[64,128]{1,0:T(8,128)(2,1)S(1)} all-reduce(bf16[64,128]{1,0:T(8,128)(2,1)S(1)} %fusion.31), channel_id=1, replica_groups=mesh['row'=8,'col'=4] {'row'}, use_global_device_ids=true, to_apply=%region_2.2 | all-reduce | flops 8192 | bytes 32768 | tf_op jit(solution)/shard_map/while/body/eval_jaxpr/psum | solution.py:43
  233.0 1.0 fusion.32
  234.0 13.7 %psum.43 = bf16[64,128]{1,0:T(8,128)(2,1)S(1)} all-reduce(bf16[64,128]{1,0:T(8,128)(2,1)S(1)} %fusion.32), channel_id=1, replica_groups=mesh['row'=8,'col'=4] {'col'}, use_global_device_ids=true, to_apply=%region_3.3 | all-reduce | flops 8192 | bytes 32768 | tf_op jit(solution)/shard_map/while/body/eval_jaxpr/psum | solution.py:11
  248.0 25.9 %psum.42 = bf16[64,128]{1,0:T(8,128)(2,1)S(1)} all-reduce(bf16[64,128]{1,0:T(8,128)(2,1)S(1)} %fusion.31), channel_id=1, replica_groups=mesh['row'=8,'col'=4] {'row'}, use_global_device_ids=true, to_apply=%region_2.2 | all-reduce | flops 8192 | bytes 32768 | tf_op jit(solution)/shard_map/while/body/eval_jaxpr/psum | solution.py:43
  274.0 1.0 fusion.32
  275.0 15.4 %psum.43 = bf16[64,128]{1,0:T(8,128)(2,1)S(1)} all-reduce(bf16[64,128]{1,0:T(8,128)(2,1)S(1)} %fusion.32), channel_id=1, replica_groups=mesh['row'=8,'col'=4] {'col'}, use_global_device_ids=true, to_apply=%region_3.3 | all-reduce | flops 8192 | bytes 32768 | tf_op jit(solution)/shard_map/while/body/eval_jaxpr/psum | solution.py:11
  290.7 25.9 %psum.42 = bf16[64,128]{1,0:T(8,128)(2,1)S(1)} all-reduce(bf16[64,128]{1,0:T(8,128)(2,1)S(1)} %fusion.31), channel_id=1, replica_groups=mesh['row'=8,'col'=4] {'row'}, use_global_device_ids=true, to_apply=%region_2.2 | all-reduce | flops 8192 | bytes 32768 | tf_op jit(solution)/shard_map/while/body/eval_jaxpr/psum | solution.py:43
  316.6 1.0 fusion.32
  317.7 13.8 %psum.43 = bf16[64,128]{1,0:T(8,128)(2,1)S(1)} all-reduce(bf16[64,128]{1,0:T(8,128)(2,1)S(1)} %fusion.32), channel_id=1, replica_groups=mesh['row'=8,'col'=4] {'col'}, use_global_device_ids=true, to_apply=%region_3.3 | all-reduce | flops 8192 | bytes 32768 | tf_op jit(solution)/shard_map/while/body/eval_jaxpr/psum | solution.py:11
  331.7 25.9 %psum.42 = bf16[64,128]{1,0:T(8,128)(2,1)S(1)} all-reduce(bf16[64,128]{1,0:T(8,128)(2,1)S(1)} %fusion.31), channel_id=1, replica_groups=mesh['row'=8,'col'=4] {'row'}, use_global_device_ids=true, to_apply=%region_2.2 | all-reduce | flops 8192 | bytes 32768 | tf_op jit(solution)/shard_map/while/body/eval_jaxpr/psum | solution.py:43
  357.6 1.0 fusion.32
  358.7 15.4 %psum.43 = bf16[64,128]{1,0:T(8,128)(2,1)S(1)} all-reduce(bf16[64,128]{1,0:T(8,128)(2,1)S(1)} %fusion.32), channel_id=1, replica_groups=mesh['row'=8,'col'=4] {'col'}, use_global_device_ids=true, to_apply=%region_3.3 | all-reduce | flops 8192 | bytes 32768 | tf_op jit(solution)/shard_map/while/body/eval_jaxpr/psum | solution.py:11
  374.4 25.9 %psum.42 = bf16[64,128]{1,0:T(8,128)(2,1)S(1)} all-reduce(bf16[64,128]{1,0:T(8,128)(2,1)S(1)} %fusion.31), channel_id=1, replica_groups=mesh['row'=8,'col'=4] {'row'}, use_global_device_ids=true, to_apply=%region_2.2 | all-reduce | flops 8192 | bytes 32768 | tf_op jit(solution)/shard_map/while/body/eval_jaxpr/psum | solution.py:43
  400.3 1.0 fusion.32
  401.3 13.8 %psum.43 = bf16[64,128]{1,0:T(8,128)(2,1)S(1)} all-reduce(bf16[64,128]{1,0:T(8,128)(2,1)S(1)} %fusion.32), channel_id=1, replica_groups=mesh['row'=8,'col'=4] {'col'}, use_global_device_ids=true, to_apply=%region_3.3 | all-reduce | flops 8192 | bytes 32768 | tf_op jit(solution)/shard_map/while/body/eval_jaxpr/psum | solution.py:11
  415.1 0.2 fusion.33
  415.4 25.9 %psum.42 = bf16[64,128]{1,0:T(8,128)(2,1)S(1)} all-reduce(bf16[64,128]{1,0:T(8,128)(2,1)S(1)} %fusion.31), channel_id=1, replica_groups=mesh['row'=8,'col'=4] {'row'}, use_global_device_ids=true, to_apply=%region_2.2 | all-reduce | flops 8192 | bytes 32768 | tf_op jit(solution)/shard_map/while/body/eval_jaxpr/psum | solution.py:43
  441.3 1.0 fusion.32
  442.3 15.4 %psum.43 = bf16[64,128]{1,0:T(8,128)(2,1)S(1)} all-reduce(bf16[64,128]{1,0:T(8,128)(2,1)S(1)} %fusion.32), channel_id=1, replica_groups=mesh['row'=8,'col'=4] {'col'}, use_global_device_ids=true, to_apply=%region_3.3 | all-reduce | flops 8192 | bytes 32768 | tf_op jit(solution)/shard_map/while/body/eval_jaxpr/psum | solution.py:11
  457.8 0.2 fusion.33
  458.0 25.9 %psum.42 = bf16[64,128]{1,0:T(8,128)(2,1)S(1)} all-reduce(bf16[64,128]{1,0:T(8,128)(2,1)S(1)} %fusion.31), channel_id=1, replica_groups=mesh['row'=8,'col'=4] {'row'}, use_global_device_ids=true, to_apply=%region_2.2 | all-reduce | flops 8192 | bytes 32768 | tf_op jit(solution)/shard_map/while/body/eval_jaxpr/psum | solution.py:43
  483.9 1.0 fusion.32
  485.0 13.8 %psum.43 = bf16[64,128]{1,0:T(8,128)(2,1)S(1)} all-reduce(bf16[64,128]{1,0:T(8,128)(2,1)S(1)} %fusion.32), channel_id=1, replica_groups=mesh['row'=8,'col'=4] {'col'}, use_global_device_ids=true, to_apply=%region_3.3 | all-reduce | flops 8192 | bytes 32768 | tf_op jit(solution)/shard_map/while/body/eval_jaxpr/psum | solution.py:11
  499.0 25.9 %psum.42 = bf16[64,128]{1,0:T(8,128)(2,1)S(1)} all-reduce(bf16[64,128]{1,0:T(8,128)(2,1)S(1)} %fusion.31), channel_id=1, replica_groups=mesh['row'=8,'col'=4] {'row'}, use_global_device_ids=true, to_apply=%region_2.2 | all-reduce | flops 8192 | bytes 32768 | tf_op jit(solution)/shard_map/while/body/eval_jaxpr/psum | solution.py:43
  525.0 1.0 fusion.32
  526.0 15.4 %psum.43 = bf16[64,128]{1,0:T(8,128)(2,1)S(1)} all-reduce(bf16[64,128]{1,0:T(8,128)(2,1)S(1)} %fusion.32), channel_id=1, replica_groups=mesh['row'=8,'col'=4] {'col'}, use_global_device_ids=true, to_apply=%region_3.3 | all-reduce | flops 8192 | bytes 32768 | tf_op jit(solution)/shard_map/while/body/eval_jaxpr/psum | solution.py:11
  541.7 25.9 %psum.42 = bf16[64,128]{1,0:T(8,128)(2,1)S(1)} all-reduce(bf16[64,128]{1,0:T(8,128)(2,1)S(1)} %fusion.31), channel_id=1, replica_groups=mesh['row'=8,'col'=4] {'row'}, use_global_device_ids=true, to_apply=%region_2.2 | all-reduce | flops 8192 | bytes 32768 | tf_op jit(solution)/shard_map/while/body/eval_jaxpr/psum | solution.py:43
  567.6 1.0 fusion.32
  568.6 13.8 %psum.43 = bf16[64,128]{1,0:T(8,128)(2,1)S(1)} all-reduce(bf16[64,128]{1,0:T(8,128)(2,1)S(1)} %fusion.32), channel_id=1, replica_groups=mesh['row'=8,'col'=4] {'col'}, use_global_device_ids=true, to_apply=%region_3.3 | all-reduce | flops 8192 | bytes 32768 | tf_op jit(solution)/shard_map/while/body/eval_jaxpr/psum | solution.py:11
  582.7 25.9 %psum.42 = bf16[64,128]{1,0:T(8,128)(2,1)S(1)} all-reduce(bf16[64,128]{1,0:T(8,128)(2,1)S(1)} %fusion.31), channel_id=1, replica_groups=mesh['row'=8,'col'=4] {'row'}, use_global_device_ids=true, to_apply=%region_2.2 | all-reduce | flops 8192 | bytes 32768 | tf_op jit(solution)/shard_map/while/body/eval_jaxpr/psum | solution.py:43
  608.6 1.0 fusion.32
  609.7 15.4 %psum.43 = bf16[64,128]{1,0:T(8,128)(2,1)S(1)} all-reduce(bf16[64,128]{1,0:T(8,128)(2,1)S(1)} %fusion.32), channel_id=1, replica_groups=mesh['row'=8,'col'=4] {'col'}, use_global_device_ids=true, to_apply=%region_3.3 | all-reduce | flops 8192 | bytes 32768 | tf_op jit(solution)/shard_map/while/body/eval_jaxpr/psum | solution.py:11
  625.1 0.2 fusion.33
  625.3 25.9 %psum.42 = bf16[64,128]{1,0:T(8,128)(2,1)S(1)} all-reduce(bf16[64,128]{1,0:T(8,128)(2,1)S(1)} %fusion.31), channel_id=1, replica_groups=mesh['row'=8,'col'=4] {'row'}, use_global_device_ids=true, to_apply=%region_2.2 | all-reduce | flops 8192 | bytes 32768 | tf_op jit(solution)/shard_map/while/body/eval_jaxpr/psum | solution.py:43
  651.3 1.0 fusion.32
  652.3 13.8 %psum.43 = bf16[64,128]{1,0:T(8,128)(2,1)S(1)} all-reduce(bf16[64,128]{1,0:T(8,128)(2,1)S(1)} %fusion.32), channel_id=1, replica_groups=mesh['row'=8,'col'=4] {'col'}, use_global_device_ids=true, to_apply=%region_3.3 | all-reduce | flops 8192 | bytes 32768 | tf_op jit(solution)/shard_map/while/body/eval_jaxpr/psum | solution.py:11
  666.4 25.9 %psum.42 = bf16[64,128]{1,0:T(8,128)(2,1)S(1)} all-reduce(bf16[64,128]{1,0:T(8,128)(2,1)S(1)} %fusion.31), channel_id=1, replica_groups=mesh['row'=8,'col'=4] {'row'}, use_global_device_ids=true, to_apply=%region_2.2 | all-reduce | flops 8192 | bytes 32768 | tf_op jit(solution)/shard_map/while/body/eval_jaxpr/psum | solution.py:43
  692.3 1.0 fusion.32
  693.3 15.4 %psum.43 = bf16[64,128]{1,0:T(8,128)(2,1)S(1)} all-reduce(bf16[64,128]{1,0:T(8,128)(2,1)S(1)} %fusion.32), channel_id=1, replica_groups=mesh['row'=8,'col'=4] {'col'}, use_global_device_ids=true, to_apply=%region_3.3 | all-reduce | flops 8192 | bytes 32768 | tf_op jit(solution)/shard_map/while/body/eval_jaxpr/psum | solution.py:11
  709.0 25.9 %psum.42 = bf16[64,128]{1,0:T(8,128)(2,1)S(1)} all-reduce(bf16[64,128]{1,0:T(8,128)(2,1)S(1)} %fusion.31), channel_id=1, replica_groups=mesh['row'=8,'col'=4] {'row'}, use_global_device_ids=true, to_apply=%region_2.2 | all-reduce | flops 8192 | bytes 32768 | tf_op jit(solution)/shard_map/while/body/eval_jaxpr/psum | solution.py:43
  734.9 1.0 fusion.32
  736.0 13.8 %psum.43 = bf16[64,128]{1,0:T(8,128)(2,1)S(1)} all-reduce(bf16[64,128]{1,0:T(8,128)(2,1)S(1)} %fusion.32), channel_id=1, replica_groups=mesh['row'=8,'col'=4] {'col'}, use_global_device_ids=true, to_apply=%region_3.3 | all-reduce | flops 8192 | bytes 32768 | tf_op jit(solution)/shard_map/while/body/eval_jaxpr/psum | solution.py:11
  749.8 0.2 fusion.33
  750.0 0.6 gather_fusion.1
  750.5 0.7 broadcast_select_fusion.1
  (86 shorter events, 2.5 us)
Async XLA Ops:
  6.5 72.5 %copy-start.1 = (f32[4,64,128]{2,1,0:T(8,128)S(1)}, f32[4,64,128]{2,1,0:T(8,128)}, u32[]{:S(2)}) copy-start(f32[4,64,128]{2,1,0:T(8,128)} %param.8) | copy-start | bytes 393220
  6.5 73.5 %copy-start = (bf16[2,4,128,128]{3,2,1,0:T(8,128)(2,1)S(1)}, bf16[2,4,128,128]{3,2,1,0:T(8,128)(2,1)}, u32[]{:S(2)}) copy-start(bf16[2,4,128,128]{3,2,1,0:T(8,128)(2,1)} %param.10) | copy-start | bytes 786436
  6.5 72.5 %all-reduce.2.cloned.1.call-start = ((), (), s32[]{:S(2)}) async-start(), calls=%async_computation | async-start | bytes 262144 | tf_op jit(solution)/shard_map/psum | solution.py:32
Sparse Core Ops, SparseCore 0:
  24.6 54.4 all-reduce.1
where the time goes:
time: 760 us; the launch traced here: 758 us
  blocking collectives  659 us (87%)
  waiting for transfers between devices  54.6 us (7%)
  matrix products  24.6 us (3%)
  between operations  13.5 us (2%)
    psum x16, blocking collectives, step_reduced(): lax.psum(partial_value.astype(jnp.bfloat16), 'row').astype(jnp.float32)  415 us
    psum x16, blocking collectives, spread(): return lax.psum(jnp.where(mine, array, jnp.zeros_like(array)), axis)  234 us
    psum x1, waiting for transfers between devices, body(): off_sum = lax.psum(off_part, 'row')  54.5 us
    dot_general x16, matrix products, finish_block(): jnp.dot(total, inverse, precision=lax.Precision.HIGHEST, preferred_elemen...  16.4 us
  transfers between devices with their start and end apart: 1, of which 1 were waited for; matrix products, arithmetic and copies ran while one was open for 0% of the time, Pallas kernels for 0%

commit v1 on v0

v1 whole, which is shorter than its diff:
```python
import functools

import jax
import jax.numpy as jnp
from jax import lax
from jax.experimental import pallas as pl
from jax.experimental.pallas import tpu as pltpu
from jax.sharding import PartitionSpec as P

NB = 16
AXES = ("row", "col")
VMEM_LIMIT = 48 * 1024 * 1024
HIGHEST = lax.Precision.HIGHEST


def tile_slots(rows, cols):
    return [
        (a, b)
        for a in reversed(range(NB // rows))
        for b in reversed(range(NB // cols))
        if a * rows + rows - 1 > b * cols
    ]


def send(array, rows, cols, target):
    pairs = []
    for r in range(rows):
        for c in range(cols):
            to_r, to_c = target(r, c)
            pairs.append((r * cols + c, to_r * cols + to_c))
    return lax.ppermute(array, AXES, pairs)


def along_z(array, rows, cols, step):
    return send(array, rows, cols, lambda r, c: ((r + 2 * step) % rows, c))


def along_col(array, rows, cols, step):
    return send(array, rows, cols, lambda r, c: (r, (c + step) % cols))


def other_core(array, rows, cols):
    return send(array, rows, cols, lambda r, c: (r ^ 1, c))


def fold_kernel(slots, panel_ref, inverse_ref, out_ref):
    for at, (a, b) in enumerate(slots):
        inverse = inverse_ref[b]
        high = inverse.astype(jnp.bfloat16)
        low = (inverse - high.astype(jnp.float32)).astype(jnp.bfloat16)
        tile = panel_ref[a, b]
        out_ref[at] = (
            jnp.dot(tile, high, preferred_element_type=jnp.float32)
            + jnp.dot(tile, low, preferred_element_type=jnp.float32)
        ).astype(jnp.bfloat16)


def fold_panel(panel, inverse, slots):
    bs = panel.shape[-1]
    return pl.pallas_call(
        functools.partial(fold_kernel, slots),
        out_shape=jax.ShapeDtypeStruct((len(slots), bs, bs), jnp.bfloat16),
        compiler_params=pltpu.CompilerParams(vmem_limit_bytes=VMEM_LIMIT),
        name="fold_panel",
    )(panel, inverse)


def segment_kernel(chunk, index_ref, tiles_ref, out_ref, sums):
    step = pl.program_id(0)
    blocks, bs = tiles_ref.shape[1], tiles_ref.shape[2]

    @pl.when(step == 0)
    def _():
        sums[...] = jnp.zeros_like(sums)

    for p in range(chunk):
        segment = index_ref[step * chunk + p]
        for b in range(blocks):
            cols = slice(b * bs, (b + 1) * bs)
            sums[segment, :, cols] += tiles_ref[p, b].astype(jnp.float32)

    @pl.when(step == pl.num_programs(0) - 1)
    def _():
        out_ref[...] = sums[...].astype(jnp.bfloat16)


def segment_sums(offdiag, row_index, segments):
    tiles, blocks, bs, _ = offdiag.shape
    chunk = 8
    return pl.pallas_call(
        functools.partial(segment_kernel, chunk),
        grid_spec=pltpu.PrefetchScalarGridSpec(
            num_scalar_prefetch=1,
            grid=(tiles // chunk,),
            in_specs=[pl.BlockSpec((chunk, blocks, bs, bs), lambda i, index: (i, 0, 0, 0))],
            out_specs=pl.BlockSpec((segments, bs, blocks * bs), lambda i, index: (0, 0, 0)),
            scratch_shapes=[pltpu.VMEM((segments, bs, blocks * bs), jnp.float32)],
        ),
        out_shape=jax.ShapeDtypeStruct((segments, bs, blocks * bs), jnp.bfloat16),
        compiler_params=pltpu.CompilerParams(vmem_limit_bytes=VMEM_LIMIT),
        cost_estimate=pl.CostEstimate(
            flops=offdiag.size, bytes_accessed=2 * offdiag.size, transcendentals=0
        ),
        name="segment_sums",
    )(row_index, offdiag)


def update_kernel(cols, *refs):
    known_refs, (sums_ref, rhs_ref, inverse_ref, keep_ref, give_ref, whole) = refs[:cols], refs[cols:]
    blocks, count, bs = rhs_ref.shape
    per = known_refs[0].shape[0]
    row_id, col_id = lax.axis_index("row"), lax.axis_index("col")
    off = jnp.zeros((count, blocks * bs), jnp.float32)
    for step in range(cols):
        first = lax.rem(col_id + cols - step, cols) * per
        for i in range(per):
            off += jnp.dot(
                known_refs[step][i], sums_ref[first + i], preferred_element_type=jnp.float32
            )
    adds = (row_id == 0).astype(jnp.float32)
    for b in range(blocks):
        total = rhs_ref[b] * adds - off[:, b * bs : (b + 1) * bs]
        whole[b] = jnp.dot(
            total, inverse_ref[b], precision=HIGHEST, preferred_element_type=jnp.float32
        )
    half = count // 2
    core = lax.rem(row_id, 2)
    keep = pl.ds(pl.multiple_of(core * half, half), half)
    give = pl.ds(pl.multiple_of((1 - core) * half, half), half)
    keep_ref[...] = whole[:, keep, :]
    give_ref[...] = whole[:, give, :].astype(jnp.bfloat16)


def local_update(known, sums, rhs, inverse):
    blocks, count, bs = rhs.shape
    half = (blocks, count // 2, bs)
    return pl.pallas_call(
        functools.partial(update_kernel, len(known)),
        out_shape=(
            jax.ShapeDtypeStruct(half, jnp.float32),
            jax.ShapeDtypeStruct(half, jnp.bfloat16),
        ),
        scratch_shapes=[pltpu.VMEM(rhs.shape, jnp.float32)],
        compiler_params=pltpu.CompilerParams(vmem_limit_bytes=VMEM_LIMIT),
        name="local_update",
    )(*known, sums, rhs, inverse)


def chain_kernel(rows, cols, slots, *refs):
    zs = rows // 2
    value_refs, refs = refs[:cols], refs[cols:]
    piece_refs, refs = (refs[:cols], refs[cols : 2 * cols]), refs[2 * cols :]
    out_ref, tiles, values, solved, sems = refs
    row_id, col_id = lax.axis_index("row"), lax.axis_index("col")
    core, z = lax.rem(row_id, 2), row_id // 2
    copies = []
    for side in range(2):
        for step in range(cols):
            owner_col = lax.rem(col_id + cols - step, cols)
            for back in range(zs):
                owner_z = lax.rem(z + zs - back, zs)
                owner_core = core if side == 0 else 1 - core
                copy = pltpu.make_async_copy(
                    piece_refs[side][step].at[back],
                    tiles.at[2 * owner_z + owner_core, owner_col],
                    sems.at[len(copies)],
                )
                copy.start()
                copies.append(copy)
    per = value_refs[0].shape[0]
    for step in range(cols):
        owner_col = lax.rem(col_id + cols - step, cols)
        for b in range(per):
            values[b * cols + owner_col] = value_refs[step][b].astype(jnp.float32)
    for copy in copies:
        copy.wait()
    sums = [values[k] for k in range(NB)]
    for j in reversed(range(NB)):
        block = sums[j].astype(jnp.bfloat16)
        solved[j] = block
        for k in reversed(range(j)):
            at = slots.index((j // rows, k // cols))
            sums[k] = sums[k] - jnp.dot(
                block, tiles[j % rows, k % cols, at], preferred_element_type=jnp.float32
            )
    for b in range(per):
        out_ref[b] = solved[b * cols + col_id]


def chain(values, own, other, rows, cols, slots):
    per, half, bs = values[0].shape
    anywhere = pl.BlockSpec(memory_space=pl.ANY)
    vmem = pl.BlockSpec(memory_space=pltpu.VMEM)
    return pl.pallas_call(
        functools.partial(chain_kernel, rows, cols, slots),
        in_specs=[vmem] * cols + [anywhere] * (2 * cols),
        out_specs=vmem,
        out_shape=jax.ShapeDtypeStruct((per, half, bs), jnp.bfloat16),
        scratch_shapes=[
            pltpu.VMEM((rows, cols, len(slots), bs, bs), jnp.bfloat16),
            pltpu.VMEM((NB, half, bs), jnp.float32),
            pltpu.VMEM((NB, half, bs), jnp.bfloat16),
            pltpu.SemaphoreType.DMA((rows * cols,)),
        ],
        compiler_params=pltpu.CompilerParams(vmem_limit_bytes=VMEM_LIMIT),
        name="chain",
    )(*values, *own, *other)


def body(rhs, diag_inv, panel, offdiag, known, row_index):
    rows, cols = lax.axis_size("row"), lax.axis_size("col")
    zs = rows // 2
    slots = tile_slots(rows, cols)

    known_all = [known] + [along_col(known, rows, cols, d) for d in range(1, cols)]
    folded = fold_panel(panel, diag_inv, slots)
    line = jnp.stack([folded] + [along_z(folded, rows, cols, d) for d in range(1, zs)])
    own = [line] + [along_col(line, rows, cols, d) for d in range(1, cols)]
    other = [other_core(piece, rows, cols) for piece in own]

    sums = segment_sums(offdiag, row_index, known.shape[0] * cols)
    keep, give = local_update(known_all, sums, rhs, diag_inv)
    part = (keep + other_core(give, rows, cols).astype(jnp.float32)).astype(jnp.bfloat16)
    total = part.astype(jnp.float32)
    for d in range(1, zs):
        total = total + along_z(part, rows, cols, d).astype(jnp.float32)
    total = total.astype(jnp.bfloat16)
    values = [total] + [along_col(total, rows, cols, d) for d in range(1, cols)]

    mine = chain(values, own, other, rows, cols, slots)
    theirs = other_core(mine, rows, cols)
    first = lax.rem(lax.axis_index("row"), 2) == 0
    return jnp.concatenate(
        [jnp.where(first, mine, theirs), jnp.where(first, theirs, mine)], axis=1
    )


def solution(mesh):
    placed = (
        P("col", None, None),
        P("col", None, None),
        P("row", "col", None, None),
        P("row", "col", None, None),
        P(("row", "col"), None, None),
        P("row"),
    )
    return jax.shard_map(
        body, mesh=mesh, in_specs=placed, out_specs=P("col", None, None), check_vma=False
    )
```

time: 760 us -> 120 us (0.16)
  blocking collectives: 659 us -> 0 us
  starting transfers between devices: 0.01 us -> 28.5 us
  matrix products: 24.6 us -> 0 us
  Pallas kernels: 0 us -> 18.9 us
  waiting for transfers between devices: 54.6 us -> 68.4 us
  between operations: 13.5 us -> 0.14 us
    psum x32 -> x0, blocking collectives: 648 us -> none  [the longest x16 415 us: step_reduced(): lax.psum(partial_value.astype(jnp.bfloat16), 'row').astype(jnp.float32)]
    ppermute x0 -> x21, waiting for transfers between devices: none -> 68.4 us  [send(): return lax.ppermute(array, AXES, pairs)]
    psum x1 -> x0, waiting for transfers between devices: 54.5 us -> none  [body(): off_sum = lax.psum(off_part, 'row')]
    ppermute x0 -> x21, starting transfers between devices: none -> 28.5 us  [send(): return lax.ppermute(array, AXES, pairs)]
    dot_general x33 -> x0, matrix products: 24.6 us -> none  [the longest x16 16.4 us: finish_block(): jnp.dot(total, inverse, precision=lax.Precision.HIGHEST, preferred_elemen...]
    pallas_call x0 -> x4, Pallas kernels: none -> 18.9 us  [the longest x1 10.8 us: chain(): pl.pallas_call(functools.partial(chain_kernel, rows, cols, slots), in_spe...]
    all_gather x1 -> x0, blocking collectives: 10.1 us -> none  [body(): known_row = lax.all_gather(known, 'col', axis=0, tiled=True)]
  transfers between devices with their start and end apart: 1 -> 21, of which waited for: 1 -> 15; matrix products, arithmetic and copies ran while one was open for 0% -> 0% of each run, Pallas kernels for 0% -> 6%
where the time goes in v1:
time: 120 us
  waiting for transfers between devices  68.4 us (57%)
  starting transfers between devices  28.5 us (24%)
  Pallas kernels  18.9 us (16%)
  local copies, waits for them, and re-layouts  3.45 us (3%)
    ppermute x21, waiting for transfers between devices, send(): return lax.ppermute(array, AXES, pairs)  68.4 us
    ppermute x21, starting transfers between devices, send(): return lax.ppermute(array, AXES, pairs)  28.5 us
    pallas_call x1, Pallas kernels, chain(): pl.pallas_call(functools.partial(chain_kernel, rows, cols, slots), in_spe...  10.8 us
    pallas_call x1, Pallas kernels, segment_sums(): pl.pallas_call(functools.partial(segment_kernel, chunk), grid_spec=pltpu....  7.17 us
    unnamed x14, local copies, waits for them, and re-layouts  3.45 us
  transfers between devices with their start and end apart: 21, of which 15 were waited for; matrix products, arithmetic and copies ran while one was open for 0% of the time, Pallas kernels for 6%

profile of v1, /device:TPU:0, one launch (start us, length us, event | category | flops | bytes accessed | tf_op | source)
XLA Modules:
  0.0 120.2 jit_solution(939385520242335782)
XLA Ops:
  0.0 0.0 copy-start
  0.0 0.9 copy-done
  1.0 0.0 copy-start.2
  1.0 0.9 copy-done.2
  1.9 0.0 copy-start.1
  1.9 0.0 copy-start.3
  1.9 0.0 copy-start.4
  1.9 0.3 fold_panel.1
  2.2 3.1 %collective-permute-start.10 = (bf16[6,128,128]{2,1,0:T(8,128)(2,1)S(1)}, bf16[6,128,128]{2,1,0:T(8,128)(2,1)S(1)}, u32[]{:S(2)}, u32[]{:S(2)}) collective-permute-start(bf16[6,128,128]{2,1,0:T(8,128)(2,1)S(1)} %fold_panel.1), channel_id=1, source_target_pairs={{0,8},{1,9},{2,10},{3,11},{4,12},{5,13},{6,14},{7,15},{8,16},{9,17... | collective-permute-start | bytes 589832 | tf_op jit(solution)/shard_map/ppermute | solution.py:31
  5.3 2.6 %collective-permute-start.11 = (bf16[6,128,128]{2,1,0:T(8,128)(2,1)S(1)}, bf16[6,128,128]{2,1,0:T(8,128)(2,1)S(1)}, u32[]{:S(2)}, u32[]{:S(2)}) collective-permute-start(bf16[6,128,128]{2,1,0:T(8,128)(2,1)S(1)} %fold_panel.1), channel_id=1, source_target_pairs={{0,16},{1,17},{2,18},{3,19},{4,20},{5,21},{6,22},{7,23},{8,24},{9,... | collective-permute-start | bytes 589832 | tf_op jit(solution)/shard_map/ppermute | solution.py:31
  7.8 1.3 %collective-permute-start.12 = (bf16[6,128,128]{2,1,0:T(8,128)(2,1)S(1)}, bf16[6,128,128]{2,1,0:T(8,128)(2,1)S(1)}, u32[]{:S(2)}, u32[]{:S(2)}) collective-permute-start(bf16[6,128,128]{2,1,0:T(8,128)(2,1)S(1)} %fold_panel.1), channel_id=1, source_target_pairs={{0,24},{1,25},{2,26},{3,27},{4,28},{5,29},{6,30},{7,31},{8,0},{9,1... | collective-permute-start | bytes 589832 | tf_op jit(solution)/shard_map/ppermute | solution.py:31
  9.2 3.9 %collective-permute-done.10 = bf16[6,128,128]{2,1,0:T(8,128)(2,1)S(1)} collective-permute-done((bf16[6,128,128]{2,1,0:T(8,128)(2,1)S(1)}, bf16[6,128,128]{2,1,0:T(8,128)(2,1)S(1)}, u32[]{:S(2)}, u32[]{:S(2)}) %collective-permute-start.10) | collective-permute-done | bytes 196640 | tf_op jit(solution)/shard_map/ppermute | solution.py:31
  13.1 7.6 %collective-permute-done.11 = bf16[6,128,128]{2,1,0:T(8,128)(2,1)S(1)} collective-permute-done((bf16[6,128,128]{2,1,0:T(8,128)(2,1)S(1)}, bf16[6,128,128]{2,1,0:T(8,128)(2,1)S(1)}, u32[]{:S(2)}, u32[]{:S(2)}) %collective-permute-start.11) | collective-permute-done | bytes 196640 | tf_op jit(solution)/shard_map/ppermute | solution.py:31
  20.7 0.0 collective-permute-done.12
  20.7 0.1 pad_maximum_fusion.refs_4_
  20.8 1.5 %collective-permute-start.13 = (bf16[4,6,128,128]{3,2,1,0:T(8,128)(2,1)S(1)}, bf16[4,6,128,128]{3,2,1,0:T(8,128)(2,1)S(1)}, u32[]{:S(2)}, u32[]{:S(2)}) collective-permute-start(bf16[4,6,128,128]{3,2,1,0:T(8,128)(2,1)S(1)} %pad_maximum_fusion.refs_4_), channel_id=1, source_target_pairs={{0,1},{1,2},{2,3},{3,0},{4,5},{5,6},{6,7},{7,4},{8,9},{9,10},{10,1... | collective-permute-start | bytes 2359304 | tf_op jit(solution)/shard_map/ppermute | solution.py:31
  22.3 1.5 %collective-permute-start.14 = (bf16[4,6,128,128]{3,2,1,0:T(8,128)(2,1)S(1)}, bf16[4,6,128,128]{3,2,1,0:T(8,128)(2,1)S(1)}, u32[]{:S(2)}, u32[]{:S(2)}) collective-permute-start(bf16[4,6,128,128]{3,2,1,0:T(8,128)(2,1)S(1)} %pad_maximum_fusion.refs_4_), channel_id=1, source_target_pairs={{0,2},{1,3},{2,0},{3,1},{4,6},{5,7},{6,4},{7,5},{8,10},{9,11},{10,... | collective-permute-start | bytes 2359304 | tf_op jit(solution)/shard_map/ppermute | solution.py:31
  23.9 1.4 %collective-permute-start.15 = (bf16[4,6,128,128]{3,2,1,0:T(8,128)(2,1)S(1)}, bf16[4,6,128,128]{3,2,1,0:T(8,128)(2,1)S(1)}, u32[]{:S(2)}, u32[]{:S(2)}) collective-permute-start(bf16[4,6,128,128]{3,2,1,0:T(8,128)(2,1)S(1)} %pad_maximum_fusion.refs_4_), channel_id=1, source_target_pairs={{0,3},{1,0},{2,1},{3,2},{4,7},{5,4},{6,5},{7,6},{8,11},{9,8},{10,9... | collective-permute-start | bytes 2359304 | tf_op jit(solution)/shard_map/ppermute | solution.py:31
  25.3 0.0 collective-permute-start.16
  25.3 16.9 %collective-permute-done.13.refs_5_ = bf16[4,6,128,128]{3,2,1,0:T(8,128)(2,1)S(1)} collective-permute-done((bf16[4,6,128,128]{3,2,1,0:T(8,128)(2,1)S(1)}, bf16[4,6,128,128]{3,2,1,0:T(8,128)(2,1)S(1)}, u32[]{:S(2)}, u32[]{:S(2)}) %collective-permute-start.13) | collective-permute-done | bytes 786464 | tf_op jit(solution)/shard_map/ppermute | solution.py:31
  42.2 0.0 collective-permute-start.17
  42.3 15.8 %collective-permute-done.14.refs_6_ = bf16[4,6,128,128]{3,2,1,0:T(8,128)(2,1)S(1)} collective-permute-done((bf16[4,6,128,128]{3,2,1,0:T(8,128)(2,1)S(1)}, bf16[4,6,128,128]{3,2,1,0:T(8,128)(2,1)S(1)}, u32[]{:S(2)}, u32[]{:S(2)}) %collective-permute-start.14) | collective-permute-done | bytes 786464 | tf_op jit(solution)/shard_map/ppermute | solution.py:31
  58.0 0.0 collective-permute-start.18
  58.0 0.1 collective-permute-done.15.refs_7_
  58.1 0.4 collective-permute-start.19
  58.5 1.8 %collective-permute-start = (bf16[2,64,128]{2,1,0:T(8,128)(2,1)}, bf16[2,64,128]{2,1,0:T(8,128)(2,1)S(1)}, u32[]{:S(2)}, u32[]{:S(2)}) collective-permute-start(bf16[2,64,128]{2,1,0:T(8,128)(2,1)} %refs_0_.1), channel_id=1, source_target_pairs={{0,1},{1,2},{2,3},{3,0},{4,5},{5,6},{6,7},{7,4},{8,9},{9,10},{10,1... | collective-permute-start | bytes 98312 | tf_op jit(solution)/shard_map/ppermute | solution.py:31
  60.3 3.2 %collective-permute-done.refs_1_ = bf16[2,64,128]{2,1,0:T(8,128)(2,1)S(1)} collective-permute-done((bf16[2,64,128]{2,1,0:T(8,128)(2,1)}, bf16[2,64,128]{2,1,0:T(8,128)(2,1)S(1)}, u32[]{:S(2)}, u32[]{:S(2)}) %collective-permute-start) | collective-permute-done | bytes 32800 | tf_op jit(solution)/shard_map/ppermute | solution.py:31
  63.5 1.5 %collective-permute-start.1 = (bf16[2,64,128]{2,1,0:T(8,128)(2,1)}, bf16[2,64,128]{2,1,0:T(8,128)(2,1)S(1)}, u32[]{:S(2)}, u32[]{:S(2)}) collective-permute-start(bf16[2,64,128]{2,1,0:T(8,128)(2,1)} %refs_0_.1), channel_id=1, source_target_pairs={{0,2},{1,3},{2,0},{3,1},{4,6},{5,7},{6,4},{7,5},{8,10},{9,11},{10,... | collective-permute-start | bytes 98312 | tf_op jit(solution)/shard_map/ppermute | solution.py:31
  65.0 2.6 %collective-permute-done.1.refs_2_ = bf16[2,64,128]{2,1,0:T(8,128)(2,1)S(1)} collective-permute-done((bf16[2,64,128]{2,1,0:T(8,128)(2,1)}, bf16[2,64,128]{2,1,0:T(8,128)(2,1)S(1)}, u32[]{:S(2)}, u32[]{:S(2)}) %collective-permute-start.1) | collective-permute-done | bytes 32800 | tf_op jit(solution)/shard_map/ppermute | solution.py:31
  67.7 0.8 collective-permute-start.2
  68.5 0.0 copy-start.5
  68.5 0.7 copy-done.5
  69.2 7.2 %segment_sums.1.refs_4_ = bf16[8,128,512]{2,1,0:T(8,128)(2,1)S(1)} custom-call(s32[64]{0:T(128)S(1)} %copy-done.5, bf16[64,4,128,128]{3,2,1,0:T(8,128)(2,1)} %tiles_ref.1), custom_call_target="tpu_custom_call" | custom-call | flops 4194304 | bytes 8388608 | tf_op jit(solution)/shard_map/segment_sums/pallas_call | solution.py:90
  76.4 0.0 collective-permute-done.2.refs_3_
  76.4 0.0 copy-done.1
  76.4 0.0 copy-done.3
  76.4 0.0 copy-done.4
  76.4 0.6 local_update.1
  77.0 0.1 collective-permute-start.3
  77.1 1.2 collective-permute-done.3
  78.3 4.8 %collective-permute-start.4 = (bf16[4,32,128]{2,1,0:T(8,128)(2,1)S(1)}, bf16[4,32,128]{2,1,0:T(8,128)(2,1)S(1)}, u32[]{:S(2)}, u32[]{:S(2)}) collective-permute-start(bf16[4,32,128]{2,1,0:T(8,128)(2,1)S(1)} %add_convert_fusion.1), channel_id=1, source_target_pairs={{0,8},{1,9},{2,10},{3,11},{4,12},{5,13},{6,14},{7,15},{8,16},{9,17... | collective-permute-start | bytes 98312 | tf_op jit(solution)/shard_map/ppermute | solution.py:31
  83.1 1.9 %collective-permute-done.4 = bf16[4,32,128]{2,1,0:T(8,128)(2,1)S(1)} collective-permute-done((bf16[4,32,128]{2,1,0:T(8,128)(2,1)S(1)}, bf16[4,32,128]{2,1,0:T(8,128)(2,1)S(1)}, u32[]{:S(2)}, u32[]{:S(2)}) %collective-permute-start.4) | collective-permute-done | bytes 32800 | tf_op jit(solution)/shard_map/ppermute | solution.py:31
  85.0 1.5 %collective-permute-start.5 = (bf16[4,32,128]{2,1,0:T(8,128)(2,1)S(1)}, bf16[4,32,128]{2,1,0:T(8,128)(2,1)S(1)}, u32[]{:S(2)}, u32[]{:S(2)}) collective-permute-start(bf16[4,32,128]{2,1,0:T(8,128)(2,1)S(1)} %add_convert_fusion.1), channel_id=1, source_target_pairs={{0,16},{1,17},{2,18},{3,19},{4,20},{5,21},{6,22},{7,23},{8,24},{9,... | collective-permute-start | bytes 98312 | tf_op jit(solution)/shard_map/ppermute | solution.py:31
  86.5 3.3 %collective-permute-done.5 = bf16[4,32,128]{2,1,0:T(8,128)(2,1)S(1)} collective-permute-done((bf16[4,32,128]{2,1,0:T(8,128)(2,1)S(1)}, bf16[4,32,128]{2,1,0:T(8,128)(2,1)S(1)}, u32[]{:S(2)}, u32[]{:S(2)}) %collective-permute-start.5) | collective-permute-done | bytes 32800 | tf_op jit(solution)/shard_map/ppermute | solution.py:31
  89.8 2.0 %collective-permute-start.6 = (bf16[4,32,128]{2,1,0:T(8,128)(2,1)S(1)}, bf16[4,32,128]{2,1,0:T(8,128)(2,1)S(1)}, u32[]{:S(2)}, u32[]{:S(2)}) collective-permute-start(bf16[4,32,128]{2,1,0:T(8,128)(2,1)S(1)} %add_convert_fusion.1), channel_id=1, source_target_pairs={{0,24},{1,25},{2,26},{3,27},{4,28},{5,29},{6,30},{7,31},{8,0},{9,1... | collective-permute-start | bytes 98312 | tf_op jit(solution)/shard_map/ppermute | solution.py:31
  91.9 1.9 %collective-permute-done.6 = bf16[4,32,128]{2,1,0:T(8,128)(2,1)S(1)} collective-permute-done((bf16[4,32,128]{2,1,0:T(8,128)(2,1)S(1)}, bf16[4,32,128]{2,1,0:T(8,128)(2,1)S(1)}, u32[]{:S(2)}, u32[]{:S(2)}) %collective-permute-start.6) | collective-permute-done | bytes 32800 | tf_op jit(solution)/shard_map/ppermute | solution.py:31
  93.8 1.2 %collective-permute-start.7 = (bf16[4,32,128]{2,1,0:T(8,128)(2,1)S(1)}, bf16[4,32,128]{2,1,0:T(8,128)(2,1)S(1)}, u32[]{:S(2)}, u32[]{:S(2)}) collective-permute-start(bf16[4,32,128]{2,1,0:T(8,128)(2,1)S(1)} %add_convert_fusion.refs_0_), channel_id=1, source_target_pairs={{0,1},{1,2},{2,3},{3,0},{4,5},{5,6},{6,7},{7,4},{8,9},{9,10},{10,1... | collective-permute-start | bytes 98312 | tf_op jit(solution)/shard_map/ppermute | solution.py:31
  95.0 3.6 %collective-permute-done.7.refs_1_ = bf16[4,32,128]{2,1,0:T(8,128)(2,1)S(1)} collective-permute-done((bf16[4,32,128]{2,1,0:T(8,128)(2,1)S(1)}, bf16[4,32,128]{2,1,0:T(8,128)(2,1)S(1)}, u32[]{:S(2)}, u32[]{:S(2)}) %collective-permute-start.7) | collective-permute-done | bytes 32800 | tf_op jit(solution)/shard_map/ppermute | solution.py:31
  98.7 1.5 %collective-permute-start.8 = (bf16[4,32,128]{2,1,0:T(8,128)(2,1)S(1)}, bf16[4,32,128]{2,1,0:T(8,128)(2,1)S(1)}, u32[]{:S(2)}, u32[]{:S(2)}) collective-permute-start(bf16[4,32,128]{2,1,0:T(8,128)(2,1)S(1)} %add_convert_fusion.refs_0_), channel_id=1, source_target_pairs={{0,2},{1,3},{2,0},{3,1},{4,6},{5,7},{6,4},{7,5},{8,10},{9,11},{10,... | collective-permute-start | bytes 98312 | tf_op jit(solution)/shard_map/ppermute | solution.py:31
  100.2 2.4 %collective-permute-done.8.refs_2_ = bf16[4,32,128]{2,1,0:T(8,128)(2,1)S(1)} collective-permute-done((bf16[4,32,128]{2,1,0:T(8,128)(2,1)S(1)}, bf16[4,32,128]{2,1,0:T(8,128)(2,1)S(1)}, u32[]{:S(2)}, u32[]{:S(2)}) %collective-permute-start.8) | collective-permute-done | bytes 32800 | tf_op jit(solution)/shard_map/ppermute | solution.py:31
  102.6 1.2 %collective-permute-start.9 = (bf16[4,32,128]{2,1,0:T(8,128)(2,1)S(1)}, bf16[4,32,128]{2,1,0:T(8,128)(2,1)S(1)}, u32[]{:S(2)}, u32[]{:S(2)}) collective-permute-start(bf16[4,32,128]{2,1,0:T(8,128)(2,1)S(1)} %add_convert_fusion.refs_0_), channel_id=1, source_target_pairs={{0,3},{1,0},{2,1},{3,2},{4,7},{5,4},{6,5},{7,6},{8,11},{9,8},{10,9... | collective-permute-start | bytes 98312 | tf_op jit(solution)/shard_map/ppermute | solution.py:31
  103.8 2.7 %collective-permute-done.9.refs_3_ = bf16[4,32,128]{2,1,0:T(8,128)(2,1)S(1)} collective-permute-done((bf16[4,32,128]{2,1,0:T(8,128)(2,1)S(1)}, bf16[4,32,128]{2,1,0:T(8,128)(2,1)S(1)}, u32[]{:S(2)}, u32[]{:S(2)}) %collective-permute-start.9) | collective-permute-done | bytes 32800 | tf_op jit(solution)/shard_map/ppermute | solution.py:31
  106.5 0.0 collective-permute-done.16.refs_8_
  106.5 0.0 collective-permute-done.17.refs_9_
  106.5 0.0 collective-permute-done.18.refs_10_
  106.5 0.0 collective-permute-done.19.refs_11_
  106.5 0.0 copy-start.6
  106.5 0.9 copy-done.6
  107.4 10.8 %chain.1 = bf16[4,32,128]{2,1,0:T(8,128)(2,1)S(1)} custom-call(bf16[4,32,128]{2,1,0:T(8,128)(2,1)S(1)} %add_convert_fusion.refs_0_, bf16[4,32,128]{2,1,0:T(8,128)(2,1)S(1)} %collective-permute-done.7.refs_1_, bf16[4,32,128]{2,1,0:T(8,128)(2,1)S(1)} %collective-permute-done.8.refs_2_, bf16[4,32,128]{2,1,0:T(8,128)(2,1)S(1)} %collective-permute-done.9.refs_3_, ...), custom_call_target="tpu_custom_call" | custom-call | tf_op jit(solution)/shard_map/chain/pallas_call | solution.py:194
  118.2 0.1 collective-permute-start.20
  118.3 1.2 collective-permute-done.20
  119.5 0.6 pad_maximum_fusion.1
  (3 shorter events, 0.0 us)
Async XLA Ops:
  0.0 0.9 copy-start
  1.0 0.9 copy-start.2
  1.9 74.5 %copy-start.1 = (f32[4,128,128]{2,1,0:T(8,128)S(1)}, f32[4,128,128]{2,1,0:T(8,128)}, u32[]{:S(2)}) copy-start(f32[4,128,128]{2,1,0:T(8,128)} %inverse_ref.1) | copy-start | bytes 786436
  1.9 74.5 %copy-start.3 = (f32[4,64,128]{2,1,0:T(8,128)S(1)}, f32[4,64,128]{2,1,0:T(8,128)}, u32[]{:S(2)}) copy-start(f32[4,64,128]{2,1,0:T(8,128)} %refs_5_.1) | copy-start | bytes 393220
  1.9 74.5 %copy-start.4 = (bf16[2,64,128]{2,1,0:T(8,128)(2,1)S(1)}, bf16[2,64,128]{2,1,0:T(8,128)(2,1)}, u32[]{:S(2)}) copy-start(bf16[2,64,128]{2,1,0:T(8,128)(2,1)} %refs_0_.1) | copy-start | bytes 98308
  2.2 11.0 %collective-permute-start.10 = (bf16[6,128,128]{2,1,0:T(8,128)(2,1)S(1)}, bf16[6,128,128]{2,1,0:T(8,128)(2,1)S(1)}, u32[]{:S(2)}, u32[]{:S(2)}) collective-permute-start(bf16[6,128,128]{2,1,0:T(8,128)(2,1)S(1)} %fold_panel.1), channel_id=1, source_target_pairs={{0,8},{1,9},{2,10},{3,11},{4,12},{5,13},{6,14},{7,15},{8,16},{9,17... | collective-permute-start | bytes 589832 | tf_op jit(solution)/shard_map/ppermute | solution.py:31
  5.3 15.5 %collective-permute-start.11 = (bf16[6,128,128]{2,1,0:T(8,128)(2,1)S(1)}, bf16[6,128,128]{2,1,0:T(8,128)(2,1)S(1)}, u32[]{:S(2)}, u32[]{:S(2)}) collective-permute-start(bf16[6,128,128]{2,1,0:T(8,128)(2,1)S(1)} %fold_panel.1), channel_id=1, source_target_pairs={{0,16},{1,17},{2,18},{3,19},{4,20},{5,21},{6,22},{7,23},{8,24},{9,... | collective-permute-start | bytes 589832 | tf_op jit(solution)/shard_map/ppermute | solution.py:31
  7.8 12.9 %collective-permute-start.12 = (bf16[6,128,128]{2,1,0:T(8,128)(2,1)S(1)}, bf16[6,128,128]{2,1,0:T(8,128)(2,1)S(1)}, u32[]{:S(2)}, u32[]{:S(2)}) collective-permute-start(bf16[6,128,128]{2,1,0:T(8,128)(2,1)S(1)} %fold_panel.1), channel_id=1, source_target_pairs={{0,24},{1,25},{2,26},{3,27},{4,28},{5,29},{6,30},{7,31},{8,0},{9,1... | collective-permute-start | bytes 589832 | tf_op jit(solution)/shard_map/ppermute | solution.py:31
  20.8 21.4 %collective-permute-start.13 = (bf16[4,6,128,128]{3,2,1,0:T(8,128)(2,1)S(1)}, bf16[4,6,128,128]{3,2,1,0:T(8,128)(2,1)S(1)}, u32[]{:S(2)}, u32[]{:S(2)}) collective-permute-start(bf16[4,6,128,128]{3,2,1,0:T(8,128)(2,1)S(1)} %pad_maximum_fusion.refs_4_), channel_id=1, source_target_pairs={{0,1},{1,2},{2,3},{3,0},{4,5},{5,6},{6,7},{7,4},{8,9},{9,10},{10,1... | collective-permute-start | bytes 2359304 | tf_op jit(solution)/shard_map/ppermute | solution.py:31
  22.3 35.7 %collective-permute-start.14 = (bf16[4,6,128,128]{3,2,1,0:T(8,128)(2,1)S(1)}, bf16[4,6,128,128]{3,2,1,0:T(8,128)(2,1)S(1)}, u32[]{:S(2)}, u32[]{:S(2)}) collective-permute-start(bf16[4,6,128,128]{3,2,1,0:T(8,128)(2,1)S(1)} %pad_maximum_fusion.refs_4_), channel_id=1, source_target_pairs={{0,2},{1,3},{2,0},{3,1},{4,6},{5,7},{6,4},{7,5},{8,10},{9,11},{10,... | collective-permute-start | bytes 2359304 | tf_op jit(solution)/shard_map/ppermute | solution.py:31
  23.9 34.2 %collective-permute-start.15 = (bf16[4,6,128,128]{3,2,1,0:T(8,128)(2,1)S(1)}, bf16[4,6,128,128]{3,2,1,0:T(8,128)(2,1)S(1)}, u32[]{:S(2)}, u32[]{:S(2)}) collective-permute-start(bf16[4,6,128,128]{3,2,1,0:T(8,128)(2,1)S(1)} %pad_maximum_fusion.refs_4_), channel_id=1, source_target_pairs={{0,3},{1,0},{2,1},{3,2},{4,7},{5,4},{6,5},{7,6},{8,11},{9,8},{10,9... | collective-permute-start | bytes 2359304 | tf_op jit(solution)/shard_map/ppermute | solution.py:31
  25.3 81.2 %collective-permute-start.16 = (bf16[4,6,128,128]{3,2,1,0:T(8,128)(2,1)S(1)}, bf16[4,6,128,128]{3,2,1,0:T(8,128)(2,1)S(1)}, u32[]{:S(2)}, u32[]{:S(2)}) collective-permute-start(bf16[4,6,128,128]{3,2,1,0:T(8,128)(2,1)S(1)} %pad_maximum_fusion.refs_4_), channel_id=1, source_target_pairs={{0,4},{1,5},{2,6},{3,7},{4,0},{5,1},{6,2},{7,3},{8,12},{9,13},{10,... | collective-permute-start | bytes 2359304 | tf_op jit(solution)/shard_map/ppermute | solution.py:31
  42.2 64.2 %collective-permute-start.17 = (bf16[4,6,128,128]{3,2,1,0:T(8,128)(2,1)S(1)}, bf16[4,6,128,128]{3,2,1,0:T(8,128)(2,1)S(1)}, u32[]{:S(2)}, u32[]{:S(2)}) collective-permute-start(bf16[4,6,128,128]{3,2,1,0:T(8,128)(2,1)S(1)} %collective-permute-done.13.refs_5_), channel_id=1, source_target_pairs={{0,4},{1,5},{2,6},{3,7},{4,0},{5,1},{6,2},{7,3},{8,12},{9,13},{10,... | collective-permute-start | bytes 2359304 | tf_op jit(solution)/shard_map/ppermute | solution.py:31
  58.0 48.5 %collective-permute-start.18 = (bf16[4,6,128,128]{3,2,1,0:T(8,128)(2,1)S(1)}, bf16[4,6,128,128]{3,2,1,0:T(8,128)(2,1)S(1)}, u32[]{:S(2)}, u32[]{:S(2)}) collective-permute-start(bf16[4,6,128,128]{3,2,1,0:T(8,128)(2,1)S(1)} %collective-permute-done.14.refs_6_), channel_id=1, source_target_pairs={{0,4},{1,5},{2,6},{3,7},{4,0},{5,1},{6,2},{7,3},{8,12},{9,13},{10,... | collective-permute-start | bytes 2359304 | tf_op jit(solution)/shard_map/ppermute | solution.py:31
  58.1 48.4 %collective-permute-start.19 = (bf16[4,6,128,128]{3,2,1,0:T(8,128)(2,1)S(1)}, bf16[4,6,128,128]{3,2,1,0:T(8,128)(2,1)S(1)}, u32[]{:S(2)}, u32[]{:S(2)}) collective-permute-start(bf16[4,6,128,128]{3,2,1,0:T(8,128)(2,1)S(1)} %collective-permute-done.15.refs_7_), channel_id=1, source_target_pairs={{0,4},{1,5},{2,6},{3,7},{4,0},{5,1},{6,2},{7,3},{8,12},{9,13},{10,... | collective-permute-start | bytes 2359304 | tf_op jit(solution)/shard_map/ppermute | solution.py:31
  58.5 5.0 %collective-permute-start = (bf16[2,64,128]{2,1,0:T(8,128)(2,1)}, bf16[2,64,128]{2,1,0:T(8,128)(2,1)S(1)}, u32[]{:S(2)}, u32[]{:S(2)}) collective-permute-start(bf16[2,64,128]{2,1,0:T(8,128)(2,1)} %refs_0_.1), channel_id=1, source_target_pairs={{0,1},{1,2},{2,3},{3,0},{4,5},{5,6},{6,7},{7,4},{8,9},{9,10},{10,1... | collective-permute-start | bytes 98312 | tf_op jit(solution)/shard_map/ppermute | solution.py:31
  63.5 4.1 %collective-permute-start.1 = (bf16[2,64,128]{2,1,0:T(8,128)(2,1)}, bf16[2,64,128]{2,1,0:T(8,128)(2,1)S(1)}, u32[]{:S(2)}, u32[]{:S(2)}) collective-permute-start(bf16[2,64,128]{2,1,0:T(8,128)(2,1)} %refs_0_.1), channel_id=1, source_target_pairs={{0,2},{1,3},{2,0},{3,1},{4,6},{5,7},{6,4},{7,5},{8,10},{9,11},{10,... | collective-permute-start | bytes 98312 | tf_op jit(solution)/shard_map/ppermute | solution.py:31
  67.7 8.7 %collective-permute-start.2 = (bf16[2,64,128]{2,1,0:T(8,128)(2,1)}, bf16[2,64,128]{2,1,0:T(8,128)(2,1)S(1)}, u32[]{:S(2)}, u32[]{:S(2)}) collective-permute-start(bf16[2,64,128]{2,1,0:T(8,128)(2,1)} %refs_0_.1), channel_id=1, source_target_pairs={{0,3},{1,0},{2,1},{3,2},{4,7},{5,4},{6,5},{7,6},{8,11},{9,8},{10,9... | collective-permute-start | bytes 98312 | tf_op jit(solution)/shard_map/ppermute | solution.py:31
  68.5 0.7 copy-start.5
  77.0 1.3 %collective-permute-start.3 = (bf16[4,32,128]{2,1,0:T(8,128)(2,1)S(1)}, bf16[4,32,128]{2,1,0:T(8,128)(2,1)S(1)}, u32[]{:S(2)}, u32[]{:S(2)}) collective-permute-start(bf16[4,32,128]{2,1,0:T(8,128)(2,1)S(1)} %get-tuple-element.8), channel_id=1, source_target_pairs={{0,4},{1,5},{2,6},{3,7},{4,0},{5,1},{6,2},{7,3},{8,12},{9,13},{10,... | collective-permute-start | bytes 98312 | tf_op jit(solution)/shard_map/ppermute | solution.py:31
  78.3 6.7 %collective-permute-start.4 = (bf16[4,32,128]{2,1,0:T(8,128)(2,1)S(1)}, bf16[4,32,128]{2,1,0:T(8,128)(2,1)S(1)}, u32[]{:S(2)}, u32[]{:S(2)}) collective-permute-start(bf16[4,32,128]{2,1,0:T(8,128)(2,1)S(1)} %add_convert_fusion.1), channel_id=1, source_target_pairs={{0,8},{1,9},{2,10},{3,11},{4,12},{5,13},{6,14},{7,15},{8,16},{9,17... | collective-permute-start | bytes 98312 | tf_op jit(solution)/shard_map/ppermute | solution.py:31
  85.0 4.8 %collective-permute-start.5 = (bf16[4,32,128]{2,1,0:T(8,128)(2,1)S(1)}, bf16[4,32,128]{2,1,0:T(8,128)(2,1)S(1)}, u32[]{:S(2)}, u32[]{:S(2)}) collective-permute-start(bf16[4,32,128]{2,1,0:T(8,128)(2,1)S(1)} %add_convert_fusion.1), channel_id=1, source_target_pairs={{0,16},{1,17},{2,18},{3,19},{4,20},{5,21},{6,22},{7,23},{8,24},{9,... | collective-permute-start | bytes 98312 | tf_op jit(solution)/shard_map/ppermute | solution.py:31
  89.8 3.9 %collective-permute-start.6 = (bf16[4,32,128]{2,1,0:T(8,128)(2,1)S(1)}, bf16[4,32,128]{2,1,0:T(8,128)(2,1)S(1)}, u32[]{:S(2)}, u32[]{:S(2)}) collective-permute-start(bf16[4,32,128]{2,1,0:T(8,128)(2,1)S(1)} %add_convert_fusion.1), channel_id=1, source_target_pairs={{0,24},{1,25},{2,26},{3,27},{4,28},{5,29},{6,30},{7,31},{8,0},{9,1... | collective-permute-start | bytes 98312 | tf_op jit(solution)/shard_map/ppermute | solution.py:31
  93.8 4.9 %collective-permute-start.7 = (bf16[4,32,128]{2,1,0:T(8,128)(2,1)S(1)}, bf16[4,32,128]{2,1,0:T(8,128)(2,1)S(1)}, u32[]{:S(2)}, u32[]{:S(2)}) collective-permute-start(bf16[4,32,128]{2,1,0:T(8,128)(2,1)S(1)} %add_convert_fusion.refs_0_), channel_id=1, source_target_pairs={{0,1},{1,2},{2,3},{3,0},{4,5},{5,6},{6,7},{7,4},{8,9},{9,10},{10,1... | collective-permute-start | bytes 98312 | tf_op jit(solution)/shard_map/ppermute | solution.py:31
  98.7 3.9 %collective-permute-start.8 = (bf16[4,32,128]{2,1,0:T(8,128)(2,1)S(1)}, bf16[4,32,128]{2,1,0:T(8,128)(2,1)S(1)}, u32[]{:S(2)}, u32[]{:S(2)}) collective-permute-start(bf16[4,32,128]{2,1,0:T(8,128)(2,1)S(1)} %add_convert_fusion.refs_0_), channel_id=1, source_target_pairs={{0,2},{1,3},{2,0},{3,1},{4,6},{5,7},{6,4},{7,5},{8,10},{9,11},{10,... | collective-permute-start | bytes 98312 | tf_op jit(solution)/shard_map/ppermute | solution.py:31
  102.6 3.9 %collective-permute-start.9 = (bf16[4,32,128]{2,1,0:T(8,128)(2,1)S(1)}, bf16[4,32,128]{2,1,0:T(8,128)(2,1)S(1)}, u32[]{:S(2)}, u32[]{:S(2)}) collective-permute-start(bf16[4,32,128]{2,1,0:T(8,128)(2,1)S(1)} %add_convert_fusion.refs_0_), channel_id=1, source_target_pairs={{0,3},{1,0},{2,1},{3,2},{4,7},{5,4},{6,5},{7,6},{8,11},{9,8},{10,9... | collective-permute-start | bytes 98312 | tf_op jit(solution)/shard_map/ppermute | solution.py:31
  106.5 0.9 copy-start.6
  118.2 1.3 %collective-permute-start.20 = (bf16[4,32,128]{2,1,0:T(8,128)(2,1)S(1)}, bf16[4,32,128]{2,1,0:T(8,128)(2,1)S(1)}, u32[]{:S(2)}, u32[]{:S(2)}) collective-permute-start(bf16[4,32,128]{2,1,0:T(8,128)(2,1)S(1)} %chain.1), channel_id=1, source_target_pairs={{0,4},{1,5},{2,6},{3,7},{4,0},{5,1},{6,2},{7,3},{8,12},{9,13},{10,... | collective-permute-start | bytes 98312 | tf_op jit(solution)/shard_map/ppermute | solution.py:31

commit v2 on v1

--- a/solution.py
+++ b/solution.py
@@ -146,92 +146,203 @@
     )(*known, sums, rhs, inverse)
 
 
-def chain_kernel(rows, cols, slots, *refs):
-    zs = rows // 2
+def span(slots, rows, cols, wanted):
+    found = [
+        at
+        for at, (a, b) in enumerate(slots)
+        for r in range(rows)
+        for c in range(cols)
+        if a * rows + r > b * cols + c and wanted(a * rows + r, b * cols + c)
+    ]
+    return min(found), max(found) + 1 - min(found)
+
+
+def make_plan(rows, cols):
+    half = NB // 2
+    slots = tile_slots(rows, cols)
+    return dict(
+        rows=rows,
+        cols=cols,
+        slots=slots,
+        high=span(slots, rows, cols, lambda j, k: k >= half),
+        cross=span(slots, rows, cols, lambda j, k: j >= half > k),
+        low=span(slots, rows, cols, lambda j, k: j < half),
+        upper=(half // cols, NB // cols - half // cols),
+        lower=(0, -(-half // cols)),
+    )
+
+
+def solve_half(sums, tile, first, solved):
+    for i in reversed(range(len(sums))):
+        block = sums[i].astype(jnp.bfloat16)
+        solved[i] = block
+        for m in reversed(range(i)):
+            sums[m] = sums[m] - jnp.dot(
+                block, tile(first + i, first + m), preferred_element_type=jnp.float32
+            )
+
+
+def place(refs, into, cols, col_id):
+    for step, ref in enumerate(refs):
+        owner = lax.rem(col_id + cols - step, cols)
+        for b in range(ref.shape[0]):
+            into[b * cols + owner] = ref[b].astype(jnp.float32)
+
+
+def start_tiles(plan, part, line_ref, mine, theirs, tiles, sems):
+    cols = plan["cols"]
+    col_id, core = lax.axis_index("col"), lax.rem(lax.axis_index("row"), 2)
+    first, count = plan[part]
+    pairs = [(line_ref.at[:, :, pl.ds(first, count)], tiles.at[:, :, col_id])]
+    for step in range(1, cols):
+        owner = lax.rem(col_id + cols - step, cols)
+        pairs.append((mine[step - 1], tiles.at[:, core, owner]))
+        pairs.append((theirs[step - 1], tiles.at[:, 1 - core, owner]))
+    copies = [pltpu.make_async_copy(a, b, sems.at[i]) for i, (a, b) in enumerate(pairs)]
+    for copy in copies:
+        copy.start()
+    return copies
+
+
+def tile_reader(plan, part, tiles):
+    def read(j, k):
+        at = plan["slots"].index((j // plan["rows"], k // plan["cols"])) - plan[part][0]
+        r = j % plan["rows"]
+        return tiles[r // 2, r % 2, k % plan["cols"], at]
+
+    return read
+
+
+def upper_kernel(plan, *refs):
+    rows, cols = plan["rows"], plan["cols"]
+    half, others = NB // 2, cols - 1
     value_refs, refs = refs[:cols], refs[cols:]
-    piece_refs, refs = (refs[:cols], refs[cols : 2 * cols]), refs[2 * cols :]
-    out_ref, tiles, values, solved, sems = refs
-    row_id, col_id = lax.axis_index("row"), lax.axis_index("col")
-    core, z = lax.rem(row_id, 2), row_id // 2
-    copies = []
-    for side in range(2):
-        for step in range(cols):
-            owner_col = lax.rem(col_id + cols - step, cols)
-            for back in range(zs):
-                owner_z = lax.rem(z + zs - back, zs)
-                owner_core = core if side == 0 else 1 - core
-                copy = pltpu.make_async_copy(
-                    piece_refs[side][step].at[back],
-                    tiles.at[2 * owner_z + owner_core, owner_col],
-                    sems.at[len(copies)],
-                )
-                copy.start()
-                copies.append(copy)
-    per = value_refs[0].shape[0]
-    for step in range(cols):
-        owner_col = lax.rem(col_id + cols - step, cols)
-        for b in range(per):
-            values[b * cols + owner_col] = value_refs[step][b].astype(jnp.float32)
+    own_ref, line_ref, refs = refs[0], refs[1], refs[2:]
+    mine, theirs, refs = refs[:others], refs[others : 2 * others], refs[2 * others :]
+    solved, lower_ref, tiles, cross, values, sems = refs
+    copies = start_tiles(plan, "high", line_ref, mine, theirs, tiles, sems)
+    wanted = line_ref.at[:, :, pl.ds(*plan["cross"])]
+    copies.append(pltpu.make_async_copy(wanted, cross, sems.at[len(copies)]))
+    copies[-1].start()
+    place(value_refs, values, cols, lax.axis_index("col"))
     for copy in copies:
         copy.wait()
-    sums = [values[k] for k in range(NB)]
-    for j in reversed(range(NB)):
-        block = sums[j].astype(jnp.bfloat16)
-        solved[j] = block
-        for k in reversed(range(j)):
-            at = slots.index((j // rows, k // cols))
-            sums[k] = sums[k] - jnp.dot(
-                block, tiles[j % rows, k % cols, at], preferred_element_type=jnp.float32
+    skip = plan["upper"][0] * cols
+    sums = [values[half + i - skip] for i in range(half)]
+    solve_half(sums, tile_reader(plan, "high", tiles), half, solved)
+    for b in range(plan["lower"][1]):
+        total = own_ref[b]
+        for j in range(half, NB):
+            at = plan["slots"].index((j // rows, b)) - plan["cross"][0]
+            r = j % rows
+            total = total - jnp.dot(
+                solved[j - half], cross[r // 2, r % 2, at], preferred_element_type=jnp.float32
             )
-    for b in range(per):
+        lower_ref[b] = total.astype(jnp.bfloat16)
+
+
+def lower_kernel(plan, *refs):
+    cols = plan["cols"]
+    half, others = NB // 2, cols - 1
+    value_refs, refs = refs[:cols], refs[cols:]
+    upper_ref, line_ref, refs = refs[0], refs[1], refs[2:]
+    mine, theirs, refs = refs[:others], refs[others : 2 * others], refs[2 * others :]
+    out_ref, tiles, values, solved, sems = refs
+    copies = start_tiles(plan, "low", line_ref, mine, theirs, tiles, sems)
+    col_id = lax.axis_index("col")
+    place(value_refs, values, cols, col_id)
+    solved[pl.ds(half, half)] = upper_ref[...]
+    for copy in copies:
+        copy.wait()
+    sums = [values[i] for i in range(half)]
+    solve_half(sums, tile_reader(plan, "low", tiles), 0, solved)
+    for b in range(out_ref.shape[0]):
         out_ref[b] = solved[b * cols + col_id]
 
 
-def chain(values, own, other, rows, cols, slots):
-    per, half, bs = values[0].shape
-    anywhere = pl.BlockSpec(memory_space=pl.ANY)
-    vmem = pl.BlockSpec(memory_space=pltpu.VMEM)
+def call_half(kernel, plan, part, values, extra, line, mine, theirs, out_shape, scratch):
+    rows, cols = plan["rows"], plan["cols"]
+    bs = line.shape[-1]
+    blocks, count, _ = values[0].shape
+    vmem, anywhere = (pl.BlockSpec(memory_space=m) for m in (pltpu.VMEM, pl.ANY))
     return pl.pallas_call(
-        functools.partial(chain_kernel, rows, cols, slots),
-        in_specs=[vmem] * cols + [anywhere] * (2 * cols),
-        out_specs=vmem,
-        out_shape=jax.ShapeDtypeStruct((per, half, bs), jnp.bfloat16),
+        functools.partial(kernel, plan),
+        in_specs=[vmem] * (cols + 1) + [anywhere] * (1 + len(mine) + len(theirs)),
+        out_specs=jax.tree.map(lambda _: vmem, out_shape),
+        out_shape=out_shape,
         scratch_shapes=[
-            pltpu.VMEM((rows, cols, len(slots), bs, bs), jnp.bfloat16),
-            pltpu.VMEM((NB, half, bs), jnp.float32),
-            pltpu.VMEM((NB, half, bs), jnp.bfloat16),
-            pltpu.SemaphoreType.DMA((rows * cols,)),
+            pltpu.VMEM((rows // 2, 2, cols, plan[part][1], bs, bs), jnp.bfloat16),
+            *scratch,
+            pltpu.SemaphoreType.DMA((2 * cols,)),
         ],
         compiler_params=pltpu.CompilerParams(vmem_limit_bytes=VMEM_LIMIT),
-        name="chain",
-    )(*values, *own, *other)
+        name=part + "_half",
+    )(*values, extra, line, *mine, *theirs)
+
+
+def upper_half(plan, values, own, line, mine, theirs):
+    rows, cols, half = plan["rows"], plan["cols"], NB // 2
+    bs, count = line.shape[-1], own.shape[1]
+    return call_half(
+        upper_kernel, plan, "high", values, own, line, mine, theirs,
+        (
+            jax.ShapeDtypeStruct((half, count, bs), jnp.bfloat16),
+            jax.ShapeDtypeStruct(own.shape, jnp.bfloat16),
+        ),
+        [
+            pltpu.VMEM((rows // 2, 2, plan["cross"][1], bs, bs), jnp.bfloat16),
+            pltpu.VMEM((plan["upper"][1] * cols, count, bs), jnp.float32),
+        ],
+    )
+
+
+def lower_half(plan, values, upper, line, mine, theirs):
+    cols, bs, count = plan["cols"], line.shape[-1], upper.shape[1]
+    return call_half(
+        lower_kernel, plan, "low", values, upper, line, mine, theirs,
+        jax.ShapeDtypeStruct((NB // cols, count, bs), jnp.bfloat16),
+        [
+            pltpu.VMEM((plan["lower"][1] * cols, count, bs), jnp.float32),
+            pltpu.VMEM((NB, count, bs), jnp.bfloat16),
+        ],
+    )
+
+
+def gather_tiles(plan, part, line, core):
+    rows, cols = plan["rows"], plan["cols"]
+    first, count = plan[part]
+    piece = lax.dynamic_index_in_dim(line, core, 1, keepdims=False)[:, first : first + count]
+    mine = [along_col(piece, rows, cols, d) for d in range(1, cols)]
+    return mine, [other_core(got, rows, cols) for got in mine]
 
 
 def body(rhs, diag_inv, panel, offdiag, known, row_index):
     rows, cols = lax.axis_size("row"), lax.axis_size("col")
-    zs = rows // 2
-    slots = tile_slots(rows, cols)
-
+    plan = make_plan(rows, cols)
+    core = lax.rem(lax.axis_index("row"), 2)
+
+    folded = fold_panel(panel, diag_inv, plan["slots"])
+    line = lax.all_gather(folded, "row", axis=0)
+    line = line.reshape(rows // 2, 2, *folded.shape)
     known_all = [known] + [along_col(known, rows, cols, d) for d in range(1, cols)]
-    folded = fold_panel(panel, diag_inv, slots)
-    line = jnp.stack([folded] + [along_z(folded, rows, cols, d) for d in range(1, zs)])
-    own = [line] + [along_col(line, rows, cols, d) for d in range(1, cols)]
-    other = [other_core(piece, rows, cols) for piece in own]
 
     sums = segment_sums(offdiag, row_index, known.shape[0] * cols)
     keep, give = local_update(known_all, sums, rhs, diag_inv)
     part = (keep + other_core(give, rows, cols).astype(jnp.float32)).astype(jnp.bfloat16)
-    total = part.astype(jnp.float32)
-    for d in range(1, zs):
-        total = total + along_z(part, rows, cols, d).astype(jnp.float32)
-    total = total.astype(jnp.bfloat16)
-    values = [total] + [along_col(total, rows, cols, d) for d in range(1, cols)]
-
-    mine = chain(values, own, other, rows, cols, slots)
+    parts = [part] + [along_z(part, rows, cols, d) for d in range(1, rows // 2)]
+    total = sum(p.astype(jnp.float32) for p in parts)
+    first, count = plan["upper"]
+    upper = total[first : first + count].astype(jnp.bfloat16)
+    values = [upper] + [along_col(upper, rows, cols, d) for d in range(1, cols)]
+
+    high = gather_tiles(plan, "high", line, core)
+    low = gather_tiles(plan, "low", line, core)
+    solved, lower = upper_half(plan, values, total[: plan["lower"][1]], line, *high)
+    values = [lower] + [along_col(lower, rows, cols, d) for d in range(1, cols)]
+    mine = lower_half(plan, values, solved, line, *low)
     theirs = other_core(mine, rows, cols)
-    first = lax.rem(lax.axis_index("row"), 2) == 0
     return jnp.concatenate(
-        [jnp.where(first, mine, theirs), jnp.where(first, theirs, mine)], axis=1
+        [jnp.where(core == 0, mine, theirs), jnp.where(core == 0, theirs, mine)], axis=1
     )
 
 

time: 120 us -> 90.7 us (0.76)
  waiting for transfers between devices: 68.4 us -> 33.4 us
  between operations: 0.14 us -> 13.6 us
  Pallas kernels: 18.9 us -> 11.3 us
    ppermute x21 -> x26, waiting for transfers between devices: 68.4 us -> 22.8 us  [send(): return lax.ppermute(array, AXES, pairs)]
    all_gather x0 -> x1, waiting for transfers between devices: none -> 10.6 us  [body(): line = lax.all_gather(folded, 'row', axis=0)]
    pallas_call x1 -> x2, Pallas kernels: 10.8 us -> 2.48 us  [call_half(): pl.pallas_call(functools.partial(kernel, plan), in_specs=[vmem] * (cols +...]
    squeeze x0 -> x1, local copies, waits for them, and re-layouts: none -> 1.32 us  [gather_tiles(): lax.dynamic_index_in_dim(line, core, 1, keepdims=False)]
    ppermute x21 -> x26, starting transfers between devices: 28.5 us -> 27.5 us  [send(): return lax.ppermute(array, AXES, pairs)]
  transfers between devices with their start and end apart: 21 -> 27, of which waited for: 15 -> 11; matrix products, arithmetic and copies ran while one was open for 0% -> 2% of each run, Pallas kernels for 6% -> 10%
where the time goes in v2:
time: 90.7 us; the launch traced here: 90.4 us
  waiting for transfers between devices  33.4 us (37%)
  starting transfers between devices  27.5 us (30%)
  between operations  13.6 us (15%)
  Pallas kernels  11.3 us (12%)
  local copies, waits for them, and re-layouts  3.95 us (4%)
    ppermute x26, starting transfers between devices, send(): return lax.ppermute(array, AXES, pairs)  27.5 us
    ppermute x26, waiting for transfers between devices, send(): return lax.ppermute(array, AXES, pairs)  22.8 us
    all_gather x1, waiting for transfers between devices, body(): line = lax.all_gather(folded, 'row', axis=0)  10.6 us
    pallas_call x1, Pallas kernels, segment_sums(): pl.pallas_call(functools.partial(segment_kernel, chunk), grid_spec=pltpu....  7.22 us
    unnamed x14, local copies, waits for them, and re-layouts  2.58 us
    pallas_call x2, Pallas kernels, call_half(): pl.pallas_call(functools.partial(kernel, plan), in_specs=[vmem] * (cols +...  2.48 us
  transfers between devices with their start and end apart: 27, of which 11 were waited for; matrix products, arithmetic and copies ran while one was open for 2% of the time, Pallas kernels for 10%

profile of v2, /device:TPU:0, one launch (start us, length us, event | category | flops | bytes accessed | tf_op | source)
XLA Modules:
  0.0 90.4 jit_solution(13636382153086788820)
XLA Ops:
  6.5 0.9 %copy-done.1 = f32[4,128,128]{2,1,0:T(8,128)S(1)} copy-done((f32[4,128,128]{2,1,0:T(8,128)S(1)}, f32[4,128,128]{2,1,0:T(8,128)}, u32[]{:S(2)}) %copy-start.1) | copy-done | bytes 262168
  7.5 0.9 %copy-done.3 = bf16[2,4,128,128]{3,2,1,0:T(8,128)(2,1)S(1)} copy-done((bf16[2,4,128,128]{3,2,1,0:T(8,128)(2,1)S(1)}, bf16[2,4,128,128]{3,2,1,0:T(8,128)(2,1)}, u32[]{:S(2)}) %copy-start.3) | copy-done | bytes 262168
  8.4 0.9 %fold_panel.1 = bf16[6,128,128]{2,1,0:T(8,128)(2,1)} custom-call(bf16[2,4,128,128]{3,2,1,0:T(8,128)(2,1)S(1)} %copy-done.3, f32[4,128,128]{2,1,0:T(8,128)S(1)} %copy-done.1), custom_call_target="tpu_custom_call" | custom-call | tf_op jit(solution)/shard_map/fold_panel/pallas_call | solution.py:60
  9.4 0.0 all-gather.3.cloned.1.call-update
  9.4 0.0 copy-start.2
  9.4 0.0 copy-start.4
  9.4 0.0 copy-start.5
  9.4 3.0 %collective-permute-start = (bf16[2,64,128]{2,1,0:T(8,128)(2,1)}, bf16[2,64,128]{2,1,0:T(8,128)(2,1)S(1)}, u32[]{:S(2)}, u32[]{:S(2)}) collective-permute-start(bf16[2,64,128]{2,1,0:T(8,128)(2,1)} %refs_0_.1), channel_id=1, source_target_pairs={{0,1},{1,2},{2,3},{3,0},{4,5},{5,6},{6,7},{7,4},{8,9},{9,10},{10,1... | collective-permute-start | bytes 98312 | tf_op jit(solution)/shard_map/ppermute | solution.py:31
  12.4 1.5 %collective-permute-start.1 = (bf16[2,64,128]{2,1,0:T(8,128)(2,1)}, bf16[2,64,128]{2,1,0:T(8,128)(2,1)S(1)}, u32[]{:S(2)}, u32[]{:S(2)}) collective-permute-start(bf16[2,64,128]{2,1,0:T(8,128)(2,1)} %refs_0_.1), channel_id=1, source_target_pairs={{0,2},{1,3},{2,0},{3,1},{4,6},{5,7},{6,4},{7,5},{8,10},{9,11},{10,... | collective-permute-start | bytes 98312 | tf_op jit(solution)/shard_map/ppermute | solution.py:31
  14.0 1.4 %collective-permute-start.2 = (bf16[2,64,128]{2,1,0:T(8,128)(2,1)}, bf16[2,64,128]{2,1,0:T(8,128)(2,1)S(1)}, u32[]{:S(2)}, u32[]{:S(2)}) collective-permute-start(bf16[2,64,128]{2,1,0:T(8,128)(2,1)} %refs_0_.1), channel_id=1, source_target_pairs={{0,3},{1,0},{2,1},{3,2},{4,7},{5,4},{6,5},{7,6},{8,11},{9,8},{10,9... | collective-permute-start | bytes 98312 | tf_op jit(solution)/shard_map/ppermute | solution.py:31
  15.4 0.7 copy-done.6
  16.0 7.2 %segment_sums.1.refs_4_ = bf16[8,128,512]{2,1,0:T(8,128)(2,1)S(1)} custom-call(s32[64]{0:T(128)S(1)} %copy-done.6, bf16[64,4,128,128]{3,2,1,0:T(8,128)(2,1)} %tiles_ref.1), custom_call_target="tpu_custom_call" | custom-call | flops 4194304 | bytes 8388608 | tf_op jit(solution)/shard_map/segment_sums/pallas_call | solution.py:90
  23.3 0.0 collective-permute-done.refs_1_
  23.3 0.0 collective-permute-done.1.refs_2_
  23.3 0.0 collective-permute-done.2.refs_3_
  23.3 0.6 local_update.1
  24.0 0.1 collective-permute-start.3
  24.1 1.2 %collective-permute-done.3 = bf16[4,32,128]{2,1,0:T(8,128)(2,1)S(1)} collective-permute-done((bf16[4,32,128]{2,1,0:T(8,128)(2,1)S(1)}, bf16[4,32,128]{2,1,0:T(8,128)(2,1)S(1)}, u32[]{:S(2)}, u32[]{:S(2)}) %collective-permute-start.3) | collective-permute-done | bytes 32800 | tf_op jit(solution)/shard_map/ppermute | solution.py:31
  25.3 3.7 %collective-permute-start.6 = (bf16[4,32,128]{2,1,0:T(8,128)(2,1)S(1)}, bf16[4,32,128]{2,1,0:T(8,128)(2,1)S(1)}, u32[]{:S(2)}, u32[]{:S(2)}) collective-permute-start(bf16[4,32,128]{2,1,0:T(8,128)(2,1)S(1)} %add_convert_fusion), channel_id=1, source_target_pairs={{0,24},{1,25},{2,26},{3,27},{4,28},{5,29},{6,30},{7,31},{8,0},{9,1... | collective-permute-start | bytes 98312 | tf_op jit(solution)/shard_map/ppermute | solution.py:31
  28.9 0.0 collective-permute-start.5
  28.9 1.0 %collective-permute-start.4 = (bf16[4,32,128]{2,1,0:T(8,128)(2,1)S(1)}, bf16[4,32,128]{2,1,0:T(8,128)(2,1)S(1)}, u32[]{:S(2)}, u32[]{:S(2)}) collective-permute-start(bf16[4,32,128]{2,1,0:T(8,128)(2,1)S(1)} %add_convert_fusion), channel_id=1, source_target_pairs={{0,8},{1,9},{2,10},{3,11},{4,12},{5,13},{6,14},{7,15},{8,16},{9,17... | collective-permute-start | bytes 98312 | tf_op jit(solution)/shard_map/ppermute | solution.py:31
  30.0 10.6 %all-gather.3.cloned.1.call-done = bf16[48,128,128]{2,1,0:T(8,128)(2,1)} async-done(((bf16[6,128,128]{2,1,0:T(8,128)(2,1)}), bf16[48,128,128]{2,1,0:T(8,128)(2,1)}) %all-gather.3.cloned.1.call-update) | async-done | bytes 1572880 | tf_op jit(solution)/shard_map/all_gather | solution.py:325
  40.6 1.3 %dynamic-slice_bitcast_fusion = bf16[4,6,128,128]{3,2,1,0:T(8,128)(2,1)S(1)} fusion(bf16[4,2,6,128,128]{4,3,2,1,0:T(8,128)(2,1)} %bitcast.3, s32[]{:T(128)S(6)} %select_n.18), kind=kLoop, calls=%fused_computation | loop fusion | bytes 1572868 | tf_op jit(solution)/shard_map/jit(dynamic_index_in_dim)/squeeze | solution.py:314
  42.0 1.5 %collective-permute-start.10 = (bf16[4,2,128,128]{3,2,1,0:T(8,128)(2,1)S(1)}, bf16[4,2,128,128]{3,2,1,0:T(8,128)(2,1)S(1)}, u32[]{:S(2)}, u32[]{:S(2)}) collective-permute-start(bf16[4,2,128,128]{3,2,1,0:T(8,128)(2,1)S(1)} %get-tuple-element.14), channel_id=1, source_target_pairs={{0,1},{1,2},{2,3},{3,0},{4,5},{5,6},{6,7},{7,4},{8,9},{9,10},{10,1... | collective-permute-start | bytes 786440 | tf_op jit(solution)/shard_map/ppermute | solution.py:31
  43.5 1.3 %collective-permute-start.11 = (bf16[4,2,128,128]{3,2,1,0:T(8,128)(2,1)S(1)}, bf16[4,2,128,128]{3,2,1,0:T(8,128)(2,1)S(1)}, u32[]{:S(2)}, u32[]{:S(2)}) collective-permute-start(bf16[4,2,128,128]{3,2,1,0:T(8,128)(2,1)S(1)} %get-tuple-element.14), channel_id=1, source_target_pairs={{0,2},{1,3},{2,0},{3,1},{4,6},{5,7},{6,4},{7,5},{8,10},{9,11},{10,... | collective-permute-start | bytes 786440 | tf_op jit(solution)/shard_map/ppermute | solution.py:31
  44.8 0.0 collective-permute-done.6
  44.8 0.0 collective-permute-done.5
  44.8 0.0 collective-permute-done.4
  44.9 0.8 collective-permute-start.7
  45.6 1.5 %collective-permute-start.8 = (bf16[2,32,128]{2,1,0:T(8,128)(2,1)S(1)}, bf16[2,32,128]{2,1,0:T(8,128)(2,1)S(1)}, u32[]{:S(2)}, u32[]{:S(2)}) collective-permute-start(bf16[2,32,128]{2,1,0:T(8,128)(2,1)S(1)} %slice.22.refs_0_), channel_id=1, source_target_pairs={{0,2},{1,3},{2,0},{3,1},{4,6},{5,7},{6,4},{7,5},{8,10},{9,11},{10,... | collective-permute-start | bytes 49160 | tf_op jit(solution)/shard_map/ppermute | solution.py:31
  47.1 1.5 %collective-permute-start.9 = (bf16[2,32,128]{2,1,0:T(8,128)(2,1)S(1)}, bf16[2,32,128]{2,1,0:T(8,128)(2,1)S(1)}, u32[]{:S(2)}, u32[]{:S(2)}) collective-permute-start(bf16[2,32,128]{2,1,0:T(8,128)(2,1)S(1)} %slice.22.refs_0_), channel_id=1, source_target_pairs={{0,3},{1,0},{2,1},{3,2},{4,7},{5,4},{6,5},{7,6},{8,11},{9,8},{10,9... | collective-permute-start | bytes 49160 | tf_op jit(solution)/shard_map/ppermute | solution.py:31
  48.5 3.5 %collective-permute-done.7.refs_1_ = bf16[2,32,128]{2,1,0:T(8,128)(2,1)S(1)} collective-permute-done((bf16[2,32,128]{2,1,0:T(8,128)(2,1)S(1)}, bf16[2,32,128]{2,1,0:T(8,128)(2,1)S(1)}, u32[]{:S(2)}, u32[]{:S(2)}) %collective-permute-start.7) | collective-permute-done | bytes 16416 | tf_op jit(solution)/shard_map/ppermute | solution.py:31
  52.0 1.2 %collective-permute-start.12 = (bf16[4,2,128,128]{3,2,1,0:T(8,128)(2,1)S(1)}, bf16[4,2,128,128]{3,2,1,0:T(8,128)(2,1)S(1)}, u32[]{:S(2)}, u32[]{:S(2)}) collective-permute-start(bf16[4,2,128,128]{3,2,1,0:T(8,128)(2,1)S(1)} %get-tuple-element.14), channel_id=1, source_target_pairs={{0,3},{1,0},{2,1},{3,2},{4,7},{5,4},{6,5},{7,6},{8,11},{9,8},{10,9... | collective-permute-start | bytes 786440 | tf_op jit(solution)/shard_map/ppermute | solution.py:31
  53.2 4.5 %collective-permute-done.8.refs_2_ = bf16[2,32,128]{2,1,0:T(8,128)(2,1)S(1)} collective-permute-done((bf16[2,32,128]{2,1,0:T(8,128)(2,1)S(1)}, bf16[2,32,128]{2,1,0:T(8,128)(2,1)S(1)}, u32[]{:S(2)}, u32[]{:S(2)}) %collective-permute-start.8) | collective-permute-done | bytes 16416 | tf_op jit(solution)/shard_map/ppermute | solution.py:31
  57.7 0.0 collective-permute-start.19
  57.7 0.0 collective-permute-done.9.refs_3_
  57.7 1.5 %collective-permute-start.20 = (bf16[4,2,128,128]{3,2,1,0:T(8,128)(2,1)S(1)}, bf16[4,2,128,128]{3,2,1,0:T(8,128)(2,1)S(1)}, u32[]{:S(2)}, u32[]{:S(2)}) collective-permute-start(bf16[4,2,128,128]{3,2,1,0:T(8,128)(2,1)S(1)} %get-tuple-element.13), channel_id=1, source_target_pairs={{0,2},{1,3},{2,0},{3,1},{4,6},{5,7},{6,4},{7,5},{8,10},{9,11},{10,... | collective-permute-start | bytes 786440 | tf_op jit(solution)/shard_map/ppermute | solution.py:31
  59.2 0.0 collective-permute-done.10.refs_6_
  59.2 2.9 %collective-permute-start.21 = (bf16[4,2,128,128]{3,2,1,0:T(8,128)(2,1)S(1)}, bf16[4,2,128,128]{3,2,1,0:T(8,128)(2,1)S(1)}, u32[]{:S(2)}, u32[]{:S(2)}) collective-permute-start(bf16[4,2,128,128]{3,2,1,0:T(8,128)(2,1)S(1)} %get-tuple-element.13), channel_id=1, source_target_pairs={{0,3},{1,0},{2,1},{3,2},{4,7},{5,4},{6,5},{7,6},{8,11},{9,8},{10,9... | collective-permute-start | bytes 786440 | tf_op jit(solution)/shard_map/ppermute | solution.py:31
  62.1 0.0 collective-permute-done.11.refs_7_
  62.1 0.0 collective-permute-start.13
  62.1 0.0 collective-permute-done.12.refs_8_
  62.1 0.5 collective-permute-start.14
  62.6 5.2 %collective-permute-done.19.refs_6_ = bf16[4,2,128,128]{3,2,1,0:T(8,128)(2,1)S(1)} collective-permute-done((bf16[4,2,128,128]{3,2,1,0:T(8,128)(2,1)S(1)}, bf16[4,2,128,128]{3,2,1,0:T(8,128)(2,1)S(1)}, u32[]{:S(2)}, u32[]{:S(2)}) %collective-permute-start.19) | collective-permute-done | bytes 262176 | tf_op jit(solution)/shard_map/ppermute | solution.py:31
  67.8 0.0 collective-permute-start.15
  67.8 3.7 %collective-permute-done.20.refs_7_ = bf16[4,2,128,128]{3,2,1,0:T(8,128)(2,1)S(1)} collective-permute-done((bf16[4,2,128,128]{3,2,1,0:T(8,128)(2,1)S(1)}, bf16[4,2,128,128]{3,2,1,0:T(8,128)(2,1)S(1)}, u32[]{:S(2)}, u32[]{:S(2)}) %collective-permute-start.20) | collective-permute-done | bytes 262176 | tf_op jit(solution)/shard_map/ppermute | solution.py:31
  71.5 0.0 collective-permute-start.22
  71.5 0.9 %collective-permute-done.21.refs_8_ = bf16[4,2,128,128]{3,2,1,0:T(8,128)(2,1)S(1)} collective-permute-done((bf16[4,2,128,128]{3,2,1,0:T(8,128)(2,1)S(1)}, bf16[4,2,128,128]{3,2,1,0:T(8,128)(2,1)S(1)}, u32[]{:S(2)}, u32[]{:S(2)}) %collective-permute-start.21) | collective-permute-done | bytes 262176 | tf_op jit(solution)/shard_map/ppermute | solution.py:31
  72.5 0.0 collective-permute-start.23
  72.5 0.5 collective-permute-start.24
  73.0 0.0 collective-permute-done.14.refs_10_
  73.0 0.0 collective-permute-done.15.refs_11_
  73.0 1.4 %high_half.1 = (bf16[8,32,128]{2,1,0:T(8,128)(2,1)S(1)}, bf16[2,32,128]{2,1,0:T(8,128)(2,1)S(1)}) custom-call(bf16[2,32,128]{2,1,0:T(8,128)(2,1)S(1)} %slice.22.refs_0_, bf16[2,32,128]{2,1,0:T(8,128)(2,1)S(1)} %collective-permute-done.7.refs_1_, bf16[2,32,128]{2,1,0:T(8,128)(2,1)S(1)} %collective-permute-done.8.refs_2_, ...), custom_call_target="tpu_custom_call" | custom-call | tf_op jit(solution)/shard_map/high_half/pallas_call | solution.py:268
  74.4 1.8 %collective-permute-start.16 = (bf16[2,32,128]{2,1,0:T(8,128)(2,1)S(1)}, bf16[2,32,128]{2,1,0:T(8,128)(2,1)S(1)}, u32[]{:S(2)}, u32[]{:S(2)}) collective-permute-start(bf16[2,32,128]{2,1,0:T(8,128)(2,1)S(1)} %get-tuple-element.11.refs_0_), channel_id=1, source_target_pairs={{0,1},{1,2},{2,3},{3,0},{4,5},{5,6},{6,7},{7,4},{8,9},{9,10},{10,1... | collective-permute-start | bytes 49160 | tf_op jit(solution)/shard_map/ppermute | solution.py:31
  76.2 0.6 collective-permute-start.17
  76.8 1.2 %collective-permute-start.18 = (bf16[2,32,128]{2,1,0:T(8,128)(2,1)S(1)}, bf16[2,32,128]{2,1,0:T(8,128)(2,1)S(1)}, u32[]{:S(2)}, u32[]{:S(2)}) collective-permute-start(bf16[2,32,128]{2,1,0:T(8,128)(2,1)S(1)} %get-tuple-element.11.refs_0_), channel_id=1, source_target_pairs={{0,3},{1,0},{2,1},{3,2},{4,7},{5,4},{6,5},{7,6},{8,11},{9,8},{10,9... | collective-permute-start | bytes 49160 | tf_op jit(solution)/shard_map/ppermute | solution.py:31
  78.0 0.0 collective-permute-done.24.refs_11_
  78.0 1.1 %collective-permute-done.16.refs_1_ = bf16[2,32,128]{2,1,0:T(8,128)(2,1)S(1)} collective-permute-done((bf16[2,32,128]{2,1,0:T(8,128)(2,1)S(1)}, bf16[2,32,128]{2,1,0:T(8,128)(2,1)S(1)}, u32[]{:S(2)}, u32[]{:S(2)}) %collective-permute-start.16) | collective-permute-done | bytes 16416 | tf_op jit(solution)/shard_map/ppermute | solution.py:31
  79.1 0.9 collective-permute-done.17.refs_2_
  80.0 0.6 collective-permute-done.18.refs_3_
  80.6 1.1 %low_half.1 = bf16[4,32,128]{2,1,0:T(8,128)(2,1)S(1)} custom-call(bf16[2,32,128]{2,1,0:T(8,128)(2,1)S(1)} %get-tuple-element.11.refs_0_, bf16[2,32,128]{2,1,0:T(8,128)(2,1)S(1)} %collective-permute-done.16.refs_1_, bf16[2,32,128]{2,1,0:T(8,128)(2,1)S(1)} %collective-permute-done.17.refs_2_, bf16[2,32,128]{2,1,0:T(8,128)(2,1)S(1)} %collective-permute-done.18.refs_3_, ...), custom_call_target="tpu_custom_call" | custom-call | tf_op jit(solution)/shard_map/low_half/pallas_call | solution.py:268
  81.7 0.1 collective-permute-start.25
  81.7 1.2 %collective-permute-done.25 = bf16[4,32,128]{2,1,0:T(8,128)(2,1)S(1)} collective-permute-done((bf16[4,32,128]{2,1,0:T(8,128)(2,1)S(1)}, bf16[4,32,128]{2,1,0:T(8,128)(2,1)S(1)}, u32[]{:S(2)}, u32[]{:S(2)}) %collective-permute-start.25) | collective-permute-done | bytes 32800 | tf_op jit(solution)/shard_map/ppermute | solution.py:31
  82.9 0.6 pad_maximum_fusion
  (18 shorter events, 0.1 us)
Async XLA Ops:
  6.5 34.1 %all-gather.3.cloned.1.call-start = ((), (), s32[]{:S(2)}) async-start(), calls=%async_computation | async-start | bytes 1769472 | tf_op jit(solution)/shard_map/all_gather | solution.py:325
  6.5 0.9 %copy-start.1 = (f32[4,128,128]{2,1,0:T(8,128)S(1)}, f32[4,128,128]{2,1,0:T(8,128)}, u32[]{:S(2)}) copy-start(f32[4,128,128]{2,1,0:T(8,128)} %inverse_ref.1) | copy-start | bytes 786436
  7.5 0.9 %copy-start.3 = (bf16[2,4,128,128]{3,2,1,0:T(8,128)(2,1)S(1)}, bf16[2,4,128,128]{3,2,1,0:T(8,128)(2,1)}, u32[]{:S(2)}) copy-start(bf16[2,4,128,128]{3,2,1,0:T(8,128)(2,1)} %panel_ref.1) | copy-start | bytes 786436
  9.4 13.9 %copy-start.2 = (f32[4,128,128]{2,1,0:T(8,128)S(1)}, f32[4,128,128]{2,1,0:T(8,128)}, u32[]{:S(2)}) copy-start(f32[4,128,128]{2,1,0:T(8,128)} %inverse_ref.1) | copy-start | bytes 786436
  9.4 13.9 %copy-start.4 = (f32[4,64,128]{2,1,0:T(8,128)S(1)}, f32[4,64,128]{2,1,0:T(8,128)}, u32[]{:S(2)}) copy-start(f32[4,64,128]{2,1,0:T(8,128)} %refs_5_.1) | copy-start | bytes 393220
  9.4 13.9 %copy-start.5 = (bf16[2,64,128]{2,1,0:T(8,128)(2,1)S(1)}, bf16[2,64,128]{2,1,0:T(8,128)(2,1)}, u32[]{:S(2)}) copy-start(bf16[2,64,128]{2,1,0:T(8,128)(2,1)} %refs_0_.1) | copy-start | bytes 98308
  9.4 13.8 %collective-permute-start = (bf16[2,64,128]{2,1,0:T(8,128)(2,1)}, bf16[2,64,128]{2,1,0:T(8,128)(2,1)S(1)}, u32[]{:S(2)}, u32[]{:S(2)}) collective-permute-start(bf16[2,64,128]{2,1,0:T(8,128)(2,1)} %refs_0_.1), channel_id=1, source_target_pairs={{0,1},{1,2},{2,3},{3,0},{4,5},{5,6},{6,7},{7,4},{8,9},{9,10},{10,1... | collective-permute-start | bytes 98312 | tf_op jit(solution)/shard_map/ppermute | solution.py:31
  12.4 10.9 %collective-permute-start.1 = (bf16[2,64,128]{2,1,0:T(8,128)(2,1)}, bf16[2,64,128]{2,1,0:T(8,128)(2,1)S(1)}, u32[]{:S(2)}, u32[]{:S(2)}) collective-permute-start(bf16[2,64,128]{2,1,0:T(8,128)(2,1)} %refs_0_.1), channel_id=1, source_target_pairs={{0,2},{1,3},{2,0},{3,1},{4,6},{5,7},{6,4},{7,5},{8,10},{9,11},{10,... | collective-permute-start | bytes 98312 | tf_op jit(solution)/shard_map/ppermute | solution.py:31
  14.0 9.3 %collective-permute-start.2 = (bf16[2,64,128]{2,1,0:T(8,128)(2,1)}, bf16[2,64,128]{2,1,0:T(8,128)(2,1)S(1)}, u32[]{:S(2)}, u32[]{:S(2)}) collective-permute-start(bf16[2,64,128]{2,1,0:T(8,128)(2,1)} %refs_0_.1), channel_id=1, source_target_pairs={{0,3},{1,0},{2,1},{3,2},{4,7},{5,4},{6,5},{7,6},{8,11},{9,8},{10,9... | collective-permute-start | bytes 98312 | tf_op jit(solution)/shard_map/ppermute | solution.py:31
  15.4 0.7 copy-start.6
  24.0 1.3 %collective-permute-start.3 = (bf16[4,32,128]{2,1,0:T(8,128)(2,1)S(1)}, bf16[4,32,128]{2,1,0:T(8,128)(2,1)S(1)}, u32[]{:S(2)}, u32[]{:S(2)}) collective-permute-start(bf16[4,32,128]{2,1,0:T(8,128)(2,1)S(1)} %get-tuple-element.10), channel_id=1, source_target_pairs={{0,4},{1,5},{2,6},{3,7},{4,0},{5,1},{6,2},{7,3},{8,12},{9,13},{10,... | collective-permute-start | bytes 98312 | tf_op jit(solution)/shard_map/ppermute | solution.py:31
  25.3 19.5 %collective-permute-start.6 = (bf16[4,32,128]{2,1,0:T(8,128)(2,1)S(1)}, bf16[4,32,128]{2,1,0:T(8,128)(2,1)S(1)}, u32[]{:S(2)}, u32[]{:S(2)}) collective-permute-start(bf16[4,32,128]{2,1,0:T(8,128)(2,1)S(1)} %add_convert_fusion), channel_id=1, source_target_pairs={{0,24},{1,25},{2,26},{3,27},{4,28},{5,29},{6,30},{7,31},{8,0},{9,1... | collective-permute-start | bytes 98312 | tf_op jit(solution)/shard_map/ppermute | solution.py:31
  28.9 15.9 %collective-permute-start.5 = (bf16[4,32,128]{2,1,0:T(8,128)(2,1)S(1)}, bf16[4,32,128]{2,1,0:T(8,128)(2,1)S(1)}, u32[]{:S(2)}, u32[]{:S(2)}) collective-permute-start(bf16[4,32,128]{2,1,0:T(8,128)(2,1)S(1)} %add_convert_fusion), channel_id=1, source_target_pairs={{0,16},{1,17},{2,18},{3,19},{4,20},{5,21},{6,22},{7,23},{8,24},{9,... | collective-permute-start | bytes 98312 | tf_op jit(solution)/shard_map/ppermute | solution.py:31
  28.9 15.9 %collective-permute-start.4 = (bf16[4,32,128]{2,1,0:T(8,128)(2,1)S(1)}, bf16[4,32,128]{2,1,0:T(8,128)(2,1)S(1)}, u32[]{:S(2)}, u32[]{:S(2)}) collective-permute-start(bf16[4,32,128]{2,1,0:T(8,128)(2,1)S(1)} %add_convert_fusion), channel_id=1, source_target_pairs={{0,8},{1,9},{2,10},{3,11},{4,12},{5,13},{6,14},{7,15},{8,16},{9,17... | collective-permute-start | bytes 98312 | tf_op jit(solution)/shard_map/ppermute | solution.py:31
  40.6 32.4 %copy-start = (bf16[48,128,128]{2,1,0:T(8,128)(2,1)S(1)}, bf16[48,128,128]{2,1,0:T(8,128)(2,1)}, u32[]{:S(2)}) copy-start(bf16[48,128,128]{2,1,0:T(8,128)(2,1)} %all-gather.3.cloned.1.call-done) | copy-start | bytes 4718596
  42.0 17.2 %collective-permute-start.10 = (bf16[4,2,128,128]{3,2,1,0:T(8,128)(2,1)S(1)}, bf16[4,2,128,128]{3,2,1,0:T(8,128)(2,1)S(1)}, u32[]{:S(2)}, u32[]{:S(2)}) collective-permute-start(bf16[4,2,128,128]{3,2,1,0:T(8,128)(2,1)S(1)} %get-tuple-element.14), channel_id=1, source_target_pairs={{0,1},{1,2},{2,3},{3,0},{4,5},{5,6},{6,7},{7,4},{8,9},{9,10},{10,1... | collective-permute-start | bytes 786440 | tf_op jit(solution)/shard_map/ppermute | solution.py:31
  43.5 18.6 %collective-permute-start.11 = (bf16[4,2,128,128]{3,2,1,0:T(8,128)(2,1)S(1)}, bf16[4,2,128,128]{3,2,1,0:T(8,128)(2,1)S(1)}, u32[]{:S(2)}, u32[]{:S(2)}) collective-permute-start(bf16[4,2,128,128]{3,2,1,0:T(8,128)(2,1)S(1)} %get-tuple-element.14), channel_id=1, source_target_pairs={{0,2},{1,3},{2,0},{3,1},{4,6},{5,7},{6,4},{7,5},{8,10},{9,11},{10,... | collective-permute-start | bytes 786440 | tf_op jit(solution)/shard_map/ppermute | solution.py:31
  44.9 7.1 %collective-permute-start.7 = (bf16[2,32,128]{2,1,0:T(8,128)(2,1)S(1)}, bf16[2,32,128]{2,1,0:T(8,128)(2,1)S(1)}, u32[]{:S(2)}, u32[]{:S(2)}) collective-permute-start(bf16[2,32,128]{2,1,0:T(8,128)(2,1)S(1)} %slice.22.refs_0_), channel_id=1, source_target_pairs={{0,1},{1,2},{2,3},{3,0},{4,5},{5,6},{6,7},{7,4},{8,9},{9,10},{10,1... | collective-permute-start | bytes 49160 | tf_op jit(solution)/shard_map/ppermute | solution.py:31
  45.6 12.1 %collective-permute-start.8 = (bf16[2,32,128]{2,1,0:T(8,128)(2,1)S(1)}, bf16[2,32,128]{2,1,0:T(8,128)(2,1)S(1)}, u32[]{:S(2)}, u32[]{:S(2)}) collective-permute-start(bf16[2,32,128]{2,1,0:T(8,128)(2,1)S(1)} %slice.22.refs_0_), channel_id=1, source_target_pairs={{0,2},{1,3},{2,0},{3,1},{4,6},{5,7},{6,4},{7,5},{8,10},{9,11},{10,... | collective-permute-start | bytes 49160 | tf_op jit(solution)/shard_map/ppermute | solution.py:31
  47.1 10.6 %collective-permute-start.9 = (bf16[2,32,128]{2,1,0:T(8,128)(2,1)S(1)}, bf16[2,32,128]{2,1,0:T(8,128)(2,1)S(1)}, u32[]{:S(2)}, u32[]{:S(2)}) collective-permute-start(bf16[2,32,128]{2,1,0:T(8,128)(2,1)S(1)} %slice.22.refs_0_), channel_id=1, source_target_pairs={{0,3},{1,0},{2,1},{3,2},{4,7},{5,4},{6,5},{7,6},{8,11},{9,8},{10,9... | collective-permute-start | bytes 49160 | tf_op jit(solution)/shard_map/ppermute | solution.py:31
  52.0 10.1 %collective-permute-start.12 = (bf16[4,2,128,128]{3,2,1,0:T(8,128)(2,1)S(1)}, bf16[4,2,128,128]{3,2,1,0:T(8,128)(2,1)S(1)}, u32[]{:S(2)}, u32[]{:S(2)}) collective-permute-start(bf16[4,2,128,128]{3,2,1,0:T(8,128)(2,1)S(1)} %get-tuple-element.14), channel_id=1, source_target_pairs={{0,3},{1,0},{2,1},{3,2},{4,7},{5,4},{6,5},{7,6},{8,11},{9,8},{10,9... | collective-permute-start | bytes 786440 | tf_op jit(solution)/shard_map/ppermute | solution.py:31
  57.7 10.1 %collective-permute-start.19 = (bf16[4,2,128,128]{3,2,1,0:T(8,128)(2,1)S(1)}, bf16[4,2,128,128]{3,2,1,0:T(8,128)(2,1)S(1)}, u32[]{:S(2)}, u32[]{:S(2)}) collective-permute-start(bf16[4,2,128,128]{3,2,1,0:T(8,128)(2,1)S(1)} %get-tuple-element.13), channel_id=1, source_target_pairs={{0,1},{1,2},{2,3},{3,0},{4,5},{5,6},{6,7},{7,4},{8,9},{9,10},{10,1... | collective-permute-start | bytes 786440 | tf_op jit(solution)/shard_map/ppermute | solution.py:31
  57.7 13.8 %collective-permute-start.20 = (bf16[4,2,128,128]{3,2,1,0:T(8,128)(2,1)S(1)}, bf16[4,2,128,128]{3,2,1,0:T(8,128)(2,1)S(1)}, u32[]{:S(2)}, u32[]{:S(2)}) collective-permute-start(bf16[4,2,128,128]{3,2,1,0:T(8,128)(2,1)S(1)} %get-tuple-element.13), channel_id=1, source_target_pairs={{0,2},{1,3},{2,0},{3,1},{4,6},{5,7},{6,4},{7,5},{8,10},{9,11},{10,... | collective-permute-start | bytes 786440 | tf_op jit(solution)/shard_map/ppermute | solution.py:31
  59.2 13.3 %collective-permute-start.21 = (bf16[4,2,128,128]{3,2,1,0:T(8,128)(2,1)S(1)}, bf16[4,2,128,128]{3,2,1,0:T(8,128)(2,1)S(1)}, u32[]{:S(2)}, u32[]{:S(2)}) collective-permute-start(bf16[4,2,128,128]{3,2,1,0:T(8,128)(2,1)S(1)} %get-tuple-element.13), channel_id=1, source_target_pairs={{0,3},{1,0},{2,1},{3,2},{4,7},{5,4},{6,5},{7,6},{8,11},{9,8},{10,9... | collective-permute-start | bytes 786440 | tf_op jit(solution)/shard_map/ppermute | solution.py:31
  62.1 10.4 %collective-permute-start.13 = (bf16[4,2,128,128]{3,2,1,0:T(8,128)(2,1)S(1)}, bf16[4,2,128,128]{3,2,1,0:T(8,128)(2,1)S(1)}, u32[]{:S(2)}, u32[]{:S(2)}) collective-permute-start(bf16[4,2,128,128]{3,2,1,0:T(8,128)(2,1)S(1)} %collective-permute-done.10.refs_6_), channel_id=1, source_target_pairs={{0,4},{1,5},{2,6},{3,7},{4,0},{5,1},{6,2},{7,3},{8,12},{9,13},{10,... | collective-permute-start | bytes 786440 | tf_op jit(solution)/shard_map/ppermute | solution.py:31
  62.1 10.9 %collective-permute-start.14 = (bf16[4,2,128,128]{3,2,1,0:T(8,128)(2,1)S(1)}, bf16[4,2,128,128]{3,2,1,0:T(8,128)(2,1)S(1)}, u32[]{:S(2)}, u32[]{:S(2)}) collective-permute-start(bf16[4,2,128,128]{3,2,1,0:T(8,128)(2,1)S(1)} %collective-permute-done.11.refs_7_), channel_id=1, source_target_pairs={{0,4},{1,5},{2,6},{3,7},{4,0},{5,1},{6,2},{7,3},{8,12},{9,13},{10,... | collective-permute-start | bytes 786440 | tf_op jit(solution)/shard_map/ppermute | solution.py:31
  67.8 5.2 %collective-permute-start.15 = (bf16[4,2,128,128]{3,2,1,0:T(8,128)(2,1)S(1)}, bf16[4,2,128,128]{3,2,1,0:T(8,128)(2,1)S(1)}, u32[]{:S(2)}, u32[]{:S(2)}) collective-permute-start(bf16[4,2,128,128]{3,2,1,0:T(8,128)(2,1)S(1)} %collective-permute-done.12.refs_8_), channel_id=1, source_target_pairs={{0,4},{1,5},{2,6},{3,7},{4,0},{5,1},{6,2},{7,3},{8,12},{9,13},{10,... | collective-permute-start | bytes 786440 | tf_op jit(solution)/shard_map/ppermute | solution.py:31
  71.5 5.3 %collective-permute-start.22 = (bf16[4,2,128,128]{3,2,1,0:T(8,128)(2,1)S(1)}, bf16[4,2,128,128]{3,2,1,0:T(8,128)(2,1)S(1)}, u32[]{:S(2)}, u32[]{:S(2)}) collective-permute-start(bf16[4,2,128,128]{3,2,1,0:T(8,128)(2,1)S(1)} %collective-permute-done.19.refs_6_), channel_id=1, source_target_pairs={{0,4},{1,5},{2,6},{3,7},{4,0},{5,1},{6,2},{7,3},{8,12},{9,13},{10,... | collective-permute-start | bytes 786440 | tf_op jit(solution)/shard_map/ppermute | solution.py:31
  72.5 5.5 %collective-permute-start.23 = (bf16[4,2,128,128]{3,2,1,0:T(8,128)(2,1)S(1)}, bf16[4,2,128,128]{3,2,1,0:T(8,128)(2,1)S(1)}, u32[]{:S(2)}, u32[]{:S(2)}) collective-permute-start(bf16[4,2,128,128]{3,2,1,0:T(8,128)(2,1)S(1)} %collective-permute-done.20.refs_7_), channel_id=1, source_target_pairs={{0,4},{1,5},{2,6},{3,7},{4,0},{5,1},{6,2},{7,3},{8,12},{9,13},{10,... | collective-permute-start | bytes 786440 | tf_op jit(solution)/shard_map/ppermute | solution.py:31
  72.5 5.5 %collective-permute-start.24 = (bf16[4,2,128,128]{3,2,1,0:T(8,128)(2,1)S(1)}, bf16[4,2,128,128]{3,2,1,0:T(8,128)(2,1)S(1)}, u32[]{:S(2)}, u32[]{:S(2)}) collective-permute-start(bf16[4,2,128,128]{3,2,1,0:T(8,128)(2,1)S(1)} %collective-permute-done.21.refs_8_), channel_id=1, source_target_pairs={{0,4},{1,5},{2,6},{3,7},{4,0},{5,1},{6,2},{7,3},{8,12},{9,13},{10,... | collective-permute-start | bytes 786440 | tf_op jit(solution)/shard_map/ppermute | solution.py:31
  74.4 4.7 %collective-permute-start.16 = (bf16[2,32,128]{2,1,0:T(8,128)(2,1)S(1)}, bf16[2,32,128]{2,1,0:T(8,128)(2,1)S(1)}, u32[]{:S(2)}, u32[]{:S(2)}) collective-permute-start(bf16[2,32,128]{2,1,0:T(8,128)(2,1)S(1)} %get-tuple-element.11.refs_0_), channel_id=1, source_target_pairs={{0,1},{1,2},{2,3},{3,0},{4,5},{5,6},{6,7},{7,4},{8,9},{9,10},{10,1... | collective-permute-start | bytes 49160 | tf_op jit(solution)/shard_map/ppermute | solution.py:31
  76.2 3.7 %collective-permute-start.17 = (bf16[2,32,128]{2,1,0:T(8,128)(2,1)S(1)}, bf16[2,32,128]{2,1,0:T(8,128)(2,1)S(1)}, u32[]{:S(2)}, u32[]{:S(2)}) collective-permute-start(bf16[2,32,128]{2,1,0:T(8,128)(2,1)S(1)} %get-tuple-element.11.refs_0_), channel_id=1, source_target_pairs={{0,2},{1,3},{2,0},{3,1},{4,6},{5,7},{6,4},{7,5},{8,10},{9,11},{10,... | collective-permute-start | bytes 49160 | tf_op jit(solution)/shard_map/ppermute | solution.py:31
  76.8 3.7 %collective-permute-start.18 = (bf16[2,32,128]{2,1,0:T(8,128)(2,1)S(1)}, bf16[2,32,128]{2,1,0:T(8,128)(2,1)S(1)}, u32[]{:S(2)}, u32[]{:S(2)}) collective-permute-start(bf16[2,32,128]{2,1,0:T(8,128)(2,1)S(1)} %get-tuple-element.11.refs_0_), channel_id=1, source_target_pairs={{0,3},{1,0},{2,1},{3,2},{4,7},{5,4},{6,5},{7,6},{8,11},{9,8},{10,9... | collective-permute-start | bytes 49160 | tf_op jit(solution)/shard_map/ppermute | solution.py:31
  81.7 1.3 %collective-permute-start.25 = (bf16[4,32,128]{2,1,0:T(8,128)(2,1)S(1)}, bf16[4,32,128]{2,1,0:T(8,128)(2,1)S(1)}, u32[]{:S(2)}, u32[]{:S(2)}) collective-permute-start(bf16[4,32,128]{2,1,0:T(8,128)(2,1)S(1)} %low_half.1), channel_id=1, source_target_pairs={{0,4},{1,5},{2,6},{3,7},{4,0},{5,1},{6,2},{7,3},{8,12},{9,13},{10,... | collective-permute-start | bytes 98312 | tf_op jit(solution)/shard_map/ppermute | solution.py:31
Sparse Core Ops, SparseCore 0:
  9.5 31.0 all-gather.2

commit v3 on v0

v3 whole, which is shorter than its diff:
```python
import functools

import jax
import jax.numpy as jnp
from jax import lax
from jax.experimental import pallas as pl
from jax.experimental.pallas import tpu as pltpu
from jax.sharding import PartitionSpec as P

NB = 16
AXES = ("row", "col")
VMEM_LIMIT = 16 * 1024 * 1024
HIGHEST = lax.Precision.HIGHEST


class Plan:
    def __init__(self, rows, cols):
        self.rows, self.cols, self.zs = rows, cols, rows // 2
        self.slots = [
            (a, b)
            for a in reversed(range(NB // rows))
            for b in reversed(range(NB // cols))
            if a * rows + rows - 1 > b * cols
        ]
        self.lists = {
            (core, c): [
                (r, at)
                for r in range(core, rows, 2)
                for at, (a, b) in enumerate(self.slots)
                if a * rows + r > b * cols + c
            ]
            for core in range(2)
            for c in range(cols)
        }
        self.packed = max(2, *map(len, self.lists.values()))
        self.cut = self.packed // 2
        self.flips = [1 << i for i in range(cols.bit_length() - 1)]
        self.solvers = sorted({max(self.zs // 2 - 1, 0), self.zs // 2})


def send(array, plan, pairs):
    flat = [(r * plan.cols + c, to_r * plan.cols + to_c) for (r, c), (to_r, to_c) in pairs]
    return lax.ppermute(array, AXES, flat)


def across_z(array, plan, flip):
    to = {z ^ flip: z for z in plan.solvers}
    free = [z for z in range(plan.zs) if z not in to.values()]
    for z in range(plan.zs):
        if z not in to:
            to[z] = min(free, key=lambda other: abs(other - z))
            free.remove(to[z])
    pairs = [
        ((2 * z + core, c), (2 * to[z] + core, c))
        for z in range(plan.zs)
        for core in range(2)
        for c in range(plan.cols)
    ]
    return send(array, plan, pairs)


def out_of_solvers(array, plan):
    low, high = plan.solvers[0], plan.solvers[-1]
    z = lax.axis_index("row") // 2
    for step in range(1, plan.zs // 2):
        to = {low: low - step, high: high + step, low - step: low, high + step: high}
        pairs = [
            ((2 * a + core, c), (2 * to.get(a, a) + core, c))
            for a in range(plan.zs)
            for core in range(2)
            for c in range(plan.cols)
        ]
        got = send(array, plan, pairs)
        array = jnp.where(jnp.logical_or(z == low - step, z == high + step), got, array)
    return array


def across_col(array, plan, flip):
    pairs = [((r, c), (r, c ^ flip)) for r in range(plan.rows) for c in range(plan.cols)]
    return send(array, plan, pairs)


def other_core(array, plan):
    pairs = [((r, c), (r ^ 1, c)) for r in range(plan.rows) for c in range(plan.cols)]
    return send(array, plan, pairs)


def direct(array, plan):
    return jnp.stack([array] + [across_col(array, plan, m) for m in range(1, plan.cols)])


NO_COST = pl.CostEstimate(flops=0, bytes_accessed=0, transcendentals=0)


def fold_kernel(slots, panel_hbm, inverse_hbm, out_ref, panel_ref, inverse_ref, sems):
    copies = [
        pltpu.make_async_copy(inverse_hbm, inverse_ref, sems.at[0]),
        pltpu.make_async_copy(panel_hbm, panel_ref, sems.at[1]),
    ]
    for copy in copies:
        copy.start()
    for copy in copies:
        copy.wait()
    for at, (a, b) in enumerate(slots):
        inverse = inverse_ref[b]
        high = inverse.astype(jnp.bfloat16)
        low = (inverse - high.astype(jnp.float32)).astype(jnp.bfloat16)
        tile = panel_ref[a, b]
        out_ref[at] = (
            jnp.dot(tile, high, preferred_element_type=jnp.float32)
            + jnp.dot(tile, low, preferred_element_type=jnp.float32)
        ).astype(jnp.bfloat16)


def fold_panel(panel, inverse, slots):
    bs = panel.shape[-1]
    return pl.pallas_call(
        functools.partial(fold_kernel, slots),
        in_specs=[pl.BlockSpec(memory_space=pltpu.HBM)] * 2,
        out_shape=jax.ShapeDtypeStruct((len(slots), bs, bs), jnp.bfloat16),
        scratch_shapes=[
            pltpu.VMEM(panel.shape, panel.dtype),
            pltpu.VMEM(inverse.shape, inverse.dtype),
            pltpu.SemaphoreType.DMA((2,)),
        ],
        compiler_params=pltpu.CompilerParams(vmem_limit_bytes=62 * 1024 * 1024),
        cost_estimate=NO_COST,
        name="fold_panel",
    )(panel, inverse)


def segment_kernel(chunk, index_ref, tiles_hbm, out_ref, tiles, sums, sems):
    copies = [
        pltpu.make_async_copy(
            tiles_hbm.at[pl.ds(i * chunk, chunk)], tiles.at[pl.ds(i * chunk, chunk)], sems.at[i]
        )
        for i in range(tiles.shape[0] // chunk)
    ]
    for copy in copies:
        copy.start()
    sums[...] = jnp.zeros_like(sums)
    for i, copy in enumerate(copies):
        copy.wait()

        def add(p, carry):
            sums[index_ref[p]] += tiles[p].astype(jnp.float32)
            return carry

        lax.fori_loop(i * chunk, (i + 1) * chunk, add, 0)
    out_ref[...] = sums[...].astype(jnp.bfloat16)


def segment_sums(offdiag, row_index, segments):
    tiles, blocks, bs, _ = offdiag.shape
    chunk = 4
    return pl.pallas_call(
        functools.partial(segment_kernel, chunk),
        in_specs=[pl.BlockSpec(memory_space=pltpu.SMEM), pl.BlockSpec(memory_space=pltpu.HBM)],
        out_shape=jax.ShapeDtypeStruct((segments, blocks, bs, bs), jnp.bfloat16),
        scratch_shapes=[
            pltpu.VMEM(offdiag.shape, offdiag.dtype),
            pltpu.VMEM((segments, blocks, bs, bs), jnp.float32),
            pltpu.SemaphoreType.DMA((tiles // chunk,)),
        ],
        compiler_params=pltpu.CompilerParams(vmem_limit_bytes=58 * 1024 * 1024),
        cost_estimate=pl.CostEstimate(
            flops=offdiag.size, bytes_accessed=2 * offdiag.size, transcendentals=0
        ),
        name="segment_sums",
    )(row_index, offdiag)


def update_kernel(known_ref, sums_ref, rhs_ref, inverse_ref, keep_ref, give_ref, whole):
    blocks, count, bs = rhs_ref.shape
    cols, per = known_ref.shape[:2]
    row_id, col_id = lax.axis_index("row"), lax.axis_index("col")
    off = [jnp.zeros((count, bs), jnp.float32)] * blocks
    for step in range(cols):
        first = lax.bitwise_xor(col_id, step) * per
        for i in range(per):
            for b in range(blocks):
                off[b] += jnp.dot(
                    known_ref[step, i], sums_ref[first + i, b], preferred_element_type=jnp.float32
                )
    adds = (row_id == 0).astype(jnp.float32)
    for b in range(blocks):
        total = rhs_ref[b] * adds - off[b]
        whole[b] = jnp.dot(
            total, inverse_ref[b], precision=HIGHEST, preferred_element_type=jnp.float32
        )
    half = count // 2
    core = lax.rem(row_id, 2)
    keep = pl.ds(pl.multiple_of(core * half, half), half)
    give = pl.ds(pl.multiple_of((1 - core) * half, half), half)
    keep_ref[...] = whole[:, keep, :]
    give_ref[...] = whole[:, give, :].astype(jnp.bfloat16)


def local_update(known, sums, rhs, inverse):
    blocks, count, bs = rhs.shape
    half = (blocks, count // 2, bs)
    return pl.pallas_call(
        update_kernel,
        out_shape=(
            jax.ShapeDtypeStruct(half, jnp.float32),
            jax.ShapeDtypeStruct(half, jnp.bfloat16),
        ),
        scratch_shapes=[pltpu.VMEM(rhs.shape, jnp.float32)],
        compiler_params=pltpu.CompilerParams(vmem_limit_bytes=VMEM_LIMIT),
        cost_estimate=NO_COST,
        name="local_update",
    )(known, sums, rhs, inverse)


def pack_kernel(plan, *refs):
    line_refs, (first_ref, second_ref) = refs[: plan.zs], refs[plan.zs :]
    row_id, col_id = lax.axis_index("row"), lax.axis_index("col")
    core, z = lax.rem(row_id, 2), row_id // 2
    for i in range(plan.packed):
        into = first_ref.at[i] if i < plan.cut else second_ref.at[i - plan.cut]
        back, at = jnp.int32(0), jnp.int32(0)
        for (side, c), found in plan.lists.items():
            if i < len(found):
                mine = jnp.logical_and(col_id == c, core == side)
                back = jnp.where(mine, lax.bitwise_xor(z, found[i][0] // 2), back)
                at = jnp.where(mine, found[i][1], at)
        for step, line_ref in enumerate(line_refs):

            @pl.when(back == step)
            def _():
                into[...] = line_ref[at]


def pack(plan, line):
    bs = line[0].shape[-1]
    return pl.pallas_call(
        functools.partial(pack_kernel, plan),
        out_shape=[
            jax.ShapeDtypeStruct((count, bs, bs), jnp.bfloat16)
            for count in (plan.cut, plan.packed - plan.cut)
        ],
        compiler_params=pltpu.CompilerParams(vmem_limit_bytes=VMEM_LIMIT),
        cost_estimate=NO_COST,
        name="pack",
    )(*line)


def chain_kernel(plan, value_ref, *refs):
    rows, cols = plan.rows, plan.cols
    first_ref, second_ref, out_ref, values, solved = refs
    row_id, col_id = lax.axis_index("row"), lax.axis_index("col")
    core = lax.rem(row_id, 2)
    for step in range(cols):
        owner = lax.bitwise_xor(col_id, step)
        for b in range(value_ref.shape[1]):
            values[b * cols + owner] = value_ref[step, b].astype(jnp.float32)

    steps, turned = [], []
    for c in range(cols):
        step = lax.bitwise_xor(col_id, c)
        steps.append(step)
        turned.append(
            sum(
                lax.rem(step // flip, 2) * other
                for flip, other in zip(plan.flips, reversed(plan.flips))
            )
        )

    def tile(j, k):
        r, c = j % rows, k % cols
        at = plan.lists[r % 2, c].index((r, plan.slots.index((j // rows, k // cols))))
        side = lax.bitwise_xor(core, r % 2)
        if at < plan.cut:
            return first_ref[side, steps[c], at]
        return second_ref[side, turned[c], at - plan.cut]

    sums = [values[k] for k in range(NB)]
    for j in reversed(range(NB)):
        block = sums[j].astype(jnp.bfloat16)
        solved[j] = block
        for k in reversed(range(j)):
            sums[k] = sums[k] - jnp.dot(block, tile(j, k), preferred_element_type=jnp.float32)
    for b in range(out_ref.shape[0]):
        out_ref[b] = solved[b * cols + col_id]


def chain(plan, values, first, second):
    _, per, count, bs = values.shape
    return pl.pallas_call(
        functools.partial(chain_kernel, plan),
        out_shape=jax.ShapeDtypeStruct((per, count, bs), jnp.bfloat16),
        scratch_shapes=[
            pltpu.VMEM((NB, count, bs), jnp.float32),
            pltpu.VMEM((NB, count, bs), jnp.bfloat16),
        ],
        compiler_params=pltpu.CompilerParams(vmem_limit_bytes=VMEM_LIMIT),
        cost_estimate=NO_COST,
        name="chain",
    )(values, first, second)


def after(array, *done):
    return lax.optimization_barrier((array, *done))[0]


def body(rhs, diag_inv, panel, offdiag, known, row_index):
    plan = Plan(lax.axis_size("row"), lax.axis_size("col"))
    core = lax.rem(lax.axis_index("row"), 2)

    known_all = direct(known, plan)
    folded = fold_panel(panel, diag_inv, plan.slots)
    line = [folded] + [across_z(folded, plan, m) for m in range(1, plan.zs)]
    sums = segment_sums(offdiag, row_index, known.shape[0] * plan.cols)
    keep, give = local_update(known_all, sums, rhs, diag_inv)
    first, second = pack(plan, [after(piece, sums) for piece in line])

    part = (keep + other_core(give, plan).astype(jnp.float32)).astype(jnp.bfloat16)
    parts = [part] + [across_z(part, plan, m) for m in range(1, plan.zs)]
    total = sum(p.astype(jnp.float32) for p in parts).astype(jnp.bfloat16)
    values = direct(total, plan)

    halves = []
    for half, flips in ((first, plan.flips), (second, plan.flips[::-1])):
        mine, theirs = [half[None]], []
        for step, flip in enumerate(flips):
            held = mine[0] if len(mine) == 1 else jnp.concatenate(mine)
            if step == len(flips) - 1:
                held = after(held, total)
                theirs.append(other_core(held, plan))
            mine = [held, across_col(held, plan, flip)]
        theirs.append(other_core(after(mine[1], values), plan))
        halves.append(jnp.stack([jnp.concatenate(mine), jnp.concatenate(theirs)]))

    mine = out_of_solvers(chain(plan, values, *halves), plan)
    theirs = other_core(mine, plan)
    return jnp.concatenate(
        [jnp.where(core == 0, mine, theirs), jnp.where(core == 0, theirs, mine)], axis=1
    )


def solution(mesh):
    placed = (
        P("col", None, None),
        P("col", None, None),
        P("row", "col", None, None),
        P("row", "col", None, None),
        P(("row", "col"), None, None),
        P("row"),
    )
    return jax.shard_map(
        body, mesh=mesh, in_specs=placed, out_specs=P("col", None, None), check_vma=False
    )
```

time: 760 us -> 65.1 us (0.09)
  blocking collectives: 659 us -> 0 us
  waiting for transfers between devices: 54.6 us -> 26.3 us
  starting transfers between devices: 0.01 us -> 24.9 us
  matrix products: 24.6 us -> 0 us
  between operations: 13.5 us -> 0.28 us
  Pallas kernels: 0 us -> 10.3 us
    psum x32 -> x0, blocking collectives: 648 us -> none  [the longest x16 415 us: step_reduced(): lax.psum(partial_value.astype(jnp.bfloat16), 'row').astype(jnp.float32)]
    psum x1 -> x0, waiting for transfers between devices: 54.5 us -> none  [body(): off_sum = lax.psum(off_part, 'row')]
    ppermute x0 -> x23, waiting for transfers between devices: none -> 26.3 us  [send(): return lax.ppermute(array, AXES, flat)]
    ppermute x0 -> x23, starting transfers between devices: none -> 24.9 us  [send(): return lax.ppermute(array, AXES, flat)]
    dot_general x33 -> x0, matrix products: 24.6 us -> none  [the longest x16 16.4 us: finish_block(): jnp.dot(total, inverse, precision=lax.Precision.HIGHEST, preferred_elemen...]
    pallas_call x0 -> x5, Pallas kernels: none -> 10.3 us  [the longest x1 5.36 us: segment_sums(): pl.pallas_call(functools.partial(segment_kernel, chunk), in_specs=[pl.Blo...]
    all_gather x1 -> x0, blocking collectives: 10.1 us -> none  [body(): known_row = lax.all_gather(known, 'col', axis=0, tiled=True)]
  transfers between devices with their start and end apart: 1 -> 23, of which waited for: 1 -> 12; matrix products, arithmetic and copies ran while one was open for 0% -> 1% of each run, Pallas kernels for 0% -> 13%
where the time goes in v3:
time: 65.1 us; the launch traced here: 64.9 us
  waiting for transfers between devices  26.3 us (40%)
  starting transfers between devices  24.9 us (38%)
  Pallas kernels  10.3 us (16%)
  other arithmetic  1.79 us (3%)
  local copies, waits for them, and re-layouts  1.27 us (2%)
    ppermute x23, waiting for transfers between devices, send(): return lax.ppermute(array, AXES, flat)  26.3 us
    ppermute x23, starting transfers between devices, send(): return lax.ppermute(array, AXES, flat)  24.9 us
    pallas_call x1, Pallas kernels, segment_sums(): pl.pallas_call(functools.partial(segment_kernel, chunk), in_specs=[pl.Blo...  5.36 us
    pallas_call x1, Pallas kernels, fold_panel(): pl.pallas_call(functools.partial(fold_kernel, slots), in_specs=[pl.BlockS...  1.98 us
    pallas_call x1, Pallas kernels, chain(): pl.pallas_call(functools.partial(chain_kernel, plan), out_shape=jax.Shape...  1.81 us
  transfers between devices with their start and end apart: 23, of which 12 were waited for; matrix products, arithmetic and copies ran while one was open for 1% of the time, Pallas kernels for 13%

profile of v3, /device:TPU:0, one launch (start us, length us, event | category | flops | bytes accessed | tf_op | source)
XLA Modules:
  0.0 64.9 jit_solution(2157626828034795022)
XLA Ops:
  0.0 2.9 %collective-permute-start = (bf16[2,64,128]{2,1,0:T(8,128)(2,1)}, bf16[2,64,128]{2,1,0:T(8,128)(2,1)S(1)}, u32[]{:S(2)}, u32[]{:S(2)}) collective-permute-start(bf16[2,64,128]{2,1,0:T(8,128)(2,1)} %param.10), channel_id=1, source_target_pairs={{0,1},{1,0},{2,3},{3,2},{4,5},{5,4},{6,7},{7,6},{8,9},{9,8},{10,11... | collective-permute-start | bytes 98312 | tf_op jit(solution)/shard_map/ppermute | solution.py:43
  2.9 2.0 %fold_panel.1.refs_0_ = bf16[6,128,128]{2,1,0:T(8,128)(2,1)} custom-call(bf16[2,4,128,128]{3,2,1,0:T(8,128)(2,1)} %panel_hbm.1, f32[4,128,128]{2,1,0:T(8,128)} %inverse_hbm.1), custom_call_target="tpu_custom_call" | custom-call | tf_op jit(solution)/shard_map/fold_panel/pallas_call | solution.py:117
  4.9 0.0 copy-start.4
  4.9 0.0 copy-start.1
  5.0 0.0 copy-start.3
  5.0 1.6 %collective-permute-start.10 = (bf16[6,128,128]{2,1,0:T(8,128)(2,1)}, bf16[6,128,128]{2,1,0:T(8,128)(2,1)S(1)}, u32[]{:S(2)}, u32[]{:S(2)}) collective-permute-start(bf16[6,128,128]{2,1,0:T(8,128)(2,1)} %fold_panel.1.refs_0_), channel_id=1, source_target_pairs={{0,8},{1,9},{2,10},{3,11},{4,12},{5,13},{6,14},{7,15},{8,0},{9,1},... | collective-permute-start | bytes 589832 | tf_op jit(solution)/shard_map/ppermute | solution.py:43
  6.6 2.6 %collective-permute-start.11 = (bf16[6,128,128]{2,1,0:T(8,128)(2,1)}, bf16[6,128,128]{2,1,0:T(8,128)(2,1)S(1)}, u32[]{:S(2)}, u32[]{:S(2)}) collective-permute-start(bf16[6,128,128]{2,1,0:T(8,128)(2,1)} %fold_panel.1.refs_0_), channel_id=1, source_target_pairs={{0,16},{1,17},{2,18},{3,19},{4,20},{5,21},{6,22},{7,23},{8,0},{9,1... | collective-permute-start | bytes 589832 | tf_op jit(solution)/shard_map/ppermute | solution.py:43
  9.2 1.6 %collective-permute-start.12 = (bf16[6,128,128]{2,1,0:T(8,128)(2,1)}, bf16[6,128,128]{2,1,0:T(8,128)(2,1)S(1)}, u32[]{:S(2)}, u32[]{:S(2)}) collective-permute-start(bf16[6,128,128]{2,1,0:T(8,128)(2,1)} %fold_panel.1.refs_0_), channel_id=1, source_target_pairs={{0,0},{1,1},{2,2},{3,3},{4,4},{5,5},{6,6},{7,7},{8,16},{9,17},{10,... | collective-permute-start | bytes 589832 | tf_op jit(solution)/shard_map/ppermute | solution.py:43
  10.8 1.5 %collective-permute-start.1 = (bf16[2,64,128]{2,1,0:T(8,128)(2,1)}, bf16[2,64,128]{2,1,0:T(8,128)(2,1)S(1)}, u32[]{:S(2)}, u32[]{:S(2)}) collective-permute-start(bf16[2,64,128]{2,1,0:T(8,128)(2,1)} %param.10), channel_id=1, source_target_pairs={{0,2},{1,3},{2,0},{3,1},{4,6},{5,7},{6,4},{7,5},{8,10},{9,11},{10,... | collective-permute-start | bytes 98312 | tf_op jit(solution)/shard_map/ppermute | solution.py:43
  12.3 0.0 collective-permute-done
  12.3 0.5 collective-permute-start.2
  12.8 5.4 %segment_sums.1.sums_ref = bf16[8,4,128,128]{3,2,1,0:T(8,128)(2,1)} custom-call(s32[64]{0:T(128)} %index_ref.1, bf16[64,4,128,128]{3,2,1,0:T(8,128)(2,1)} %tiles_hbm.1), custom_call_target="tpu_custom_call" | custom-call | flops 4194304 | bytes 8388608 | tf_op jit(solution)/shard_map/segment_sums/pallas_call | solution.py:156
  18.1 0.0 collective-permute-done.1
  18.2 0.0 collective-permute-done.2
  18.2 1.2 %copy-done = bf16[8,4,128,128]{3,2,1,0:T(8,128)(2,1)S(1)} copy-done((bf16[8,4,128,128]{3,2,1,0:T(8,128)(2,1)S(1)}, bf16[8,4,128,128]{3,2,1,0:T(8,128)(2,1)}, u32[]{:S(2)}) %copy-start) | copy-done | bytes 1048600
  19.5 0.7 %local_update.1 = (f32[4,32,128]{2,1,0:T(8,128)S(1)}, bf16[4,32,128]{2,1,0:T(8,128)(2,1)S(1)}) custom-call(bf16[4,2,64,128]{3,2,1,0:T(8,128)(2,1)S(1)} %pad_maximum_fusion.4.known_ref, bf16[8,4,128,128]{3,2,1,0:T(8,128)(2,1)S(1)} %copy-done, f32[4,64,128]{2,1,0:T(8,128)S(1)} %copy-done.3, f32[4,128,128]{2,1,0:T(8,128)S(1)} %copy-done.1), custom_call_target="tpu_custom_call" | custom-call | tf_op jit(solution)/shard_map/local_update/pallas_call | solution.py:202
  20.2 0.1 collective-permute-start.3
  20.3 0.0 collective-permute-done.10.refs_1_
  20.3 0.0 collective-permute-done.11.refs_2_
  20.3 0.0 collective-permute-done.12.refs_3_
  20.3 0.4 pack.1
  20.8 1.6 %collective-permute-start.17 = (bf16[1,10,128,128]{3,2,1,0:T(8,128)(2,1)S(1)}, bf16[1,10,128,128]{3,2,1,0:T(8,128)(2,1)S(1)}, u32[]{:S(2)}, u32[]{:S(2)}) collective-permute-start(bf16[1,10,128,128]{3,2,1,0:T(8,128)(2,1)S(1)} %bitcast.20), channel_id=1, source_target_pairs={{0,2},{1,3},{2,0},{3,1},{4,6},{5,7},{6,4},{7,5},{8,10},{9,11},{10,... | collective-permute-start | bytes 983048 | tf_op jit(solution)/shard_map/ppermute | solution.py:43
  22.4 0.0 collective-permute-done.3
  22.4 1.5 %collective-permute-start.4 = (bf16[4,32,128]{2,1,0:T(8,128)(2,1)S(1)}, bf16[4,32,128]{2,1,0:T(8,128)(2,1)S(1)}, u32[]{:S(2)}, u32[]{:S(2)}) collective-permute-start(bf16[4,32,128]{2,1,0:T(8,128)(2,1)S(1)} %add_convert_fusion.1), channel_id=1, source_target_pairs={{0,8},{1,9},{2,10},{3,11},{4,12},{5,13},{6,14},{7,15},{8,0},{9,1},... | collective-permute-start | bytes 98312 | tf_op jit(solution)/shard_map/ppermute | solution.py:43
  23.9 0.0 collective-permute-start.5
  23.9 0.7 %collective-permute-start.6 = (bf16[4,32,128]{2,1,0:T(8,128)(2,1)S(1)}, bf16[4,32,128]{2,1,0:T(8,128)(2,1)S(1)}, u32[]{:S(2)}, u32[]{:S(2)}) collective-permute-start(bf16[4,32,128]{2,1,0:T(8,128)(2,1)S(1)} %add_convert_fusion.1), channel_id=1, source_target_pairs={{0,0},{1,1},{2,2},{3,3},{4,4},{5,5},{6,6},{7,7},{8,16},{9,17},{10,... | collective-permute-start | bytes 98312 | tf_op jit(solution)/shard_map/ppermute | solution.py:43
  24.5 1.6 %collective-permute-start.13 = (bf16[1,10,128,128]{3,2,1,0:T(8,128)(2,1)S(1)}, bf16[1,10,128,128]{3,2,1,0:T(8,128)(2,1)S(1)}, u32[]{:S(2)}, u32[]{:S(2)}) collective-permute-start(bf16[1,10,128,128]{3,2,1,0:T(8,128)(2,1)S(1)} %bitcast.18), channel_id=1, source_target_pairs={{0,1},{1,0},{2,3},{3,2},{4,5},{5,4},{6,7},{7,6},{8,9},{9,8},{10,11... | collective-permute-start | bytes 983048 | tf_op jit(solution)/shard_map/ppermute | solution.py:43
  26.1 0.3 collective-permute-done.4
  26.4 1.4 %collective-permute-done.5 = bf16[4,32,128]{2,1,0:T(8,128)(2,1)S(1)} collective-permute-done((bf16[4,32,128]{2,1,0:T(8,128)(2,1)S(1)}, bf16[4,32,128]{2,1,0:T(8,128)(2,1)S(1)}, u32[]{:S(2)}, u32[]{:S(2)}) %collective-permute-start.5) | collective-permute-done | bytes 32800 | tf_op jit(solution)/shard_map/ppermute | solution.py:43
  27.8 0.0 collective-permute-done.6
  27.8 3.1 %collective-permute-done.17 = bf16[1,10,128,128]{3,2,1,0:T(8,128)(2,1)S(1)} collective-permute-done((bf16[1,10,128,128]{3,2,1,0:T(8,128)(2,1)S(1)}, bf16[1,10,128,128]{3,2,1,0:T(8,128)(2,1)S(1)}, u32[]{:S(2)}, u32[]{:S(2)}) %collective-permute-start.17) | collective-permute-done | bytes 327712 | tf_op jit(solution)/shard_map/ppermute | solution.py:43
  30.9 0.1 pad_maximum_fusion.3
  31.0 1.6 %collective-permute-start.18 = (bf16[2,10,128,128]{3,2,1,0:T(8,128)(2,1)S(1)}, bf16[2,10,128,128]{3,2,1,0:T(8,128)(2,1)S(1)}, u32[]{:S(2)}, u32[]{:S(2)}) collective-permute-start(bf16[2,10,128,128]{3,2,1,0:T(8,128)(2,1)S(1)} %pad_maximum_fusion.3), channel_id=1, source_target_pairs={{0,1},{1,0},{2,3},{3,2},{4,5},{5,4},{6,7},{7,6},{8,9},{9,8},{10,11... | collective-permute-start | bytes 1966088 | tf_op jit(solution)/shard_map/ppermute | solution.py:43
  32.6 2.3 %collective-permute-done.13 = bf16[1,10,128,128]{3,2,1,0:T(8,128)(2,1)S(1)} collective-permute-done((bf16[1,10,128,128]{3,2,1,0:T(8,128)(2,1)S(1)}, bf16[1,10,128,128]{3,2,1,0:T(8,128)(2,1)S(1)}, u32[]{:S(2)}, u32[]{:S(2)}) %collective-permute-start.13) | collective-permute-done | bytes 327712 | tf_op jit(solution)/shard_map/ppermute | solution.py:43
  34.8 0.1 pad_maximum_fusion.2
  34.9 0.1 collective-permute-start.14
  35.0 1.6 %collective-permute-start.7 = (bf16[4,32,128]{2,1,0:T(8,128)(2,1)S(1)}, bf16[4,32,128]{2,1,0:T(8,128)(2,1)S(1)}, u32[]{:S(2)}, u32[]{:S(2)}) collective-permute-start(bf16[4,32,128]{2,1,0:T(8,128)(2,1)S(1)} %add_convert_fusion), channel_id=1, source_target_pairs={{0,1},{1,0},{2,3},{3,2},{4,5},{5,4},{6,7},{7,6},{8,9},{9,8},{10,11... | collective-permute-start | bytes 98312 | tf_op jit(solution)/shard_map/ppermute | solution.py:43
  36.5 1.9 %collective-permute-start.8 = (bf16[4,32,128]{2,1,0:T(8,128)(2,1)S(1)}, bf16[4,32,128]{2,1,0:T(8,128)(2,1)S(1)}, u32[]{:S(2)}, u32[]{:S(2)}) collective-permute-start(bf16[4,32,128]{2,1,0:T(8,128)(2,1)S(1)} %add_convert_fusion), channel_id=1, source_target_pairs={{0,2},{1,3},{2,0},{3,1},{4,6},{5,7},{6,4},{7,5},{8,10},{9,11},{10,... | collective-permute-start | bytes 98312 | tf_op jit(solution)/shard_map/ppermute | solution.py:43
  38.5 0.0 collective-permute-start.9
  38.5 10.7 %collective-permute-done.7 = bf16[4,32,128]{2,1,0:T(8,128)(2,1)S(1)} collective-permute-done((bf16[4,32,128]{2,1,0:T(8,128)(2,1)S(1)}, bf16[4,32,128]{2,1,0:T(8,128)(2,1)S(1)}, u32[]{:S(2)}, u32[]{:S(2)}) %collective-permute-start.7) | collective-permute-done | bytes 32800 | tf_op jit(solution)/shard_map/ppermute | solution.py:43
  49.2 2.1 %collective-permute-done.8 = bf16[4,32,128]{2,1,0:T(8,128)(2,1)S(1)} collective-permute-done((bf16[4,32,128]{2,1,0:T(8,128)(2,1)S(1)}, bf16[4,32,128]{2,1,0:T(8,128)(2,1)S(1)}, u32[]{:S(2)}, u32[]{:S(2)}) %collective-permute-start.8) | collective-permute-done | bytes 32800 | tf_op jit(solution)/shard_map/ppermute | solution.py:43
  51.3 0.0 collective-permute-done.9
  51.4 0.1 collective-permute-start.19
  51.4 0.0 collective-permute-done.18
  51.5 0.5 collective-permute-start.20
  51.9 0.1 collective-permute-start.15
  52.0 0.0 collective-permute-done.14
  52.0 0.4 collective-permute-start.16
  52.5 0.1 maximum_bitcast_fusion.2
  52.6 0.1 maximum_bitcast_fusion
  52.7 0.8 %collective-permute-done.19 = bf16[2,10,128,128]{3,2,1,0:T(8,128)(2,1)S(1)} collective-permute-done((bf16[2,10,128,128]{3,2,1,0:T(8,128)(2,1)S(1)}, bf16[2,10,128,128]{3,2,1,0:T(8,128)(2,1)S(1)}, u32[]{:S(2)}, u32[]{:S(2)}) %collective-permute-start.19) | collective-permute-done | bytes 655392 | tf_op jit(solution)/shard_map/ppermute | solution.py:43
  53.5 0.9 %collective-permute-done.20 = bf16[2,10,128,128]{3,2,1,0:T(8,128)(2,1)S(1)} collective-permute-done((bf16[2,10,128,128]{3,2,1,0:T(8,128)(2,1)S(1)}, bf16[2,10,128,128]{3,2,1,0:T(8,128)(2,1)S(1)}, u32[]{:S(2)}, u32[]{:S(2)}) %collective-permute-start.20) | collective-permute-done | bytes 655392 | tf_op jit(solution)/shard_map/ppermute | solution.py:43
  54.5 0.1 maximum_bitcast_fusion.3
  54.6 0.2 pad_maximum_fusion.1.refs_1_
  54.8 0.6 collective-permute-done.15
  55.4 0.9 %collective-permute-done.16 = bf16[2,10,128,128]{3,2,1,0:T(8,128)(2,1)S(1)} collective-permute-done((bf16[2,10,128,128]{3,2,1,0:T(8,128)(2,1)S(1)}, bf16[2,10,128,128]{3,2,1,0:T(8,128)(2,1)S(1)}, u32[]{:S(2)}, u32[]{:S(2)}) %collective-permute-start.16) | collective-permute-done | bytes 655392 | tf_op jit(solution)/shard_map/ppermute | solution.py:43
  56.3 0.1 maximum_bitcast_fusion.1
  56.5 0.2 pad_maximum_fusion.refs_0_
  56.7 1.8 %chain.1 = bf16[4,32,128]{2,1,0:T(8,128)(2,1)S(1)} custom-call(bf16[4,4,32,128]{3,2,1,0:T(8,128)(2,1)S(1)} %pad_maximum_fusion.5.value_ref, bf16[2,4,10,128,128]{4,3,2,1,0:T(8,128)(2,1)S(1)} %pad_maximum_fusion.refs_0_, bf16[2,4,10,128,128]{4,3,2,1,0:T(8,128)(2,1)S(1)} %pad_maximum_fusion.1.refs_1_), custom_call_target="tpu_custom_call" | custom-call | tf_op jit(solution)/shard_map/chain/pallas_call | solution.py:289
  58.5 2.5 %collective-permute-start.21 = (bf16[4,32,128]{2,1,0:T(8,128)(2,1)S(1)}, bf16[4,32,128]{2,1,0:T(8,128)(2,1)S(1)}, u32[]{:S(2)}, u32[]{:S(2)}) collective-permute-start(bf16[4,32,128]{2,1,0:T(8,128)(2,1)S(1)} %chain.1), channel_id=1, source_target_pairs={{0,8},{1,9},{2,10},{3,11},{4,12},{5,13},{6,14},{7,15},{8,0},{9,1},... | collective-permute-start | bytes 98312 | tf_op jit(solution)/shard_map/ppermute | solution.py:43
  61.1 1.9 %collective-permute-done.21 = bf16[4,32,128]{2,1,0:T(8,128)(2,1)S(1)} collective-permute-done((bf16[4,32,128]{2,1,0:T(8,128)(2,1)S(1)}, bf16[4,32,128]{2,1,0:T(8,128)(2,1)S(1)}, u32[]{:S(2)}, u32[]{:S(2)}) %collective-permute-start.21) | collective-permute-done | bytes 32800 | tf_op jit(solution)/shard_map/ppermute | solution.py:43
  63.0 0.1 collective-permute-start.22
  63.0 1.2 %collective-permute-done.22 = bf16[4,32,128]{2,1,0:T(8,128)(2,1)S(1)} collective-permute-done((bf16[4,32,128]{2,1,0:T(8,128)(2,1)S(1)}, bf16[4,32,128]{2,1,0:T(8,128)(2,1)S(1)}, u32[]{:S(2)}, u32[]{:S(2)}) %collective-permute-start.22) | collective-permute-done | bytes 32800 | tf_op jit(solution)/shard_map/ppermute | solution.py:43
  64.3 0.6 pad_maximum_fusion.6
  (12 shorter events, 0.1 us)
Async XLA Ops:
  0.0 12.3 %collective-permute-start = (bf16[2,64,128]{2,1,0:T(8,128)(2,1)}, bf16[2,64,128]{2,1,0:T(8,128)(2,1)S(1)}, u32[]{:S(2)}, u32[]{:S(2)}) collective-permute-start(bf16[2,64,128]{2,1,0:T(8,128)(2,1)} %param.10), channel_id=1, source_target_pairs={{0,1},{1,0},{2,3},{3,2},{4,5},{5,4},{6,7},{7,6},{8,9},{9,8},{10,11... | collective-permute-start | bytes 98312 | tf_op jit(solution)/shard_map/ppermute | solution.py:43
  4.9 13.2 %copy-start.4 = (bf16[2,64,128]{2,1,0:T(8,128)(2,1)S(1)}, bf16[2,64,128]{2,1,0:T(8,128)(2,1)}, u32[]{:S(2)}) copy-start(bf16[2,64,128]{2,1,0:T(8,128)(2,1)} %param.10) | copy-start | bytes 98308
  4.9 13.3 %copy-start.1 = (f32[4,128,128]{2,1,0:T(8,128)S(1)}, f32[4,128,128]{2,1,0:T(8,128)}, u32[]{:S(2)}) copy-start(f32[4,128,128]{2,1,0:T(8,128)} %inverse_hbm.1) | copy-start | bytes 786436
  5.0 13.3 %copy-start.3 = (f32[4,64,128]{2,1,0:T(8,128)S(1)}, f32[4,64,128]{2,1,0:T(8,128)}, u32[]{:S(2)}) copy-start(f32[4,64,128]{2,1,0:T(8,128)} %rhs_ref.1) | copy-start | bytes 393220
  5.0 15.3 %collective-permute-start.10 = (bf16[6,128,128]{2,1,0:T(8,128)(2,1)}, bf16[6,128,128]{2,1,0:T(8,128)(2,1)S(1)}, u32[]{:S(2)}, u32[]{:S(2)}) collective-permute-start(bf16[6,128,128]{2,1,0:T(8,128)(2,1)} %fold_panel.1.refs_0_), channel_id=1, source_target_pairs={{0,8},{1,9},{2,10},{3,11},{4,12},{5,13},{6,14},{7,15},{8,0},{9,1},... | collective-permute-start | bytes 589832 | tf_op jit(solution)/shard_map/ppermute | solution.py:43
  6.6 13.7 %collective-permute-start.11 = (bf16[6,128,128]{2,1,0:T(8,128)(2,1)}, bf16[6,128,128]{2,1,0:T(8,128)(2,1)S(1)}, u32[]{:S(2)}, u32[]{:S(2)}) collective-permute-start(bf16[6,128,128]{2,1,0:T(8,128)(2,1)} %fold_panel.1.refs_0_), channel_id=1, source_target_pairs={{0,16},{1,17},{2,18},{3,19},{4,20},{5,21},{6,22},{7,23},{8,0},{9,1... | collective-permute-start | bytes 589832 | tf_op jit(solution)/shard_map/ppermute | solution.py:43
  9.2 11.1 %collective-permute-start.12 = (bf16[6,128,128]{2,1,0:T(8,128)(2,1)}, bf16[6,128,128]{2,1,0:T(8,128)(2,1)S(1)}, u32[]{:S(2)}, u32[]{:S(2)}) collective-permute-start(bf16[6,128,128]{2,1,0:T(8,128)(2,1)} %fold_panel.1.refs_0_), channel_id=1, source_target_pairs={{0,0},{1,1},{2,2},{3,3},{4,4},{5,5},{6,6},{7,7},{8,16},{9,17},{10,... | collective-permute-start | bytes 589832 | tf_op jit(solution)/shard_map/ppermute | solution.py:43
  10.8 7.4 %collective-permute-start.1 = (bf16[2,64,128]{2,1,0:T(8,128)(2,1)}, bf16[2,64,128]{2,1,0:T(8,128)(2,1)S(1)}, u32[]{:S(2)}, u32[]{:S(2)}) collective-permute-start(bf16[2,64,128]{2,1,0:T(8,128)(2,1)} %param.10), channel_id=1, source_target_pairs={{0,2},{1,3},{2,0},{3,1},{4,6},{5,7},{6,4},{7,5},{8,10},{9,11},{10,... | collective-permute-start | bytes 98312 | tf_op jit(solution)/shard_map/ppermute | solution.py:43
  12.3 5.9 %collective-permute-start.2 = (bf16[2,64,128]{2,1,0:T(8,128)(2,1)}, bf16[2,64,128]{2,1,0:T(8,128)(2,1)S(1)}, u32[]{:S(2)}, u32[]{:S(2)}) collective-permute-start(bf16[2,64,128]{2,1,0:T(8,128)(2,1)} %param.10), channel_id=1, source_target_pairs={{0,3},{1,2},{2,1},{3,0},{4,7},{5,6},{6,5},{7,4},{8,11},{9,10},{10,... | collective-permute-start | bytes 98312 | tf_op jit(solution)/shard_map/ppermute | solution.py:43
  18.1 2.2 %copy-start.2 = (bf16[6,128,128]{2,1,0:T(8,128)(2,1)S(1)}, bf16[6,128,128]{2,1,0:T(8,128)(2,1)}, u32[]{:S(2)}) copy-start(bf16[6,128,128]{2,1,0:T(8,128)(2,1)} %fold_panel.1.refs_0_) | copy-start | bytes 589828
  18.2 1.3 %copy-start = (bf16[8,4,128,128]{3,2,1,0:T(8,128)(2,1)S(1)}, bf16[8,4,128,128]{3,2,1,0:T(8,128)(2,1)}, u32[]{:S(2)}) copy-start(bf16[8,4,128,128]{3,2,1,0:T(8,128)(2,1)} %segment_sums.1.sums_ref) | copy-start | bytes 3145732
  20.2 2.2 %collective-permute-start.3 = (bf16[4,32,128]{2,1,0:T(8,128)(2,1)S(1)}, bf16[4,32,128]{2,1,0:T(8,128)(2,1)S(1)}, u32[]{:S(2)}, u32[]{:S(2)}) collective-permute-start(bf16[4,32,128]{2,1,0:T(8,128)(2,1)S(1)} %get-tuple-element.18), channel_id=1, source_target_pairs={{0,4},{1,5},{2,6},{3,7},{4,0},{5,1},{6,2},{7,3},{8,12},{9,13},{10,... | collective-permute-start | bytes 98312 | tf_op jit(solution)/shard_map/ppermute | solution.py:43
  20.8 10.2 %collective-permute-start.17 = (bf16[1,10,128,128]{3,2,1,0:T(8,128)(2,1)S(1)}, bf16[1,10,128,128]{3,2,1,0:T(8,128)(2,1)S(1)}, u32[]{:S(2)}, u32[]{:S(2)}) collective-permute-start(bf16[1,10,128,128]{3,2,1,0:T(8,128)(2,1)S(1)} %bitcast.20), channel_id=1, source_target_pairs={{0,2},{1,3},{2,0},{3,1},{4,6},{5,7},{6,4},{7,5},{8,10},{9,11},{10,... | collective-permute-start | bytes 983048 | tf_op jit(solution)/shard_map/ppermute | solution.py:43
  22.4 4.0 %collective-permute-start.4 = (bf16[4,32,128]{2,1,0:T(8,128)(2,1)S(1)}, bf16[4,32,128]{2,1,0:T(8,128)(2,1)S(1)}, u32[]{:S(2)}, u32[]{:S(2)}) collective-permute-start(bf16[4,32,128]{2,1,0:T(8,128)(2,1)S(1)} %add_convert_fusion.1), channel_id=1, source_target_pairs={{0,8},{1,9},{2,10},{3,11},{4,12},{5,13},{6,14},{7,15},{8,0},{9,1},... | collective-permute-start | bytes 98312 | tf_op jit(solution)/shard_map/ppermute | solution.py:43
  23.9 3.9 %collective-permute-start.5 = (bf16[4,32,128]{2,1,0:T(8,128)(2,1)S(1)}, bf16[4,32,128]{2,1,0:T(8,128)(2,1)S(1)}, u32[]{:S(2)}, u32[]{:S(2)}) collective-permute-start(bf16[4,32,128]{2,1,0:T(8,128)(2,1)S(1)} %add_convert_fusion.1), channel_id=1, source_target_pairs={{0,16},{1,17},{2,18},{3,19},{4,20},{5,21},{6,22},{7,23},{8,0},{9,1... | collective-permute-start | bytes 98312 | tf_op jit(solution)/shard_map/ppermute | solution.py:43
  23.9 3.9 %collective-permute-start.6 = (bf16[4,32,128]{2,1,0:T(8,128)(2,1)S(1)}, bf16[4,32,128]{2,1,0:T(8,128)(2,1)S(1)}, u32[]{:S(2)}, u32[]{:S(2)}) collective-permute-start(bf16[4,32,128]{2,1,0:T(8,128)(2,1)S(1)} %add_convert_fusion.1), channel_id=1, source_target_pairs={{0,0},{1,1},{2,2},{3,3},{4,4},{5,5},{6,6},{7,7},{8,16},{9,17},{10,... | collective-permute-start | bytes 98312 | tf_op jit(solution)/shard_map/ppermute | solution.py:43
  24.5 10.3 %collective-permute-start.13 = (bf16[1,10,128,128]{3,2,1,0:T(8,128)(2,1)S(1)}, bf16[1,10,128,128]{3,2,1,0:T(8,128)(2,1)S(1)}, u32[]{:S(2)}, u32[]{:S(2)}) collective-permute-start(bf16[1,10,128,128]{3,2,1,0:T(8,128)(2,1)S(1)} %bitcast.18), channel_id=1, source_target_pairs={{0,1},{1,0},{2,3},{3,2},{4,5},{5,4},{6,7},{7,6},{8,9},{9,8},{10,11... | collective-permute-start | bytes 983048 | tf_op jit(solution)/shard_map/ppermute | solution.py:43
  31.0 20.4 %collective-permute-start.18 = (bf16[2,10,128,128]{3,2,1,0:T(8,128)(2,1)S(1)}, bf16[2,10,128,128]{3,2,1,0:T(8,128)(2,1)S(1)}, u32[]{:S(2)}, u32[]{:S(2)}) collective-permute-start(bf16[2,10,128,128]{3,2,1,0:T(8,128)(2,1)S(1)} %pad_maximum_fusion.3), channel_id=1, source_target_pairs={{0,1},{1,0},{2,3},{3,2},{4,5},{5,4},{6,7},{7,6},{8,9},{9,8},{10,11... | collective-permute-start | bytes 1966088 | tf_op jit(solution)/shard_map/ppermute | solution.py:43
  34.9 17.2 %collective-permute-start.14 = (bf16[2,10,128,128]{3,2,1,0:T(8,128)(2,1)S(1)}, bf16[2,10,128,128]{3,2,1,0:T(8,128)(2,1)S(1)}, u32[]{:S(2)}, u32[]{:S(2)}) collective-permute-start(bf16[2,10,128,128]{3,2,1,0:T(8,128)(2,1)S(1)} %pad_maximum_fusion.2), channel_id=1, source_target_pairs={{0,2},{1,3},{2,0},{3,1},{4,6},{5,7},{6,4},{7,5},{8,10},{9,11},{10,... | collective-permute-start | bytes 1966088 | tf_op jit(solution)/shard_map/ppermute | solution.py:43
  35.0 14.3 %collective-permute-start.7 = (bf16[4,32,128]{2,1,0:T(8,128)(2,1)S(1)}, bf16[4,32,128]{2,1,0:T(8,128)(2,1)S(1)}, u32[]{:S(2)}, u32[]{:S(2)}) collective-permute-start(bf16[4,32,128]{2,1,0:T(8,128)(2,1)S(1)} %add_convert_fusion), channel_id=1, source_target_pairs={{0,1},{1,0},{2,3},{3,2},{4,5},{5,4},{6,7},{7,6},{8,9},{9,8},{10,11... | collective-permute-start | bytes 98312 | tf_op jit(solution)/shard_map/ppermute | solution.py:43
  36.5 14.8 %collective-permute-start.8 = (bf16[4,32,128]{2,1,0:T(8,128)(2,1)S(1)}, bf16[4,32,128]{2,1,0:T(8,128)(2,1)S(1)}, u32[]{:S(2)}, u32[]{:S(2)}) collective-permute-start(bf16[4,32,128]{2,1,0:T(8,128)(2,1)S(1)} %add_convert_fusion), channel_id=1, source_target_pairs={{0,2},{1,3},{2,0},{3,1},{4,6},{5,7},{6,4},{7,5},{8,10},{9,11},{10,... | collective-permute-start | bytes 98312 | tf_op jit(solution)/shard_map/ppermute | solution.py:43
  38.5 12.9 %collective-permute-start.9 = (bf16[4,32,128]{2,1,0:T(8,128)(2,1)S(1)}, bf16[4,32,128]{2,1,0:T(8,128)(2,1)S(1)}, u32[]{:S(2)}, u32[]{:S(2)}) collective-permute-start(bf16[4,32,128]{2,1,0:T(8,128)(2,1)S(1)} %add_convert_fusion), channel_id=1, source_target_pairs={{0,3},{1,2},{2,1},{3,0},{4,7},{5,6},{6,5},{7,4},{8,11},{9,10},{10,... | collective-permute-start | bytes 98312 | tf_op jit(solution)/shard_map/ppermute | solution.py:43
  51.4 2.2 %collective-permute-start.19 = (bf16[2,10,128,128]{3,2,1,0:T(8,128)(2,1)S(1)}, bf16[2,10,128,128]{3,2,1,0:T(8,128)(2,1)S(1)}, u32[]{:S(2)}, u32[]{:S(2)}) collective-permute-start(bf16[2,10,128,128]{3,2,1,0:T(8,128)(2,1)S(1)} %pad_maximum_fusion.3), channel_id=1, source_target_pairs={{0,4},{1,5},{2,6},{3,7},{4,0},{5,1},{6,2},{7,3},{8,12},{9,13},{10,... | collective-permute-start | bytes 1966088 | tf_op jit(solution)/shard_map/ppermute | solution.py:43
  51.5 3.0 %collective-permute-start.20 = (bf16[2,10,128,128]{3,2,1,0:T(8,128)(2,1)S(1)}, bf16[2,10,128,128]{3,2,1,0:T(8,128)(2,1)S(1)}, u32[]{:S(2)}, u32[]{:S(2)}) collective-permute-start(bf16[2,10,128,128]{3,2,1,0:T(8,128)(2,1)S(1)} %collective-permute-done.18), channel_id=1, source_target_pairs={{0,4},{1,5},{2,6},{3,7},{4,0},{5,1},{6,2},{7,3},{8,12},{9,13},{10,... | collective-permute-start | bytes 1966088 | tf_op jit(solution)/shard_map/ppermute | solution.py:43
  51.9 3.5 %collective-permute-start.15 = (bf16[2,10,128,128]{3,2,1,0:T(8,128)(2,1)S(1)}, bf16[2,10,128,128]{3,2,1,0:T(8,128)(2,1)S(1)}, u32[]{:S(2)}, u32[]{:S(2)}) collective-permute-start(bf16[2,10,128,128]{3,2,1,0:T(8,128)(2,1)S(1)} %pad_maximum_fusion.2), channel_id=1, source_target_pairs={{0,4},{1,5},{2,6},{3,7},{4,0},{5,1},{6,2},{7,3},{8,12},{9,13},{10,... | collective-permute-start | bytes 1966088 | tf_op jit(solution)/shard_map/ppermute | solution.py:43
  52.0 4.3 %collective-permute-start.16 = (bf16[2,10,128,128]{3,2,1,0:T(8,128)(2,1)S(1)}, bf16[2,10,128,128]{3,2,1,0:T(8,128)(2,1)S(1)}, u32[]{:S(2)}, u32[]{:S(2)}) collective-permute-start(bf16[2,10,128,128]{3,2,1,0:T(8,128)(2,1)S(1)} %collective-permute-done.14), channel_id=1, source_target_pairs={{0,4},{1,5},{2,6},{3,7},{4,0},{5,1},{6,2},{7,3},{8,12},{9,13},{10,... | collective-permute-start | bytes 1966088 | tf_op jit(solution)/shard_map/ppermute | solution.py:43
  58.5 4.4 %collective-permute-start.21 = (bf16[4,32,128]{2,1,0:T(8,128)(2,1)S(1)}, bf16[4,32,128]{2,1,0:T(8,128)(2,1)S(1)}, u32[]{:S(2)}, u32[]{:S(2)}) collective-permute-start(bf16[4,32,128]{2,1,0:T(8,128)(2,1)S(1)} %chain.1), channel_id=1, source_target_pairs={{0,8},{1,9},{2,10},{3,11},{4,12},{5,13},{6,14},{7,15},{8,0},{9,1},... | collective-permute-start | bytes 98312 | tf_op jit(solution)/shard_map/ppermute | solution.py:43
  63.0 1.3 %collective-permute-start.22 = (bf16[4,32,128]{2,1,0:T(8,128)(2,1)S(1)}, bf16[4,32,128]{2,1,0:T(8,128)(2,1)S(1)}, u32[]{:S(2)}, u32[]{:S(2)}) collective-permute-start(bf16[4,32,128]{2,1,0:T(8,128)(2,1)S(1)} %broadcast_select_fusion), channel_id=1, source_target_pairs={{0,4},{1,5},{2,6},{3,7},{4,0},{5,1},{6,2},{7,3},{8,12},{9,13},{10,... | collective-permute-start | bytes 98312 | tf_op jit(solution)/shard_map/ppermute | solution.py:43

commit v4 on v3

v4 whole, which is shorter than its diff:
```python
import functools

import jax
import jax.numpy as jnp
from jax import lax
from jax.experimental import pallas as pl
from jax.experimental.pallas import tpu as pltpu
from jax.sharding import PartitionSpec as P

NB = 16
AXES = ("row", "col")
VMEM_LIMIT = 16 * 1024 * 1024
HIGHEST = lax.Precision.HIGHEST


class Plan:
    def __init__(self, rows, cols):
        self.rows, self.cols, self.zs = rows, cols, rows // 2
        self.slots = [
            (a, b)
            for a in reversed(range(NB // rows))
            for b in reversed(range(NB // cols))
            if a * rows + rows - 1 > b * cols
        ]
        half = NB // 2
        self.high, self.low, self.cross = {}, {}, {}
        for core in range(2):
            for c in range(cols):
                below = [
                    (r, at, a * rows + r, b * cols + c)
                    for r in range(core, rows, 2)
                    for at, (a, b) in enumerate(self.slots)
                    if a * rows + r > b * cols + c
                ]
                self.high[core, c] = [t[:2] for t in below if t[3] >= half]
                self.low[core, c] = [t[:2] for t in below if t[2] < half]
                self.cross[core, c] = [t[:2] for t in below if t[2] >= half > t[3]]
        self.lists = (self.high, self.low, self.cross)
        self.counts = [max(map(len, lists.values())) for lists in self.lists]
        self.upper = slice(half // cols, NB // cols)
        self.lower = slice(0, -(-half // cols))
        self.solvers = sorted({max(self.zs // 2 - 1, 0), self.zs // 2})
        self.arrival = [self.zs - 1, *range(1, self.zs - 1), 0]


def send(array, plan, pairs):
    flat = [(r * plan.cols + c, to_r * plan.cols + to_c) for (r, c), (to_r, to_c) in pairs]
    return lax.ppermute(array, AXES, flat)


def across_z(array, plan, flip):
    to = {z ^ flip: z for z in plan.solvers}
    free = [z for z in range(plan.zs) if z not in to.values()]
    for z in range(plan.zs):
        if z not in to:
            to[z] = min(free, key=lambda other: abs(other - z))
            free.remove(to[z])
    pairs = [
        ((2 * z + core, c), (2 * to[z] + core, c))
        for z in range(plan.zs)
        for core in range(2)
        for c in range(plan.cols)
    ]
    return send(array, plan, pairs)


def out_of_solvers(array, plan):
    low, high = plan.solvers[0], plan.solvers[-1]
    z = lax.axis_index("row") // 2
    own, other = array, other_core(array, plan)
    for step in range(1, plan.zs // 2):
        to = {low: low - step, high: high + step, low - step: low, high + step: high}
        outer = jnp.logical_or(z == low - step, z == high + step)
        got = []
        for cross in range(2):
            pairs = [
                ((2 * a + core, c), (2 * to.get(a, a) + (core ^ cross), c))
                for a in range(plan.zs)
                for core in range(2)
                for c in range(plan.cols)
            ]
            got.append(send(array, plan, pairs))
        own, other = jnp.where(outer, got[0], own), jnp.where(outer, got[1], other)
    return own, other


def across_col(array, plan, flip):
    pairs = [((r, c), (r, c ^ flip)) for r in range(plan.rows) for c in range(plan.cols)]
    return send(array, plan, pairs)


def other_core(array, plan):
    pairs = [((r, c), (r ^ 1, c)) for r in range(plan.rows) for c in range(plan.cols)]
    return send(array, plan, pairs)


def spread(array, plan):
    return lax.all_to_all(jnp.broadcast_to(array, (plan.cols, *array.shape)), "col", 0, 0)


def direct(array, plan):
    return [array] + [across_col(array, plan, m) for m in range(1, plan.cols)]


NO_COST = pl.CostEstimate(flops=0, bytes_accessed=0, transcendentals=0)


def fold_kernel(slots, panel_hbm, inverse_hbm, known_hbm, out_ref, known_ref, panel_ref, inverse_ref, sems):
    copies = [
        pltpu.make_async_copy(inverse_hbm, inverse_ref, sems.at[0]),
        pltpu.make_async_copy(panel_hbm, panel_ref, sems.at[1]),
    ]
    copies += [
        pltpu.make_async_copy(known_hbm, known_ref.at[c], sems.at[2 + c])
        for c in range(known_ref.shape[0])
    ]
    for copy in copies:
        copy.start()
    for copy in copies:
        copy.wait()
    for at, (a, b) in enumerate(slots):
        inverse = inverse_ref[b]
        high = inverse.astype(jnp.bfloat16)
        low = (inverse - high.astype(jnp.float32)).astype(jnp.bfloat16)
        tile = panel_ref[a, b]
        out_ref[at] = (
            jnp.dot(tile, high, preferred_element_type=jnp.float32)
            + jnp.dot(tile, low, preferred_element_type=jnp.float32)
        ).astype(jnp.bfloat16)


def fold_panel(panel, inverse, known, slots, cols):
    bs = panel.shape[-1]
    return pl.pallas_call(
        functools.partial(fold_kernel, slots),
        in_specs=[pl.BlockSpec(memory_space=pltpu.HBM)] * 3,
        out_shape=(
            jax.ShapeDtypeStruct((len(slots), bs, bs), jnp.bfloat16),
            jax.ShapeDtypeStruct((cols, *known.shape), known.dtype),
        ),
        scratch_shapes=[
            pltpu.VMEM(panel.shape, panel.dtype),
            pltpu.VMEM(inverse.shape, inverse.dtype),
            pltpu.SemaphoreType.DMA((2 + cols,)),
        ],
        compiler_params=pltpu.CompilerParams(vmem_limit_bytes=62 * 1024 * 1024),
        cost_estimate=NO_COST,
        name="fold_panel",
    )(panel, inverse, known)


def segment_kernel(chunk, index_ref, tiles_hbm, out_ref, tiles, sums, sems):
    copies = [
        pltpu.make_async_copy(
            tiles_hbm.at[pl.ds(i * chunk, chunk)], tiles.at[pl.ds(i * chunk, chunk)], sems.at[i]
        )
        for i in range(tiles.shape[0] // chunk)
    ]
    for copy in copies:
        copy.start()
    sums[...] = jnp.zeros_like(sums)
    for i, copy in enumerate(copies):
        copy.wait()

        def add(p, carry):
            sums[index_ref[p]] += tiles[p].astype(jnp.float32)
            return carry

        lax.fori_loop(i * chunk, (i + 1) * chunk, add, 0)
    out_ref[...] = sums[...].astype(jnp.bfloat16)


def segment_sums(offdiag, row_index, segments):
    tiles, blocks, bs, _ = offdiag.shape
    chunk = 4
    return pl.pallas_call(
        functools.partial(segment_kernel, chunk),
        in_specs=[pl.BlockSpec(memory_space=pltpu.SMEM), pl.BlockSpec(memory_space=pltpu.HBM)],
        out_shape=jax.ShapeDtypeStruct((segments, blocks, bs, bs), jnp.bfloat16),
        scratch_shapes=[
            pltpu.VMEM(offdiag.shape, offdiag.dtype),
            pltpu.VMEM((segments, blocks, bs, bs), jnp.float32),
            pltpu.SemaphoreType.DMA((tiles // chunk,)),
        ],
        compiler_params=pltpu.CompilerParams(vmem_limit_bytes=52 * 1024 * 1024),
        cost_estimate=pl.CostEstimate(
            flops=offdiag.size, bytes_accessed=2 * offdiag.size, transcendentals=0
        ),
        name="segment_sums",
    )(row_index, offdiag)


def update_kernel(known_ref, sums_ref, rhs_ref, inverse_ref, keep_ref, give_ref, whole):
    blocks, count, bs = rhs_ref.shape
    cols, per = known_ref.shape[:2]
    row_id = lax.axis_index("row")
    off = [jnp.zeros((count, bs), jnp.float32)] * blocks
    for c in range(cols):
        for i in range(per):
            for b in range(blocks):
                off[b] += jnp.dot(
                    known_ref[c, i], sums_ref[c * per + i, b], preferred_element_type=jnp.float32
                )
    adds = (row_id == 0).astype(jnp.float32)
    for b in range(blocks):
        total = rhs_ref[b] * adds - off[b]
        whole[b] = jnp.dot(
            total, inverse_ref[b], precision=HIGHEST, preferred_element_type=jnp.float32
        )
    half = count // 2
    core = lax.rem(row_id, 2)
    keep = pl.ds(pl.multiple_of(core * half, half), half)
    give = pl.ds(pl.multiple_of((1 - core) * half, half), half)
    keep_ref[...] = whole[:, keep, :]
    give_ref[...] = whole[:, give, :].astype(jnp.bfloat16)


def local_update(known, sums, rhs, inverse):
    blocks, count, bs = rhs.shape
    half = (blocks, count // 2, bs)
    return pl.pallas_call(
        update_kernel,
        out_shape=(
            jax.ShapeDtypeStruct(half, jnp.float32),
            jax.ShapeDtypeStruct(half, jnp.bfloat16),
        ),
        scratch_shapes=[pltpu.VMEM(rhs.shape, jnp.float32)],
        compiler_params=pltpu.CompilerParams(vmem_limit_bytes=VMEM_LIMIT),
        cost_estimate=NO_COST,
        name="local_update",
    )(known, sums, rhs, inverse)


def pack_kernel(plan, *refs):
    line_refs = [refs[plan.arrival.index(step)] for step in range(plan.zs)]
    row_id, col_id = lax.axis_index("row"), lax.axis_index("col")
    core, z = lax.rem(row_id, 2), row_id // 2
    within_ref, cross_ref = refs[plan.zs :]
    for which, (lists, count) in enumerate(zip(plan.lists, plan.counts)):
        out_ref = cross_ref if which == 2 else within_ref
        first = plan.counts[0] if which == 1 else 0
        for i in range(count):
            back, at = jnp.int32(0), jnp.int32(0)
            for (side, c), found in lists.items():
                if i < len(found):
                    mine = jnp.logical_and(col_id == c, core == side)
                    back = jnp.where(mine, lax.bitwise_xor(z, found[i][0] // 2), back)
                    at = jnp.where(mine, found[i][1], at)
            for step, line_ref in enumerate(line_refs):

                @pl.when(back == step)
                def _():
                    out_ref[first + i] = line_ref[at]


def pack(plan, line):
    bs = line[0].shape[-1]
    return pl.pallas_call(
        functools.partial(pack_kernel, plan),
        out_shape=[
            jax.ShapeDtypeStruct((count, bs, bs), jnp.bfloat16)
            for count in (sum(plan.counts[:2]), plan.counts[2])
        ],
        compiler_params=pltpu.CompilerParams(vmem_limit_bytes=VMEM_LIMIT),
        cost_estimate=NO_COST,
        name="pack",
    )(*[line[step] for step in plan.arrival])


def solve(plan, value_ref, tiles_ref, values, solved, first):
    rows, cols, half = plan.rows, plan.cols, NB // 2
    core, col_id = lax.rem(lax.axis_index("row"), 2), lax.axis_index("col")
    for step in range(cols):
        owner = lax.bitwise_xor(col_id, step)
        for b in range(value_ref.shape[1]):
            values[b * cols + owner] = value_ref[step, b].astype(jnp.float32)

    def tile(j, k):
        r, c = j % rows, k % cols
        lists = plan.high if first else plan.low
        at = lists[r % 2, c].index((r, plan.slots.index((j // rows, k // cols))))
        return tiles_ref[lax.bitwise_xor(core, r % 2), c, at]

    skip = first // cols * cols
    sums = [values[first - skip + i] for i in range(half)]
    for i in reversed(range(half)):
        block = sums[i].astype(jnp.bfloat16)
        solved[first + i] = block
        for m in reversed(range(i)):
            sums[m] = sums[m] - jnp.dot(
                block, tile(first + i, first + m), preferred_element_type=jnp.float32
            )


def upper_kernel(plan, value_ref, own_ref, tiles_ref, cross_ref, out_ref, lower_ref, values, solved):
    rows, half = plan.rows, NB // 2
    core = lax.rem(lax.axis_index("row"), 2)
    solve(plan, value_ref, tiles_ref, values, solved, half)
    out_ref[...] = solved[pl.ds(half, half)]
    for b in range(own_ref.shape[0]):
        total = own_ref[b]
        for j in range(half, NB):
            r = j % rows
            at = plan.cross[r % 2, 0].index((r, plan.slots.index((j // rows, b))))
            tile = cross_ref[lax.bitwise_xor(core, r % 2), at]
            total = total - jnp.dot(solved[j], tile, preferred_element_type=jnp.float32)
        lower_ref[b] = total.astype(jnp.bfloat16)


def lower_kernel(plan, value_ref, upper_ref, tiles_ref, out_ref, values, solved):
    half, col_id = NB // 2, lax.axis_index("col")
    solved[pl.ds(half, half)] = upper_ref[...]
    solve(plan, value_ref, tiles_ref, values, solved, 0)
    for b in range(out_ref.shape[0]):
        out_ref[b] = solved[b * plan.cols + col_id]


def call_half(kernel, plan, name, out_shape, values, *args):
    _, blocks, count, bs = values.shape
    return pl.pallas_call(
        functools.partial(kernel, plan),
        out_shape=[jax.ShapeDtypeStruct((n, count, bs), jnp.bfloat16) for n in out_shape],
        scratch_shapes=[
            pltpu.VMEM((blocks * plan.cols, count, bs), jnp.float32),
            pltpu.VMEM((NB, count, bs), jnp.bfloat16),
        ],
        compiler_params=pltpu.CompilerParams(vmem_limit_bytes=VMEM_LIMIT),
        cost_estimate=NO_COST,
        name=name,
    )(values, *args)


def after(array, *done):
    return lax.optimization_barrier((array, *done))[0]


def body(rhs, diag_inv, panel, offdiag, known, row_index):
    plan = Plan(lax.axis_size("row"), lax.axis_size("col"))
    core = lax.rem(lax.axis_index("row"), 2)

    folded, known = fold_panel(panel, diag_inv, known, plan.slots, plan.cols)
    line = [folded] + [across_z(folded, plan, m) for m in range(1, plan.zs)]
    known_all = lax.all_to_all(known, "col", 0, 0)
    sums = segment_sums(offdiag, row_index, known.shape[0] * known.shape[1])
    within, cross = pack(plan, [after(piece, sums, known_all) for piece in line])

    got = spread(within, plan)

    keep, give = local_update(known_all, after(sums, cross), rhs, diag_inv)
    total = keep + other_core(give, plan).astype(jnp.float32)
    sent = total.astype(jnp.bfloat16)
    for m in reversed(range(1, plan.zs)):
        total = total + across_z(sent, plan, m).astype(jnp.float32)
    cross = jnp.stack([cross, other_core(cross, plan)])
    upper = after(total[plan.upper].astype(jnp.bfloat16), cross)
    values = jnp.stack(direct(upper, plan))

    got = after(got, values)
    high, low = got[:, : plan.counts[0]], got[:, plan.counts[0] :]
    high = jnp.stack([high, other_core(high, plan)])
    sizes = (NB // 2, plan.lower.stop)
    solved, lower = call_half(
        upper_kernel, plan, "upper_half", sizes, values, total[plan.lower], high, cross
    )
    values = jnp.stack(direct(lower, plan))
    low = after(low, solved)
    low = jnp.stack([low, other_core(low, plan)])
    (mine,) = call_half(
        lower_kernel, plan, "lower_half", (NB // plan.cols,), values, solved, low
    )
    mine, theirs = out_of_solvers(mine, plan)
    return jnp.concatenate(
        [jnp.where(core == 0, mine, theirs), jnp.where(core == 0, theirs, mine)], axis=1
    )


def solution(mesh):
    placed = (
        P("col", None, None),
        P("col", None, None),
        P("row", "col", None, None),
        P("row", "col", None, None),
        P(("row", "col"), None, None),
        P("row"),
    )
    return jax.shard_map(
        body, mesh=mesh, in_specs=placed, out_specs=P("col", None, None), check_vma=False
    )
```

time: 65.1 us -> 61.1 us (0.939)
  waiting for transfers between devices: 26.3 us -> 19.2 us
  starting transfers between devices: 24.9 us -> 28.2 us
  local copies, waits for them, and re-layouts: 1.27 us -> 2.7 us
  Pallas kernels: 10.3 us -> 9.38 us
  other arithmetic: 1.79 us -> 1.04 us
    all_to_all x0 -> x2, starting transfers between devices: none -> 7.98 us  [the longest x1 4.26 us: spread(): lax.all_to_all(jnp.broadcast_to(array, (plan.cols, *array.shape)), 'col',...]
    ppermute x23 -> x19, waiting for transfers between devices: 26.3 us -> 19.1 us  [send(): return lax.ppermute(array, AXES, flat)]
    ppermute x23 -> x19, starting transfers between devices: 24.9 us -> 20.3 us  [send(): return lax.ppermute(array, AXES, flat)]
    broadcast_in_dim x0 -> x1, local copies, waits for them, and re-layouts: none -> 1.56 us  [spread(): jnp.broadcast_to(array, (plan.cols, *array.shape))]
    pallas_call x1, Pallas kernels: 5.36 us -> 4.25 us  [segment_sums(): pl.pallas_call(functools.partial(segment_kernel, chunk), in_specs=[pl.Blo...]
    pallas_call x1 -> x2, Pallas kernels: 1.81 us -> 1.95 us  [call_half(): pl.pallas_call(functools.partial(kernel, plan), out_shape=[jax.ShapeDtype...]
  transfers between devices with their start and end apart: 23 -> 21, of which waited for: 12 -> 10; matrix products, arithmetic and copies ran while one was open for 1% -> 0% of each run, Pallas kernels for 13% -> 8%
where the time goes in v4:
time: 61.1 us; the launch traced here: 60.8 us
  starting transfers between devices  28.2 us (46%)
  waiting for transfers between devices  19.2 us (31%)
  Pallas kernels  9.38 us (15%)
  local copies, waits for them, and re-layouts  2.7 us (4%)
  other arithmetic  1.04 us (2%)
    ppermute x19, starting transfers between devices, send(): return lax.ppermute(array, AXES, flat)  20.3 us
    ppermute x19, waiting for transfers between devices, send(): return lax.ppermute(array, AXES, flat)  19.1 us
    all_to_all x1, starting transfers between devices, spread(): lax.all_to_all(jnp.broadcast_to(array, (plan.cols, *array.shape)), 'col',...  4.26 us
    pallas_call x1, Pallas kernels, segment_sums(): pl.pallas_call(functools.partial(segment_kernel, chunk), in_specs=[pl.Blo...  4.25 us
    all_to_all x1, starting transfers between devices, body(): known_all = lax.all_to_all(known, 'col', 0, 0)  3.72 us
    pallas_call x1, Pallas kernels, fold_panel(): pl.pallas_call(functools.partial(fold_kernel, slots), in_specs=[pl.BlockS...  2.03 us
    pallas_call x2, Pallas kernels, call_half(): pl.pallas_call(functools.partial(kernel, plan), out_shape=[jax.ShapeDtype...  1.95 us
    broadcast_in_dim x1, local copies, waits for them, and re-layouts, spread(): jnp.broadcast_to(array, (plan.cols, *array.shape))  1.56 us
  transfers between devices with their start and end apart: 21, of which 10 were waited for; matrix products, arithmetic and copies ran while one was open for 0% of the time, Pallas kernels for 8%

profile of v4, /device:TPU:0, one launch (start us, length us, event | category | flops | bytes accessed | tf_op | source)
XLA Modules:
  0.0 60.8 jit_solution(14289717425261308749)
XLA Ops:
  0.0 2.0 %fold_panel.1 = (bf16[6,128,128]{2,1,0:T(8,128)(2,1)}, bf16[4,2,64,128]{3,2,1,0:T(8,128)(2,1)}) custom-call(bf16[2,4,128,128]{3,2,1,0:T(8,128)(2,1)} %panel_hbm.1, f32[4,128,128]{2,1,0:T(8,128)} %inverse_ref.1, bf16[2,64,128]{2,1,0:T(8,128)(2,1)} %known_hbm.1), custom_call_target="tpu_custom_call" | custom-call | tf_op jit(solution)/shard_map/fold_panel/pallas_call | solution.py:134
  2.0 4.1 %collective-permute-start.2 = (bf16[6,128,128]{2,1,0:T(8,128)(2,1)}, bf16[6,128,128]{2,1,0:T(8,128)(2,1)S(1)}, u32[]{:S(2)}, u32[]{:S(2)}) collective-permute-start(bf16[6,128,128]{2,1,0:T(8,128)(2,1)} %get-tuple-element.26.refs_3_), channel_id=1, source_target_pairs={{0,16},{1,17},{2,18},{3,19},{4,20},{5,21},{6,22},{7,23},{8,0},{9,1... | collective-permute-start | bytes 589832 | tf_op jit(solution)/shard_map/ppermute | solution.py:48
  6.1 0.0 collective-permute-start.1
  6.1 1.6 %collective-permute-start = (bf16[6,128,128]{2,1,0:T(8,128)(2,1)}, bf16[6,128,128]{2,1,0:T(8,128)(2,1)S(1)}, u32[]{:S(2)}, u32[]{:S(2)}) collective-permute-start(bf16[6,128,128]{2,1,0:T(8,128)(2,1)} %get-tuple-element.26.refs_3_), channel_id=1, source_target_pairs={{0,0},{1,1},{2,2},{3,3},{4,4},{5,5},{6,6},{7,7},{8,16},{9,17},{10,... | collective-permute-start | bytes 589832 | tf_op jit(solution)/shard_map/ppermute | solution.py:48
  7.7 3.7 %all-to-all-start = ((bf16[4,2,64,128]{3,2,1,0:T(8,128)(2,1)}), bf16[4,2,64,128]{3,2,1,0:T(8,128)(2,1)S(1)}, u32[]{:S(2)}, u32[]{:S(2)}) async-start(bf16[4,2,64,128]{3,2,1,0:T(8,128)(2,1)} %get-tuple-element.21), calls=%async_computation | async-start | bytes 262144 | tf_op jit(solution)/shard_map/all_to_all | solution.py:343
  11.4 0.0 copy-start.3
  11.4 0.7 %copy-done.3 = s32[64]{0:T(128)S(1)} copy-done((s32[64]{0:T(128)S(1)}, s32[64]{0:T(128)}, u32[]{:S(2)}) %copy-start.3) | copy-done | bytes 280
  12.1 0.0 copy-start.1
  12.1 4.3 %segment_sums.1.sums_ref = bf16[8,4,128,128]{3,2,1,0:T(8,128)(2,1)S(1)} custom-call(s32[64]{0:T(128)S(1)} %copy-done.3, bf16[64,4,128,128]{3,2,1,0:T(8,128)(2,1)} %tiles_hbm.1), custom_call_target="tpu_custom_call" | custom-call | flops 4194304 | bytes 8388608 | tf_op jit(solution)/shard_map/segment_sums/pallas_call | solution.py:176
  16.3 0.1 all-to-all-done.known_ref
  16.4 0.0 collective-permute-done.2.refs_2_
  16.4 0.0 collective-permute-done.1.refs_1_
  16.4 0.0 collective-permute-done.refs_0_
  16.5 0.0 copy-done.1
  16.5 0.4 pack.1
  16.9 1.6 %broadcast_in_dim.3 = bf16[4,12,128,128]{3,2,1,0:T(8,128)(2,1)} broadcast(bf16[12,128,128]{2,1,0:T(8,128)(2,1)S(1)} %get-tuple-element.32), dimensions={1,2,3} | broadcast | bytes 1966080 | tf_op jit(solution)/shard_map/broadcast_in_dim | solution.py:98
  18.5 0.0 copy-start
  18.5 0.0 copy-start.2
  18.5 4.3 %all-to-all-start.1 = ((bf16[4,12,128,128]{3,2,1,0:T(8,128)(2,1)}), bf16[4,12,128,128]{3,2,1,0:T(8,128)(2,1)S(1)}, u32[]{:S(2)}, u32[]{:S(2)}) async-start(bf16[4,12,128,128]{3,2,1,0:T(8,128)(2,1)} %broadcast_in_dim.3), calls=%async_computation.1 | async-start | bytes 3145728 | tf_op jit(solution)/shard_map/all_to_all | solution.py:98
  22.7 0.0 copy-done
  22.7 0.0 copy-done.2
  22.7 0.7 %local_update.1 = (f32[4,32,128]{2,1,0:T(8,128)S(1)}, bf16[4,32,128]{2,1,0:T(8,128)(2,1)S(1)}) custom-call(bf16[4,2,64,128]{3,2,1,0:T(8,128)(2,1)S(1)} %all-to-all-done.known_ref, bf16[8,4,128,128]{3,2,1,0:T(8,128)(2,1)S(1)} %segment_sums.1.sums_ref, f32[4,64,128]{2,1,0:T(8,128)S(1)} %copy-done.2, f32[4,128,128]{2,1,0:T(8,128)S(1)} %copy-done), custom_call_target="tpu_custom_call" | custom-call | tf_op jit(solution)/shard_map/local_update/pallas_call | solution.py:221
  23.5 0.1 collective-permute-start.3
  23.5 1.2 %collective-permute-done.3 = bf16[4,32,128]{2,1,0:T(8,128)(2,1)S(1)} collective-permute-done((bf16[4,32,128]{2,1,0:T(8,128)(2,1)S(1)}, bf16[4,32,128]{2,1,0:T(8,128)(2,1)S(1)}, u32[]{:S(2)}, u32[]{:S(2)}) %collective-permute-start.3) | collective-permute-done | bytes 32800 | tf_op jit(solution)/shard_map/ppermute | solution.py:48
  24.7 2.9 %collective-permute-start.6 = (bf16[4,32,128]{2,1,0:T(8,128)(2,1)S(1)}, bf16[4,32,128]{2,1,0:T(8,128)(2,1)S(1)}, u32[]{:S(2)}, u32[]{:S(2)}) collective-permute-start(bf16[4,32,128]{2,1,0:T(8,128)(2,1)S(1)} %fusion), channel_id=1, source_target_pairs={{0,8},{1,9},{2,10},{3,11},{4,12},{5,13},{6,14},{7,15},{8,0},{9,1},... | collective-permute-start | bytes 98312 | tf_op jit(solution)/shard_map/ppermute | solution.py:48
  27.6 1.1 %collective-permute-start.5 = (bf16[4,32,128]{2,1,0:T(8,128)(2,1)S(1)}, bf16[4,32,128]{2,1,0:T(8,128)(2,1)S(1)}, u32[]{:S(2)}, u32[]{:S(2)}) collective-permute-start(bf16[4,32,128]{2,1,0:T(8,128)(2,1)S(1)} %fusion), channel_id=1, source_target_pairs={{0,16},{1,17},{2,18},{3,19},{4,20},{5,21},{6,22},{7,23},{8,0},{9,1... | collective-permute-start | bytes 98312 | tf_op jit(solution)/shard_map/ppermute | solution.py:48
  28.7 0.7 %collective-permute-start.4 = (bf16[4,32,128]{2,1,0:T(8,128)(2,1)S(1)}, bf16[4,32,128]{2,1,0:T(8,128)(2,1)S(1)}, u32[]{:S(2)}, u32[]{:S(2)}) collective-permute-start(bf16[4,32,128]{2,1,0:T(8,128)(2,1)S(1)} %fusion), channel_id=1, source_target_pairs={{0,0},{1,1},{2,2},{3,3},{4,4},{5,5},{6,6},{7,7},{8,16},{9,17},{10,... | collective-permute-start | bytes 98312 | tf_op jit(solution)/shard_map/ppermute | solution.py:48
  29.4 0.1 collective-permute-start.7
  29.4 0.1 collective-permute-done.6
  29.5 2.0 %collective-permute-done.5 = bf16[4,32,128]{2,1,0:T(8,128)(2,1)S(1)} collective-permute-done((bf16[4,32,128]{2,1,0:T(8,128)(2,1)S(1)}, bf16[4,32,128]{2,1,0:T(8,128)(2,1)S(1)}, u32[]{:S(2)}, u32[]{:S(2)}) %collective-permute-start.5) | collective-permute-done | bytes 32800 | tf_op jit(solution)/shard_map/ppermute | solution.py:48
  31.5 0.0 collective-permute-done.4
  31.6 0.0 collective-permute-done.7
  31.6 0.1 pad_maximum_fusion.2.cross_ref
  31.7 3.0 %collective-permute-start.10 = (bf16[2,32,128]{2,1,0:T(8,128)(2,1)S(1)}, bf16[2,32,128]{2,1,0:T(8,128)(2,1)S(1)}, u32[]{:S(2)}, u32[]{:S(2)}) collective-permute-start(bf16[2,32,128]{2,1,0:T(8,128)(2,1)S(1)} %slice.21), channel_id=1, source_target_pairs={{0,3},{1,2},{2,1},{3,0},{4,7},{5,6},{6,5},{7,4},{8,11},{9,10},{10,... | collective-permute-start | bytes 49160 | tf_op jit(solution)/shard_map/ppermute | solution.py:48
  34.6 0.6 collective-permute-start.9
  35.2 0.1 collective-permute-start.8
  35.3 7.3 %collective-permute-done.10 = bf16[2,32,128]{2,1,0:T(8,128)(2,1)S(1)} collective-permute-done((bf16[2,32,128]{2,1,0:T(8,128)(2,1)S(1)}, bf16[2,32,128]{2,1,0:T(8,128)(2,1)S(1)}, u32[]{:S(2)}, u32[]{:S(2)}) %collective-permute-start.10) | collective-permute-done | bytes 16416 | tf_op jit(solution)/shard_map/ppermute | solution.py:48
  42.6 0.0 collective-permute-done.9
  42.6 0.0 collective-permute-done.8
  42.6 0.0 all-to-all-done.1
  42.6 0.5 fusion.1
  43.1 0.1 collective-permute-start.11
  43.2 2.3 %collective-permute-done.11 = bf16[4,6,128,128]{3,2,1,0:T(8,128)(2,1)S(1)} collective-permute-done((bf16[4,6,128,128]{3,2,1,0:T(8,128)(2,1)S(1)}, bf16[4,6,128,128]{3,2,1,0:T(8,128)(2,1)S(1)}, u32[]{:S(2)}, u32[]{:S(2)}) %collective-permute-start.11) | collective-permute-done | bytes 786464 | tf_op jit(solution)/shard_map/ppermute | solution.py:48
  45.4 0.1 pad_maximum_fusion.tiles_ref
  45.6 1.1 %upper_half.1 = (bf16[8,32,128]{2,1,0:T(8,128)(2,1)S(1)}, bf16[2,32,128]{2,1,0:T(8,128)(2,1)S(1)}) custom-call(bf16[4,2,32,128]{3,2,1,0:T(8,128)(2,1)S(1)} %pad_maximum_fusion.3.value_ref, f32[2,32,128]{2,1,0:T(8,128)S(1)} %slice.18.own_ref, bf16[2,4,6,128,128]{4,3,2,1,0:T(8,128)(2,1)S(1)} %pad_maximum_fusion.tiles_ref, ...), custom_call_target="tpu_custom_call" | custom-call | tf_op jit(solution)/shard_map/upper_half/pallas_call | solution.py:320
  46.7 0.2 collective-permute-start.15
  46.9 0.7 %collective-permute-start.14 = (bf16[2,32,128]{2,1,0:T(8,128)(2,1)S(1)}, bf16[2,32,128]{2,1,0:T(8,128)(2,1)S(1)}, u32[]{:S(2)}, u32[]{:S(2)}) collective-permute-start(bf16[2,32,128]{2,1,0:T(8,128)(2,1)S(1)} %get-tuple-element.34), channel_id=1, source_target_pairs={{0,3},{1,2},{2,1},{3,0},{4,7},{5,6},{6,5},{7,4},{8,11},{9,10},{10,... | collective-permute-start | bytes 49160 | tf_op jit(solution)/shard_map/ppermute | solution.py:48
  47.6 1.4 %collective-permute-start.13 = (bf16[2,32,128]{2,1,0:T(8,128)(2,1)S(1)}, bf16[2,32,128]{2,1,0:T(8,128)(2,1)S(1)}, u32[]{:S(2)}, u32[]{:S(2)}) collective-permute-start(bf16[2,32,128]{2,1,0:T(8,128)(2,1)S(1)} %get-tuple-element.34), channel_id=1, source_target_pairs={{0,2},{1,3},{2,0},{3,1},{4,6},{5,7},{6,4},{7,5},{8,10},{9,11},{10,... | collective-permute-start | bytes 49160 | tf_op jit(solution)/shard_map/ppermute | solution.py:48
  49.0 1.3 %collective-permute-start.12 = (bf16[2,32,128]{2,1,0:T(8,128)(2,1)S(1)}, bf16[2,32,128]{2,1,0:T(8,128)(2,1)S(1)}, u32[]{:S(2)}, u32[]{:S(2)}) collective-permute-start(bf16[2,32,128]{2,1,0:T(8,128)(2,1)S(1)} %get-tuple-element.34), channel_id=1, source_target_pairs={{0,1},{1,0},{2,3},{3,2},{4,5},{5,4},{6,7},{7,6},{8,9},{9,8},{10,11... | collective-permute-start | bytes 49160 | tf_op jit(solution)/shard_map/ppermute | solution.py:48
  50.4 1.2 %collective-permute-done.14 = bf16[2,32,128]{2,1,0:T(8,128)(2,1)S(1)} collective-permute-done((bf16[2,32,128]{2,1,0:T(8,128)(2,1)S(1)}, bf16[2,32,128]{2,1,0:T(8,128)(2,1)S(1)}, u32[]{:S(2)}, u32[]{:S(2)}) %collective-permute-start.14) | collective-permute-done | bytes 16416 | tf_op jit(solution)/shard_map/ppermute | solution.py:48
  51.6 0.0 collective-permute-done.13
  51.6 1.2 %collective-permute-done.12 = bf16[2,32,128]{2,1,0:T(8,128)(2,1)S(1)} collective-permute-done((bf16[2,32,128]{2,1,0:T(8,128)(2,1)S(1)}, bf16[2,32,128]{2,1,0:T(8,128)(2,1)S(1)}, u32[]{:S(2)}, u32[]{:S(2)}) %collective-permute-start.12) | collective-permute-done | bytes 16416 | tf_op jit(solution)/shard_map/ppermute | solution.py:48
  52.8 0.0 collective-permute-done.15
  52.8 0.1 pad_maximum_fusion.1.tiles_ref
  52.9 0.9 %lower_half.1 = bf16[4,32,128]{2,1,0:T(8,128)(2,1)S(1)} custom-call(bf16[4,2,32,128]{3,2,1,0:T(8,128)(2,1)S(1)} %pad_maximum_fusion.4.value_ref, bf16[8,32,128]{2,1,0:T(8,128)(2,1)S(1)} %get-tuple-element.35.upper_ref, bf16[2,4,6,128,128]{4,3,2,1,0:T(8,128)(2,1)S(1)} %pad_maximum_fusion.1.tiles_ref), custom_call_target="tpu_custom_call" | custom-call | tf_op jit(solution)/shard_map/lower_half/pallas_call | solution.py:320
  53.8 0.0 collective-permute-start.18
  53.8 2.4 %collective-permute-start.17 = (bf16[4,32,128]{2,1,0:T(8,128)(2,1)S(1)}, bf16[4,32,128]{2,1,0:T(8,128)(2,1)S(1)}, u32[]{:S(2)}, u32[]{:S(2)}) collective-permute-start(bf16[4,32,128]{2,1,0:T(8,128)(2,1)S(1)} %lower_half.1), channel_id=1, source_target_pairs={{0,12},{1,13},{2,14},{3,15},{4,8},{5,9},{6,10},{7,11},{8,4},{9,5},... | collective-permute-start | bytes 98312 | tf_op jit(solution)/shard_map/ppermute | solution.py:48
  56.2 0.1 collective-permute-start.16
  56.3 0.0 collective-permute-done.18
  56.3 1.7 %collective-permute-done.17 = bf16[4,32,128]{2,1,0:T(8,128)(2,1)S(1)} collective-permute-done((bf16[4,32,128]{2,1,0:T(8,128)(2,1)S(1)}, bf16[4,32,128]{2,1,0:T(8,128)(2,1)S(1)}, u32[]{:S(2)}, u32[]{:S(2)}) %collective-permute-start.17) | collective-permute-done | bytes 32800 | tf_op jit(solution)/shard_map/ppermute | solution.py:48
  57.9 2.2 %collective-permute-done.16 = bf16[4,32,128]{2,1,0:T(8,128)(2,1)S(1)} collective-permute-done((bf16[4,32,128]{2,1,0:T(8,128)(2,1)S(1)}, bf16[4,32,128]{2,1,0:T(8,128)(2,1)S(1)}, u32[]{:S(2)}, u32[]{:S(2)}) %collective-permute-start.16) | collective-permute-done | bytes 32800 | tf_op jit(solution)/shard_map/ppermute | solution.py:48
  60.1 0.6 %pad_maximum_fusion.5 = bf16[4,64,128]{2,1,0:T(8,128)(2,1)} fusion(bf16[4,32,128]{2,1,0:T(8,128)(2,1)S(1)} %get-tuple-element.41, bf16[4,32,128]{2,1,0:T(8,128)(2,1)S(1)} %get-tuple-element.40), kind=kLoop, calls=%fused_computation.5 | loop fusion | flops 131072 | bytes 131072 | tf_op jit(solution)/shard_map/concatenate | solution.py:372
  (7 shorter events, 0.1 us)
Async XLA Ops:
  2.0 14.4 %collective-permute-start.2 = (bf16[6,128,128]{2,1,0:T(8,128)(2,1)}, bf16[6,128,128]{2,1,0:T(8,128)(2,1)S(1)}, u32[]{:S(2)}, u32[]{:S(2)}) collective-permute-start(bf16[6,128,128]{2,1,0:T(8,128)(2,1)} %get-tuple-element.26.refs_3_), channel_id=1, source_target_pairs={{0,16},{1,17},{2,18},{3,19},{4,20},{5,21},{6,22},{7,23},{8,0},{9,1... | collective-permute-start | bytes 589832 | tf_op jit(solution)/shard_map/ppermute | solution.py:48
  6.1 10.3 %collective-permute-start.1 = (bf16[6,128,128]{2,1,0:T(8,128)(2,1)}, bf16[6,128,128]{2,1,0:T(8,128)(2,1)S(1)}, u32[]{:S(2)}, u32[]{:S(2)}) collective-permute-start(bf16[6,128,128]{2,1,0:T(8,128)(2,1)} %get-tuple-element.26.refs_3_), channel_id=1, source_target_pairs={{0,8},{1,9},{2,10},{3,11},{4,12},{5,13},{6,14},{7,15},{8,0},{9,1},... | collective-permute-start | bytes 589832 | tf_op jit(solution)/shard_map/ppermute | solution.py:48
  6.1 10.3 %collective-permute-start = (bf16[6,128,128]{2,1,0:T(8,128)(2,1)}, bf16[6,128,128]{2,1,0:T(8,128)(2,1)S(1)}, u32[]{:S(2)}, u32[]{:S(2)}) collective-permute-start(bf16[6,128,128]{2,1,0:T(8,128)(2,1)} %get-tuple-element.26.refs_3_), channel_id=1, source_target_pairs={{0,0},{1,1},{2,2},{3,3},{4,4},{5,5},{6,6},{7,7},{8,16},{9,17},{10,... | collective-permute-start | bytes 589832 | tf_op jit(solution)/shard_map/ppermute | solution.py:48
  7.7 8.7 %all-to-all-start = ((bf16[4,2,64,128]{3,2,1,0:T(8,128)(2,1)}), bf16[4,2,64,128]{3,2,1,0:T(8,128)(2,1)S(1)}, u32[]{:S(2)}, u32[]{:S(2)}) async-start(bf16[4,2,64,128]{3,2,1,0:T(8,128)(2,1)} %get-tuple-element.21), calls=%async_computation | async-start | bytes 262144 | tf_op jit(solution)/shard_map/all_to_all | solution.py:343
  11.4 0.7 %copy-start.3 = (s32[64]{0:T(128)S(1)}, s32[64]{0:T(128)}, u32[]{:S(2)}) copy-start(s32[64]{0:T(128)} %index_ref.1) | copy-start | bytes 772
  12.1 4.4 %copy-start.1 = (bf16[6,128,128]{2,1,0:T(8,128)(2,1)S(1)}, bf16[6,128,128]{2,1,0:T(8,128)(2,1)}, u32[]{:S(2)}) copy-start(bf16[6,128,128]{2,1,0:T(8,128)(2,1)} %get-tuple-element.26.refs_3_) | copy-start | bytes 589828
  18.5 4.3 %copy-start = (f32[4,128,128]{2,1,0:T(8,128)S(1)}, f32[4,128,128]{2,1,0:T(8,128)}, u32[]{:S(2)}) copy-start(f32[4,128,128]{2,1,0:T(8,128)} %inverse_ref.1) | copy-start | bytes 786436
  18.5 4.3 %copy-start.2 = (f32[4,64,128]{2,1,0:T(8,128)S(1)}, f32[4,64,128]{2,1,0:T(8,128)}, u32[]{:S(2)}) copy-start(f32[4,64,128]{2,1,0:T(8,128)} %rhs_ref.1) | copy-start | bytes 393220
  18.5 24.1 %all-to-all-start.1 = ((bf16[4,12,128,128]{3,2,1,0:T(8,128)(2,1)}), bf16[4,12,128,128]{3,2,1,0:T(8,128)(2,1)S(1)}, u32[]{:S(2)}, u32[]{:S(2)}) async-start(bf16[4,12,128,128]{3,2,1,0:T(8,128)(2,1)} %broadcast_in_dim.3), calls=%async_computation.1 | async-start | bytes 3145728 | tf_op jit(solution)/shard_map/all_to_all | solution.py:98
  23.5 1.3 %collective-permute-start.3 = (bf16[4,32,128]{2,1,0:T(8,128)(2,1)S(1)}, bf16[4,32,128]{2,1,0:T(8,128)(2,1)S(1)}, u32[]{:S(2)}, u32[]{:S(2)}) collective-permute-start(bf16[4,32,128]{2,1,0:T(8,128)(2,1)S(1)} %get-tuple-element.30), channel_id=1, source_target_pairs={{0,4},{1,5},{2,6},{3,7},{4,0},{5,1},{6,2},{7,3},{8,12},{9,13},{10,... | collective-permute-start | bytes 98312 | tf_op jit(solution)/shard_map/ppermute | solution.py:48
  24.7 4.8 %collective-permute-start.6 = (bf16[4,32,128]{2,1,0:T(8,128)(2,1)S(1)}, bf16[4,32,128]{2,1,0:T(8,128)(2,1)S(1)}, u32[]{:S(2)}, u32[]{:S(2)}) collective-permute-start(bf16[4,32,128]{2,1,0:T(8,128)(2,1)S(1)} %fusion), channel_id=1, source_target_pairs={{0,8},{1,9},{2,10},{3,11},{4,12},{5,13},{6,14},{7,15},{8,0},{9,1},... | collective-permute-start | bytes 98312 | tf_op jit(solution)/shard_map/ppermute | solution.py:48
  27.6 3.9 %collective-permute-start.5 = (bf16[4,32,128]{2,1,0:T(8,128)(2,1)S(1)}, bf16[4,32,128]{2,1,0:T(8,128)(2,1)S(1)}, u32[]{:S(2)}, u32[]{:S(2)}) collective-permute-start(bf16[4,32,128]{2,1,0:T(8,128)(2,1)S(1)} %fusion), channel_id=1, source_target_pairs={{0,16},{1,17},{2,18},{3,19},{4,20},{5,21},{6,22},{7,23},{8,0},{9,1... | collective-permute-start | bytes 98312 | tf_op jit(solution)/shard_map/ppermute | solution.py:48
  28.7 2.8 %collective-permute-start.4 = (bf16[4,32,128]{2,1,0:T(8,128)(2,1)S(1)}, bf16[4,32,128]{2,1,0:T(8,128)(2,1)S(1)}, u32[]{:S(2)}, u32[]{:S(2)}) collective-permute-start(bf16[4,32,128]{2,1,0:T(8,128)(2,1)S(1)} %fusion), channel_id=1, source_target_pairs={{0,0},{1,1},{2,2},{3,3},{4,4},{5,5},{6,6},{7,7},{8,16},{9,17},{10,... | collective-permute-start | bytes 98312 | tf_op jit(solution)/shard_map/ppermute | solution.py:48
  29.4 2.2 %collective-permute-start.7 = (bf16[8,128,128]{2,1,0:T(8,128)(2,1)S(1)}, bf16[8,128,128]{2,1,0:T(8,128)(2,1)S(1)}, u32[]{:S(2)}, u32[]{:S(2)}) collective-permute-start(bf16[8,128,128]{2,1,0:T(8,128)(2,1)S(1)} %get-tuple-element.27), channel_id=1, source_target_pairs={{0,4},{1,5},{2,6},{3,7},{4,0},{5,1},{6,2},{7,3},{8,12},{9,13},{10,... | collective-permute-start | bytes 786440 | tf_op jit(solution)/shard_map/ppermute | solution.py:48
  31.7 10.9 %collective-permute-start.10 = (bf16[2,32,128]{2,1,0:T(8,128)(2,1)S(1)}, bf16[2,32,128]{2,1,0:T(8,128)(2,1)S(1)}, u32[]{:S(2)}, u32[]{:S(2)}) collective-permute-start(bf16[2,32,128]{2,1,0:T(8,128)(2,1)S(1)} %slice.21), channel_id=1, source_target_pairs={{0,3},{1,2},{2,1},{3,0},{4,7},{5,6},{6,5},{7,4},{8,11},{9,10},{10,... | collective-permute-start | bytes 49160 | tf_op jit(solution)/shard_map/ppermute | solution.py:48
  34.6 7.9 %collective-permute-start.9 = (bf16[2,32,128]{2,1,0:T(8,128)(2,1)S(1)}, bf16[2,32,128]{2,1,0:T(8,128)(2,1)S(1)}, u32[]{:S(2)}, u32[]{:S(2)}) collective-permute-start(bf16[2,32,128]{2,1,0:T(8,128)(2,1)S(1)} %slice.21), channel_id=1, source_target_pairs={{0,2},{1,3},{2,0},{3,1},{4,6},{5,7},{6,4},{7,5},{8,10},{9,11},{10,... | collective-permute-start | bytes 49160 | tf_op jit(solution)/shard_map/ppermute | solution.py:48
  35.2 7.4 %collective-permute-start.8 = (bf16[2,32,128]{2,1,0:T(8,128)(2,1)S(1)}, bf16[2,32,128]{2,1,0:T(8,128)(2,1)S(1)}, u32[]{:S(2)}, u32[]{:S(2)}) collective-permute-start(bf16[2,32,128]{2,1,0:T(8,128)(2,1)S(1)} %slice.21), channel_id=1, source_target_pairs={{0,1},{1,0},{2,3},{3,2},{4,5},{5,4},{6,7},{7,6},{8,9},{9,8},{10,11... | collective-permute-start | bytes 49160 | tf_op jit(solution)/shard_map/ppermute | solution.py:48
  43.1 2.4 %collective-permute-start.11 = (bf16[4,6,128,128]{3,2,1,0:T(8,128)(2,1)S(1)}, bf16[4,6,128,128]{3,2,1,0:T(8,128)(2,1)S(1)}, u32[]{:S(2)}, u32[]{:S(2)}) collective-permute-start(bf16[4,6,128,128]{3,2,1,0:T(8,128)(2,1)S(1)} %get-tuple-element.39), channel_id=1, source_target_pairs={{0,4},{1,5},{2,6},{3,7},{4,0},{5,1},{6,2},{7,3},{8,12},{9,13},{10,... | collective-permute-start | bytes 2359304 | tf_op jit(solution)/shard_map/ppermute | solution.py:48
  46.7 6.1 %collective-permute-start.15 = (bf16[4,6,128,128]{3,2,1,0:T(8,128)(2,1)S(1)}, bf16[4,6,128,128]{3,2,1,0:T(8,128)(2,1)S(1)}, u32[]{:S(2)}, u32[]{:S(2)}) collective-permute-start(bf16[4,6,128,128]{3,2,1,0:T(8,128)(2,1)S(1)} %get-tuple-element.36), channel_id=1, source_target_pairs={{0,4},{1,5},{2,6},{3,7},{4,0},{5,1},{6,2},{7,3},{8,12},{9,13},{10,... | collective-permute-start | bytes 2359304 | tf_op jit(solution)/shard_map/ppermute | solution.py:48
  46.9 4.7 %collective-permute-start.14 = (bf16[2,32,128]{2,1,0:T(8,128)(2,1)S(1)}, bf16[2,32,128]{2,1,0:T(8,128)(2,1)S(1)}, u32[]{:S(2)}, u32[]{:S(2)}) collective-permute-start(bf16[2,32,128]{2,1,0:T(8,128)(2,1)S(1)} %get-tuple-element.34), channel_id=1, source_target_pairs={{0,3},{1,2},{2,1},{3,0},{4,7},{5,6},{6,5},{7,4},{8,11},{9,10},{10,... | collective-permute-start | bytes 49160 | tf_op jit(solution)/shard_map/ppermute | solution.py:48
  47.6 4.0 %collective-permute-start.13 = (bf16[2,32,128]{2,1,0:T(8,128)(2,1)S(1)}, bf16[2,32,128]{2,1,0:T(8,128)(2,1)S(1)}, u32[]{:S(2)}, u32[]{:S(2)}) collective-permute-start(bf16[2,32,128]{2,1,0:T(8,128)(2,1)S(1)} %get-tuple-element.34), channel_id=1, source_target_pairs={{0,2},{1,3},{2,0},{3,1},{4,6},{5,7},{6,4},{7,5},{8,10},{9,11},{10,... | collective-permute-start | bytes 49160 | tf_op jit(solution)/shard_map/ppermute | solution.py:48
  49.0 3.7 %collective-permute-start.12 = (bf16[2,32,128]{2,1,0:T(8,128)(2,1)S(1)}, bf16[2,32,128]{2,1,0:T(8,128)(2,1)S(1)}, u32[]{:S(2)}, u32[]{:S(2)}) collective-permute-start(bf16[2,32,128]{2,1,0:T(8,128)(2,1)S(1)} %get-tuple-element.34), channel_id=1, source_target_pairs={{0,1},{1,0},{2,3},{3,2},{4,5},{5,4},{6,7},{7,6},{8,9},{9,8},{10,11... | collective-permute-start | bytes 49160 | tf_op jit(solution)/shard_map/ppermute | solution.py:48
  53.8 2.5 %collective-permute-start.18 = (bf16[4,32,128]{2,1,0:T(8,128)(2,1)S(1)}, bf16[4,32,128]{2,1,0:T(8,128)(2,1)S(1)}, u32[]{:S(2)}, u32[]{:S(2)}) collective-permute-start(bf16[4,32,128]{2,1,0:T(8,128)(2,1)S(1)} %lower_half.1), channel_id=1, source_target_pairs={{0,4},{1,5},{2,6},{3,7},{4,0},{5,1},{6,2},{7,3},{8,12},{9,13},{10,... | collective-permute-start | bytes 98312 | tf_op jit(solution)/shard_map/ppermute | solution.py:48
  53.8 4.1 %collective-permute-start.17 = (bf16[4,32,128]{2,1,0:T(8,128)(2,1)S(1)}, bf16[4,32,128]{2,1,0:T(8,128)(2,1)S(1)}, u32[]{:S(2)}, u32[]{:S(2)}) collective-permute-start(bf16[4,32,128]{2,1,0:T(8,128)(2,1)S(1)} %lower_half.1), channel_id=1, source_target_pairs={{0,12},{1,13},{2,14},{3,15},{4,8},{5,9},{6,10},{7,11},{8,4},{9,5},... | collective-permute-start | bytes 98312 | tf_op jit(solution)/shard_map/ppermute | solution.py:48
  56.2 3.9 %collective-permute-start.16 = (bf16[4,32,128]{2,1,0:T(8,128)(2,1)S(1)}, bf16[4,32,128]{2,1,0:T(8,128)(2,1)S(1)}, u32[]{:S(2)}, u32[]{:S(2)}) collective-permute-start(bf16[4,32,128]{2,1,0:T(8,128)(2,1)S(1)} %lower_half.1), channel_id=1, source_target_pairs={{0,8},{1,9},{2,10},{3,11},{4,12},{5,13},{6,14},{7,15},{8,0},{9,1},... | collective-permute-start | bytes 98312 | tf_op jit(solution)/shard_map/ppermute | solution.py:48

commit v5 on v4

--- a/solution.py
+++ b/solution.py
@@ -94,10 +94,6 @@
     return send(array, plan, pairs)
 
 
-def spread(array, plan):
-    return lax.all_to_all(jnp.broadcast_to(array, (plan.cols, *array.shape)), "col", 0, 0)
-
-
 def direct(array, plan):
     return [array] + [across_col(array, plan, m) for m in range(1, plan.cols)]
 
@@ -279,7 +275,7 @@
         r, c = j % rows, k % cols
         lists = plan.high if first else plan.low
         at = lists[r % 2, c].index((r, plan.slots.index((j // rows, k // cols))))
-        return tiles_ref[lax.bitwise_xor(core, r % 2), c, at]
+        return tiles_ref[lax.bitwise_xor(core, r % 2), lax.bitwise_xor(col_id, c), at]
 
     skip = first // cols * cols
     sums = [values[first - skip + i] for i in range(half)]
@@ -344,20 +340,27 @@
     sums = segment_sums(offdiag, row_index, known.shape[0] * known.shape[1])
     within, cross = pack(plan, [after(piece, sums, known_all) for piece in line])
 
-    got = spread(within, plan)
+    got = direct(within, plan)
 
     keep, give = local_update(known_all, after(sums, cross), rhs, diag_inv)
     total = keep + other_core(give, plan).astype(jnp.float32)
     sent = total.astype(jnp.bfloat16)
-    for m in reversed(range(1, plan.zs)):
+    for m in range(1, plan.zs // 2):
         total = total + across_z(sent, plan, m).astype(jnp.float32)
+    sent = total.astype(jnp.bfloat16)
+    total = total + across_z(sent, plan, plan.zs - 1).astype(jnp.float32)
     cross = jnp.stack([cross, other_core(cross, plan)])
-    upper = after(total[plan.upper].astype(jnp.bfloat16), cross)
+    upper = after(total[plan.upper].astype(jnp.bfloat16), cross, got[1], got[2 % plan.cols])
     values = jnp.stack(direct(upper, plan))
 
-    got = after(got, values)
-    high, low = got[:, : plan.counts[0]], got[:, plan.counts[0] :]
-    high = jnp.stack([high, other_core(high, plan)])
+    split = plan.counts[0]
+    early, late = jnp.stack(got[:-1]), after(got[-1], values)[None]
+    high = [jnp.concatenate([early[:, :split], late[:, :split]])]
+    high.append(
+        jnp.concatenate([other_core(piece[:, :split], plan) for piece in (early, late)])
+    )
+    high = jnp.stack(high)
+    low = jnp.concatenate([early[:, split:], late[:, split:]])
     sizes = (NB // 2, plan.lower.stop)
     solved, lower = call_half(
         upper_kernel, plan, "upper_half", sizes, values, total[plan.lower], high, cross

time: 61.1 us -> 59.8 us (0.979)
  local copies, waits for them, and re-layouts: 2.7 us -> 0.8 us
  waiting for transfers between devices: 19.2 us -> 20.3 us
  starting transfers between devices: 28.2 us -> 27.4 us
    all_to_all x1 -> x0, starting transfers between devices: 4.26 us -> none  [spread(): lax.all_to_all(jnp.broadcast_to(array, (plan.cols, *array.shape)), 'col',...]
    ppermute x19 -> x22, starting transfers between devices: 20.3 us -> 23.6 us  [send(): return lax.ppermute(array, AXES, flat)]
    broadcast_in_dim x1 -> x0, local copies, waits for them, and re-layouts: 1.56 us -> none  [spread(): jnp.broadcast_to(array, (plan.cols, *array.shape))]
    ppermute x19 -> x22, waiting for transfers between devices: 19.1 us -> 20.2 us  [send(): return lax.ppermute(array, AXES, flat)]
  transfers between devices with their start and end apart: 21 -> 23, of which waited for: 10 -> 14; matrix products, arithmetic and copies ran while one was open for 0% -> 1% of each run, Pallas kernels for 8% -> 7%
where the time goes in v5:
time: 59.8 us; the launch traced here: 59.5 us
  starting transfers between devices  27.4 us (46%)
  waiting for transfers between devices  20.3 us (34%)
  Pallas kernels  9.39 us (16%)
  other arithmetic  1.4 us (2%)
  local copies, waits for them, and re-layouts  0.8 us (1%)
    ppermute x22, starting transfers between devices, send(): return lax.ppermute(array, AXES, flat)  23.6 us
    ppermute x22, waiting for transfers between devices, send(): return lax.ppermute(array, AXES, flat)  20.2 us
    pallas_call x1, Pallas kernels, segment_sums(): pl.pallas_call(functools.partial(segment_kernel, chunk), in_specs=[pl.Blo...  4.25 us
    all_to_all x1, starting transfers between devices, body(): known_all = lax.all_to_all(known, 'col', 0, 0)  3.72 us
    pallas_call x1, Pallas kernels, fold_panel(): pl.pallas_call(functools.partial(fold_kernel, slots), in_specs=[pl.BlockS...  2.03 us
    pallas_call x2, Pallas kernels, call_half(): pl.pallas_call(functools.partial(kernel, plan), out_shape=[jax.ShapeDtype...  1.95 us
  transfers between devices with their start and end apart: 23, of which 14 were waited for; matrix products, arithmetic and copies ran while one was open for 1% of the time, Pallas kernels for 7%

profile of v5, /device:TPU:0, one launch (start us, length us, event | category | flops | bytes accessed | tf_op | source)
XLA Modules:
  0.0 59.5 jit_solution(4316536805606681087)
XLA Ops:
  0.0 2.0 %fold_panel.1 = (bf16[6,128,128]{2,1,0:T(8,128)(2,1)}, bf16[4,2,64,128]{3,2,1,0:T(8,128)(2,1)}) custom-call(bf16[2,4,128,128]{3,2,1,0:T(8,128)(2,1)} %panel_hbm.1, f32[4,128,128]{2,1,0:T(8,128)} %inverse_ref.1, bf16[2,64,128]{2,1,0:T(8,128)(2,1)} %known_hbm.1), custom_call_target="tpu_custom_call" | custom-call | tf_op jit(solution)/shard_map/fold_panel/pallas_call | solution.py:130
  2.0 4.1 %collective-permute-start.2 = (bf16[6,128,128]{2,1,0:T(8,128)(2,1)}, bf16[6,128,128]{2,1,0:T(8,128)(2,1)S(1)}, u32[]{:S(2)}, u32[]{:S(2)}) collective-permute-start(bf16[6,128,128]{2,1,0:T(8,128)(2,1)} %get-tuple-element.26.refs_3_), channel_id=1, source_target_pairs={{0,16},{1,17},{2,18},{3,19},{4,20},{5,21},{6,22},{7,23},{8,0},{9,1... | collective-permute-start | bytes 589832 | tf_op jit(solution)/shard_map/ppermute | solution.py:48
  6.1 0.0 collective-permute-start.1
  6.1 1.6 %collective-permute-start = (bf16[6,128,128]{2,1,0:T(8,128)(2,1)}, bf16[6,128,128]{2,1,0:T(8,128)(2,1)S(1)}, u32[]{:S(2)}, u32[]{:S(2)}) collective-permute-start(bf16[6,128,128]{2,1,0:T(8,128)(2,1)} %get-tuple-element.26.refs_3_), channel_id=1, source_target_pairs={{0,0},{1,1},{2,2},{3,3},{4,4},{5,5},{6,6},{7,7},{8,16},{9,17},{10,... | collective-permute-start | bytes 589832 | tf_op jit(solution)/shard_map/ppermute | solution.py:48
  7.7 3.7 %all-to-all-start = ((bf16[4,2,64,128]{3,2,1,0:T(8,128)(2,1)}), bf16[4,2,64,128]{3,2,1,0:T(8,128)(2,1)S(1)}, u32[]{:S(2)}, u32[]{:S(2)}) async-start(bf16[4,2,64,128]{3,2,1,0:T(8,128)(2,1)} %get-tuple-element.21), calls=%async_computation | async-start | bytes 262144 | tf_op jit(solution)/shard_map/all_to_all | solution.py:339
  11.4 0.7 %copy-done.3 = s32[64]{0:T(128)S(1)} copy-done((s32[64]{0:T(128)S(1)}, s32[64]{0:T(128)}, u32[]{:S(2)}) %copy-start.3) | copy-done | bytes 280
  12.1 4.3 %segment_sums.1.sums_ref = bf16[8,4,128,128]{3,2,1,0:T(8,128)(2,1)S(1)} custom-call(s32[64]{0:T(128)S(1)} %copy-done.3, bf16[64,4,128,128]{3,2,1,0:T(8,128)(2,1)} %tiles_hbm.1), custom_call_target="tpu_custom_call" | custom-call | flops 4194304 | bytes 8388608 | tf_op jit(solution)/shard_map/segment_sums/pallas_call | solution.py:172
  16.3 0.1 all-to-all-done.known_ref
  16.4 0.0 collective-permute-done.2.refs_2_
  16.4 0.0 collective-permute-done.1.refs_1_
  16.5 0.0 collective-permute-done.refs_0_
  16.5 0.0 copy-done.1
  16.5 0.4 pack.1
  16.9 0.0 copy-done
  16.9 0.7 %local_update.1 = (f32[4,32,128]{2,1,0:T(8,128)S(1)}, bf16[4,32,128]{2,1,0:T(8,128)(2,1)S(1)}) custom-call(bf16[4,2,64,128]{3,2,1,0:T(8,128)(2,1)S(1)} %all-to-all-done.known_ref, bf16[8,4,128,128]{3,2,1,0:T(8,128)(2,1)S(1)} %segment_sums.1.sums_ref, f32[4,64,128]{2,1,0:T(8,128)S(1)} %copy-done.2, f32[4,128,128]{2,1,0:T(8,128)S(1)} %copy-done), custom_call_target="tpu_custom_call" | custom-call | tf_op jit(solution)/shard_map/local_update/pallas_call | solution.py:217
  17.7 0.1 collective-permute-start.3
  17.7 1.2 %collective-permute-done.3 = bf16[4,32,128]{2,1,0:T(8,128)(2,1)S(1)} collective-permute-done((bf16[4,32,128]{2,1,0:T(8,128)(2,1)S(1)}, bf16[4,32,128]{2,1,0:T(8,128)(2,1)S(1)}, u32[]{:S(2)}, u32[]{:S(2)}) %collective-permute-start.3) | collective-permute-done | bytes 32800 | tf_op jit(solution)/shard_map/ppermute | solution.py:48
  18.9 2.9 %collective-permute-start.4 = (bf16[4,32,128]{2,1,0:T(8,128)(2,1)S(1)}, bf16[4,32,128]{2,1,0:T(8,128)(2,1)S(1)}, u32[]{:S(2)}, u32[]{:S(2)}) collective-permute-start(bf16[4,32,128]{2,1,0:T(8,128)(2,1)S(1)} %fusion), channel_id=1, source_target_pairs={{0,8},{1,9},{2,10},{3,11},{4,12},{5,13},{6,14},{7,15},{8,0},{9,1},... | collective-permute-start | bytes 98312 | tf_op jit(solution)/shard_map/ppermute | solution.py:48
  21.8 2.0 %collective-permute-start.8 = (bf16[12,128,128]{2,1,0:T(8,128)(2,1)S(1)}, bf16[12,128,128]{2,1,0:T(8,128)(2,1)S(1)}, u32[]{:S(2)}, u32[]{:S(2)}) collective-permute-start(bf16[12,128,128]{2,1,0:T(8,128)(2,1)S(1)} %get-tuple-element.31), channel_id=1, source_target_pairs={{0,2},{1,3},{2,0},{3,1},{4,6},{5,7},{6,4},{7,5},{8,10},{9,11},{10,... | collective-permute-start | bytes 1179656 | tf_op jit(solution)/shard_map/ppermute | solution.py:48
  23.8 1.5 %collective-permute-start.7 = (bf16[12,128,128]{2,1,0:T(8,128)(2,1)S(1)}, bf16[12,128,128]{2,1,0:T(8,128)(2,1)S(1)}, u32[]{:S(2)}, u32[]{:S(2)}) collective-permute-start(bf16[12,128,128]{2,1,0:T(8,128)(2,1)S(1)} %get-tuple-element.31), channel_id=1, source_target_pairs={{0,1},{1,0},{2,3},{3,2},{4,5},{5,4},{6,7},{7,6},{8,9},{9,8},{10,11... | collective-permute-start | bytes 1179656 | tf_op jit(solution)/shard_map/ppermute | solution.py:48
  25.2 0.0 collective-permute-done.4
  25.3 0.7 %collective-permute-start.5 = (bf16[4,32,128]{2,1,0:T(8,128)(2,1)S(1)}, bf16[4,32,128]{2,1,0:T(8,128)(2,1)S(1)}, u32[]{:S(2)}, u32[]{:S(2)}) collective-permute-start(bf16[4,32,128]{2,1,0:T(8,128)(2,1)S(1)} %fusion.1), channel_id=1, source_target_pairs={{0,0},{1,1},{2,2},{3,3},{4,4},{5,5},{6,6},{7,7},{8,16},{9,17},{10,... | collective-permute-start | bytes 98312 | tf_op jit(solution)/shard_map/ppermute | solution.py:48
  25.9 0.1 collective-permute-start.6
  26.0 1.4 %collective-permute-start.12 = (bf16[12,128,128]{2,1,0:T(8,128)(2,1)S(1)}, bf16[12,128,128]{2,1,0:T(8,128)(2,1)S(1)}, u32[]{:S(2)}, u32[]{:S(2)}) collective-permute-start(bf16[12,128,128]{2,1,0:T(8,128)(2,1)S(1)} %get-tuple-element.31), channel_id=1, source_target_pairs={{0,3},{1,2},{2,1},{3,0},{4,7},{5,6},{6,5},{7,4},{8,11},{9,10},{10,... | collective-permute-start | bytes 1179656 | tf_op jit(solution)/shard_map/ppermute | solution.py:48
  27.4 0.0 collective-permute-done.5
  27.5 0.1 collective-permute-done.6
  27.5 0.1 pad_maximum_fusion.4.cross_ref
  27.6 5.3 %collective-permute-done.8 = bf16[12,128,128]{2,1,0:T(8,128)(2,1)S(1)} collective-permute-done((bf16[12,128,128]{2,1,0:T(8,128)(2,1)S(1)}, bf16[12,128,128]{2,1,0:T(8,128)(2,1)S(1)}, u32[]{:S(2)}, u32[]{:S(2)}) %collective-permute-start.8) | collective-permute-done | bytes 393248 | tf_op jit(solution)/shard_map/ppermute | solution.py:48
  32.9 2.9 %collective-permute-done.7 = bf16[12,128,128]{2,1,0:T(8,128)(2,1)S(1)} collective-permute-done((bf16[12,128,128]{2,1,0:T(8,128)(2,1)S(1)}, bf16[12,128,128]{2,1,0:T(8,128)(2,1)S(1)}, u32[]{:S(2)}, u32[]{:S(2)}) %collective-permute-start.7) | collective-permute-done | bytes 393248 | tf_op jit(solution)/shard_map/ppermute | solution.py:48
  35.8 1.5 %collective-permute-start.11 = (bf16[2,32,128]{2,1,0:T(8,128)(2,1)S(1)}, bf16[2,32,128]{2,1,0:T(8,128)(2,1)S(1)}, u32[]{:S(2)}, u32[]{:S(2)}) collective-permute-start(bf16[2,32,128]{2,1,0:T(8,128)(2,1)S(1)} %slice.34), channel_id=1, source_target_pairs={{0,3},{1,2},{2,1},{3,0},{4,7},{5,6},{6,5},{7,4},{8,11},{9,10},{10,... | collective-permute-start | bytes 49160 | tf_op jit(solution)/shard_map/ppermute | solution.py:48
  37.3 1.5 %collective-permute-start.10 = (bf16[2,32,128]{2,1,0:T(8,128)(2,1)S(1)}, bf16[2,32,128]{2,1,0:T(8,128)(2,1)S(1)}, u32[]{:S(2)}, u32[]{:S(2)}) collective-permute-start(bf16[2,32,128]{2,1,0:T(8,128)(2,1)S(1)} %slice.34), channel_id=1, source_target_pairs={{0,2},{1,3},{2,0},{3,1},{4,6},{5,7},{6,4},{7,5},{8,10},{9,11},{10,... | collective-permute-start | bytes 49160 | tf_op jit(solution)/shard_map/ppermute | solution.py:48
  38.7 0.6 collective-permute-start.9
  39.3 0.1 pad_maximum_fusion.2
  39.4 0.1 fusion.2
  39.5 0.1 collective-permute-start.13
  39.6 3.5 %collective-permute-done.11 = bf16[2,32,128]{2,1,0:T(8,128)(2,1)S(1)} collective-permute-done((bf16[2,32,128]{2,1,0:T(8,128)(2,1)S(1)}, bf16[2,32,128]{2,1,0:T(8,128)(2,1)S(1)}, u32[]{:S(2)}, u32[]{:S(2)}) %collective-permute-start.11) | collective-permute-done | bytes 16416 | tf_op jit(solution)/shard_map/ppermute | solution.py:48
  43.2 0.1 collective-permute-done.10
  43.3 0.3 collective-permute-done.9
  43.6 0.0 collective-permute-done.12
  43.6 0.1 collective-permute-start.14
  43.7 0.1 maximum_bitcast_fusion
  43.8 0.1 pad_maximum_fusion.3
  43.9 1.3 %collective-permute-done.14 = bf16[1,6,128,128]{3,2,1,0:T(8,128)(2,1)S(1)} collective-permute-done((bf16[1,6,128,128]{3,2,1,0:T(8,128)(2,1)S(1)}, bf16[1,6,128,128]{3,2,1,0:T(8,128)(2,1)S(1)}, u32[]{:S(2)}, u32[]{:S(2)}) %collective-permute-start.14) | collective-permute-done | bytes 196640 | tf_op jit(solution)/shard_map/ppermute | solution.py:48
  45.1 0.0 collective-permute-done.13
  45.1 0.1 maximum_bitcast_fusion.1
  45.2 0.1 pad_maximum_fusion.tiles_ref
  45.4 1.1 %upper_half.1 = (bf16[8,32,128]{2,1,0:T(8,128)(2,1)S(1)}, bf16[2,32,128]{2,1,0:T(8,128)(2,1)S(1)}) custom-call(bf16[4,2,32,128]{3,2,1,0:T(8,128)(2,1)S(1)} %pad_maximum_fusion.5.value_ref, f32[2,32,128]{2,1,0:T(8,128)S(1)} %slice.28.own_ref, bf16[2,4,6,128,128]{4,3,2,1,0:T(8,128)(2,1)S(1)} %pad_maximum_fusion.tiles_ref, ...), custom_call_target="tpu_custom_call" | custom-call | tf_op jit(solution)/shard_map/upper_half/pallas_call | solution.py:316
  46.5 0.2 collective-permute-start.18
  46.7 2.3 %collective-permute-start.17 = (bf16[2,32,128]{2,1,0:T(8,128)(2,1)S(1)}, bf16[2,32,128]{2,1,0:T(8,128)(2,1)S(1)}, u32[]{:S(2)}, u32[]{:S(2)}) collective-permute-start(bf16[2,32,128]{2,1,0:T(8,128)(2,1)S(1)} %get-tuple-element.34), channel_id=1, source_target_pairs={{0,3},{1,2},{2,1},{3,0},{4,7},{5,6},{6,5},{7,4},{8,11},{9,10},{10,... | collective-permute-start | bytes 49160 | tf_op jit(solution)/shard_map/ppermute | solution.py:48
  49.0 0.6 %collective-permute-start.16 = (bf16[2,32,128]{2,1,0:T(8,128)(2,1)S(1)}, bf16[2,32,128]{2,1,0:T(8,128)(2,1)S(1)}, u32[]{:S(2)}, u32[]{:S(2)}) collective-permute-start(bf16[2,32,128]{2,1,0:T(8,128)(2,1)S(1)} %get-tuple-element.34), channel_id=1, source_target_pairs={{0,2},{1,3},{2,0},{3,1},{4,6},{5,7},{6,4},{7,5},{8,10},{9,11},{10,... | collective-permute-start | bytes 49160 | tf_op jit(solution)/shard_map/ppermute | solution.py:48
  49.6 0.6 collective-permute-start.15
  50.2 1.1 %collective-permute-done.17 = bf16[2,32,128]{2,1,0:T(8,128)(2,1)S(1)} collective-permute-done((bf16[2,32,128]{2,1,0:T(8,128)(2,1)S(1)}, bf16[2,32,128]{2,1,0:T(8,128)(2,1)S(1)}, u32[]{:S(2)}, u32[]{:S(2)}) %collective-permute-start.17) | collective-permute-done | bytes 16416 | tf_op jit(solution)/shard_map/ppermute | solution.py:48
  51.3 1.4 %collective-permute-done.16 = bf16[2,32,128]{2,1,0:T(8,128)(2,1)S(1)} collective-permute-done((bf16[2,32,128]{2,1,0:T(8,128)(2,1)S(1)}, bf16[2,32,128]{2,1,0:T(8,128)(2,1)S(1)}, u32[]{:S(2)}, u32[]{:S(2)}) %collective-permute-start.16) | collective-permute-done | bytes 16416 | tf_op jit(solution)/shard_map/ppermute | solution.py:48
  52.7 0.6 %collective-permute-done.15 = bf16[2,32,128]{2,1,0:T(8,128)(2,1)S(1)} collective-permute-done((bf16[2,32,128]{2,1,0:T(8,128)(2,1)S(1)}, bf16[2,32,128]{2,1,0:T(8,128)(2,1)S(1)}, u32[]{:S(2)}, u32[]{:S(2)}) %collective-permute-start.15) | collective-permute-done | bytes 16416 | tf_op jit(solution)/shard_map/ppermute | solution.py:48
  53.4 0.0 collective-permute-done.18
  53.4 0.1 pad_maximum_fusion.1.tiles_ref
  53.5 0.9 %lower_half.1 = bf16[4,32,128]{2,1,0:T(8,128)(2,1)S(1)} custom-call(bf16[4,2,32,128]{3,2,1,0:T(8,128)(2,1)S(1)} %pad_maximum_fusion.6.value_ref, bf16[8,32,128]{2,1,0:T(8,128)(2,1)S(1)} %get-tuple-element.35.upper_ref, bf16[2,4,6,128,128]{4,3,2,1,0:T(8,128)(2,1)S(1)} %pad_maximum_fusion.1.tiles_ref), custom_call_target="tpu_custom_call" | custom-call | tf_op jit(solution)/shard_map/lower_half/pallas_call | solution.py:316
  54.4 0.0 collective-permute-start.21
  54.4 0.5 collective-permute-start.20
  54.9 1.7 %collective-permute-start.19 = (bf16[4,32,128]{2,1,0:T(8,128)(2,1)S(1)}, bf16[4,32,128]{2,1,0:T(8,128)(2,1)S(1)}, u32[]{:S(2)}, u32[]{:S(2)}) collective-permute-start(bf16[4,32,128]{2,1,0:T(8,128)(2,1)S(1)} %lower_half.1), channel_id=1, source_target_pairs={{0,8},{1,9},{2,10},{3,11},{4,12},{5,13},{6,14},{7,15},{8,0},{9,1},... | collective-permute-start | bytes 98312 | tf_op jit(solution)/shard_map/ppermute | solution.py:48
  56.5 0.0 collective-permute-done.21
  56.5 1.2 %collective-permute-done.20 = bf16[4,32,128]{2,1,0:T(8,128)(2,1)S(1)} collective-permute-done((bf16[4,32,128]{2,1,0:T(8,128)(2,1)S(1)}, bf16[4,32,128]{2,1,0:T(8,128)(2,1)S(1)}, u32[]{:S(2)}, u32[]{:S(2)}) %collective-permute-start.20) | collective-permute-done | bytes 32800 | tf_op jit(solution)/shard_map/ppermute | solution.py:48
  57.8 1.1 %collective-permute-done.19 = bf16[4,32,128]{2,1,0:T(8,128)(2,1)S(1)} collective-permute-done((bf16[4,32,128]{2,1,0:T(8,128)(2,1)S(1)}, bf16[4,32,128]{2,1,0:T(8,128)(2,1)S(1)}, u32[]{:S(2)}, u32[]{:S(2)}) %collective-permute-start.19) | collective-permute-done | bytes 32800 | tf_op jit(solution)/shard_map/ppermute | solution.py:48
  58.9 0.6 %pad_maximum_fusion.7 = bf16[4,64,128]{2,1,0:T(8,128)(2,1)} fusion(bf16[4,32,128]{2,1,0:T(8,128)(2,1)S(1)} %get-tuple-element.42, bf16[4,32,128]{2,1,0:T(8,128)(2,1)S(1)} %get-tuple-element.41), kind=kLoop, calls=%fused_computation.9 | loop fusion | flops 131072 | bytes 131072 | tf_op jit(solution)/shard_map/concatenate | solution.py:375
  (14 shorter events, 0.1 us)
Async XLA Ops:
  2.0 14.4 %collective-permute-start.2 = (bf16[6,128,128]{2,1,0:T(8,128)(2,1)}, bf16[6,128,128]{2,1,0:T(8,128)(2,1)S(1)}, u32[]{:S(2)}, u32[]{:S(2)}) collective-permute-start(bf16[6,128,128]{2,1,0:T(8,128)(2,1)} %get-tuple-element.26.refs_3_), channel_id=1, source_target_pairs={{0,16},{1,17},{2,18},{3,19},{4,20},{5,21},{6,22},{7,23},{8,0},{9,1... | collective-permute-start | bytes 589832 | tf_op jit(solution)/shard_map/ppermute | solution.py:48
  6.1 10.3 %collective-permute-start.1 = (bf16[6,128,128]{2,1,0:T(8,128)(2,1)}, bf16[6,128,128]{2,1,0:T(8,128)(2,1)S(1)}, u32[]{:S(2)}, u32[]{:S(2)}) collective-permute-start(bf16[6,128,128]{2,1,0:T(8,128)(2,1)} %get-tuple-element.26.refs_3_), channel_id=1, source_target_pairs={{0,8},{1,9},{2,10},{3,11},{4,12},{5,13},{6,14},{7,15},{8,0},{9,1},... | collective-permute-start | bytes 589832 | tf_op jit(solution)/shard_map/ppermute | solution.py:48
  6.1 10.3 %collective-permute-start = (bf16[6,128,128]{2,1,0:T(8,128)(2,1)}, bf16[6,128,128]{2,1,0:T(8,128)(2,1)S(1)}, u32[]{:S(2)}, u32[]{:S(2)}) collective-permute-start(bf16[6,128,128]{2,1,0:T(8,128)(2,1)} %get-tuple-element.26.refs_3_), channel_id=1, source_target_pairs={{0,0},{1,1},{2,2},{3,3},{4,4},{5,5},{6,6},{7,7},{8,16},{9,17},{10,... | collective-permute-start | bytes 589832 | tf_op jit(solution)/shard_map/ppermute | solution.py:48
  7.7 8.7 %all-to-all-start = ((bf16[4,2,64,128]{3,2,1,0:T(8,128)(2,1)}), bf16[4,2,64,128]{3,2,1,0:T(8,128)(2,1)S(1)}, u32[]{:S(2)}, u32[]{:S(2)}) async-start(bf16[4,2,64,128]{3,2,1,0:T(8,128)(2,1)} %get-tuple-element.21), calls=%async_computation | async-start | bytes 262144 | tf_op jit(solution)/shard_map/all_to_all | solution.py:339
  11.4 0.7 %copy-start.3 = (s32[64]{0:T(128)S(1)}, s32[64]{0:T(128)}, u32[]{:S(2)}) copy-start(s32[64]{0:T(128)} %index_ref.1) | copy-start | bytes 772
  12.1 4.4 %copy-start.1 = (bf16[6,128,128]{2,1,0:T(8,128)(2,1)S(1)}, bf16[6,128,128]{2,1,0:T(8,128)(2,1)}, u32[]{:S(2)}) copy-start(bf16[6,128,128]{2,1,0:T(8,128)(2,1)} %get-tuple-element.26.refs_3_) | copy-start | bytes 589828
  12.1 4.8 %copy-start = (f32[4,128,128]{2,1,0:T(8,128)S(1)}, f32[4,128,128]{2,1,0:T(8,128)}, u32[]{:S(2)}) copy-start(f32[4,128,128]{2,1,0:T(8,128)} %inverse_ref.1) | copy-start | bytes 786436
  12.1 4.8 %copy-start.2 = (f32[4,64,128]{2,1,0:T(8,128)S(1)}, f32[4,64,128]{2,1,0:T(8,128)}, u32[]{:S(2)}) copy-start(f32[4,64,128]{2,1,0:T(8,128)} %rhs_ref.1) | copy-start | bytes 393220
  17.7 1.3 %collective-permute-start.3 = (bf16[4,32,128]{2,1,0:T(8,128)(2,1)S(1)}, bf16[4,32,128]{2,1,0:T(8,128)(2,1)S(1)}, u32[]{:S(2)}, u32[]{:S(2)}) collective-permute-start(bf16[4,32,128]{2,1,0:T(8,128)(2,1)S(1)} %get-tuple-element.30), channel_id=1, source_target_pairs={{0,4},{1,5},{2,6},{3,7},{4,0},{5,1},{6,2},{7,3},{8,12},{9,13},{10,... | collective-permute-start | bytes 98312 | tf_op jit(solution)/shard_map/ppermute | solution.py:48
  18.9 6.3 %collective-permute-start.4 = (bf16[4,32,128]{2,1,0:T(8,128)(2,1)S(1)}, bf16[4,32,128]{2,1,0:T(8,128)(2,1)S(1)}, u32[]{:S(2)}, u32[]{:S(2)}) collective-permute-start(bf16[4,32,128]{2,1,0:T(8,128)(2,1)S(1)} %fusion), channel_id=1, source_target_pairs={{0,8},{1,9},{2,10},{3,11},{4,12},{5,13},{6,14},{7,15},{8,0},{9,1},... | collective-permute-start | bytes 98312 | tf_op jit(solution)/shard_map/ppermute | solution.py:48
  21.8 11.1 %collective-permute-start.8 = (bf16[12,128,128]{2,1,0:T(8,128)(2,1)S(1)}, bf16[12,128,128]{2,1,0:T(8,128)(2,1)S(1)}, u32[]{:S(2)}, u32[]{:S(2)}) collective-permute-start(bf16[12,128,128]{2,1,0:T(8,128)(2,1)S(1)} %get-tuple-element.31), channel_id=1, source_target_pairs={{0,2},{1,3},{2,0},{3,1},{4,6},{5,7},{6,4},{7,5},{8,10},{9,11},{10,... | collective-permute-start | bytes 1179656 | tf_op jit(solution)/shard_map/ppermute | solution.py:48
  23.8 12.0 %collective-permute-start.7 = (bf16[12,128,128]{2,1,0:T(8,128)(2,1)S(1)}, bf16[12,128,128]{2,1,0:T(8,128)(2,1)S(1)}, u32[]{:S(2)}, u32[]{:S(2)}) collective-permute-start(bf16[12,128,128]{2,1,0:T(8,128)(2,1)S(1)} %get-tuple-element.31), channel_id=1, source_target_pairs={{0,1},{1,0},{2,3},{3,2},{4,5},{5,4},{6,7},{7,6},{8,9},{9,8},{10,11... | collective-permute-start | bytes 1179656 | tf_op jit(solution)/shard_map/ppermute | solution.py:48
  25.3 2.1 %collective-permute-start.5 = (bf16[4,32,128]{2,1,0:T(8,128)(2,1)S(1)}, bf16[4,32,128]{2,1,0:T(8,128)(2,1)S(1)}, u32[]{:S(2)}, u32[]{:S(2)}) collective-permute-start(bf16[4,32,128]{2,1,0:T(8,128)(2,1)S(1)} %fusion.1), channel_id=1, source_target_pairs={{0,0},{1,1},{2,2},{3,3},{4,4},{5,5},{6,6},{7,7},{8,16},{9,17},{10,... | collective-permute-start | bytes 98312 | tf_op jit(solution)/shard_map/ppermute | solution.py:48
  25.9 1.6 %collective-permute-start.6 = (bf16[8,128,128]{2,1,0:T(8,128)(2,1)S(1)}, bf16[8,128,128]{2,1,0:T(8,128)(2,1)S(1)}, u32[]{:S(2)}, u32[]{:S(2)}) collective-permute-start(bf16[8,128,128]{2,1,0:T(8,128)(2,1)S(1)} %get-tuple-element.27), channel_id=1, source_target_pairs={{0,4},{1,5},{2,6},{3,7},{4,0},{5,1},{6,2},{7,3},{8,12},{9,13},{10,... | collective-permute-start | bytes 786440 | tf_op jit(solution)/shard_map/ppermute | solution.py:48
  26.0 17.6 %collective-permute-start.12 = (bf16[12,128,128]{2,1,0:T(8,128)(2,1)S(1)}, bf16[12,128,128]{2,1,0:T(8,128)(2,1)S(1)}, u32[]{:S(2)}, u32[]{:S(2)}) collective-permute-start(bf16[12,128,128]{2,1,0:T(8,128)(2,1)S(1)} %get-tuple-element.31), channel_id=1, source_target_pairs={{0,3},{1,2},{2,1},{3,0},{4,7},{5,6},{6,5},{7,4},{8,11},{9,10},{10,... | collective-permute-start | bytes 1179656 | tf_op jit(solution)/shard_map/ppermute | solution.py:48
  35.8 7.4 %collective-permute-start.11 = (bf16[2,32,128]{2,1,0:T(8,128)(2,1)S(1)}, bf16[2,32,128]{2,1,0:T(8,128)(2,1)S(1)}, u32[]{:S(2)}, u32[]{:S(2)}) collective-permute-start(bf16[2,32,128]{2,1,0:T(8,128)(2,1)S(1)} %slice.34), channel_id=1, source_target_pairs={{0,3},{1,2},{2,1},{3,0},{4,7},{5,6},{6,5},{7,4},{8,11},{9,10},{10,... | collective-permute-start | bytes 49160 | tf_op jit(solution)/shard_map/ppermute | solution.py:48
  37.3 6.0 %collective-permute-start.10 = (bf16[2,32,128]{2,1,0:T(8,128)(2,1)S(1)}, bf16[2,32,128]{2,1,0:T(8,128)(2,1)S(1)}, u32[]{:S(2)}, u32[]{:S(2)}) collective-permute-start(bf16[2,32,128]{2,1,0:T(8,128)(2,1)S(1)} %slice.34), channel_id=1, source_target_pairs={{0,2},{1,3},{2,0},{3,1},{4,6},{5,7},{6,4},{7,5},{8,10},{9,11},{10,... | collective-permute-start | bytes 49160 | tf_op jit(solution)/shard_map/ppermute | solution.py:48
  38.7 4.8 %collective-permute-start.9 = (bf16[2,32,128]{2,1,0:T(8,128)(2,1)S(1)}, bf16[2,32,128]{2,1,0:T(8,128)(2,1)S(1)}, u32[]{:S(2)}, u32[]{:S(2)}) collective-permute-start(bf16[2,32,128]{2,1,0:T(8,128)(2,1)S(1)} %slice.34), channel_id=1, source_target_pairs={{0,1},{1,0},{2,3},{3,2},{4,5},{5,4},{6,7},{7,6},{8,9},{9,8},{10,11... | collective-permute-start | bytes 49160 | tf_op jit(solution)/shard_map/ppermute | solution.py:48
  39.5 5.6 %collective-permute-start.13 = (bf16[3,6,128,128]{3,2,1,0:T(8,128)(2,1)S(1)}, bf16[3,6,128,128]{3,2,1,0:T(8,128)(2,1)S(1)}, u32[]{:S(2)}, u32[]{:S(2)}) collective-permute-start(bf16[3,6,128,128]{3,2,1,0:T(8,128)(2,1)S(1)} %get-tuple-element.38), channel_id=1, source_target_pairs={{0,4},{1,5},{2,6},{3,7},{4,0},{5,1},{6,2},{7,3},{8,12},{9,13},{10,... | collective-permute-start | bytes 1769480 | tf_op jit(solution)/shard_map/ppermute | solution.py:48
  43.6 1.5 %collective-permute-start.14 = (bf16[1,6,128,128]{3,2,1,0:T(8,128)(2,1)S(1)}, bf16[1,6,128,128]{3,2,1,0:T(8,128)(2,1)S(1)}, u32[]{:S(2)}, u32[]{:S(2)}) collective-permute-start(bf16[1,6,128,128]{3,2,1,0:T(8,128)(2,1)S(1)} %get-tuple-element.40), channel_id=1, source_target_pairs={{0,4},{1,5},{2,6},{3,7},{4,0},{5,1},{6,2},{7,3},{8,12},{9,13},{10,... | collective-permute-start | bytes 589832 | tf_op jit(solution)/shard_map/ppermute | solution.py:48
  46.5 6.9 %collective-permute-start.18 = (bf16[4,6,128,128]{3,2,1,0:T(8,128)(2,1)S(1)}, bf16[4,6,128,128]{3,2,1,0:T(8,128)(2,1)S(1)}, u32[]{:S(2)}, u32[]{:S(2)}) collective-permute-start(bf16[4,6,128,128]{3,2,1,0:T(8,128)(2,1)S(1)} %pad_maximum_fusion.3), channel_id=1, source_target_pairs={{0,4},{1,5},{2,6},{3,7},{4,0},{5,1},{6,2},{7,3},{8,12},{9,13},{10,... | collective-permute-start | bytes 2359304 | tf_op jit(solution)/shard_map/ppermute | solution.py:48
  46.7 4.7 %collective-permute-start.17 = (bf16[2,32,128]{2,1,0:T(8,128)(2,1)S(1)}, bf16[2,32,128]{2,1,0:T(8,128)(2,1)S(1)}, u32[]{:S(2)}, u32[]{:S(2)}) collective-permute-start(bf16[2,32,128]{2,1,0:T(8,128)(2,1)S(1)} %get-tuple-element.34), channel_id=1, source_target_pairs={{0,3},{1,2},{2,1},{3,0},{4,7},{5,6},{6,5},{7,4},{8,11},{9,10},{10,... | collective-permute-start | bytes 49160 | tf_op jit(solution)/shard_map/ppermute | solution.py:48
  49.0 3.7 %collective-permute-start.16 = (bf16[2,32,128]{2,1,0:T(8,128)(2,1)S(1)}, bf16[2,32,128]{2,1,0:T(8,128)(2,1)S(1)}, u32[]{:S(2)}, u32[]{:S(2)}) collective-permute-start(bf16[2,32,128]{2,1,0:T(8,128)(2,1)S(1)} %get-tuple-element.34), channel_id=1, source_target_pairs={{0,2},{1,3},{2,0},{3,1},{4,6},{5,7},{6,4},{7,5},{8,10},{9,11},{10,... | collective-permute-start | bytes 49160 | tf_op jit(solution)/shard_map/ppermute | solution.py:48
  49.6 3.7 %collective-permute-start.15 = (bf16[2,32,128]{2,1,0:T(8,128)(2,1)S(1)}, bf16[2,32,128]{2,1,0:T(8,128)(2,1)S(1)}, u32[]{:S(2)}, u32[]{:S(2)}) collective-permute-start(bf16[2,32,128]{2,1,0:T(8,128)(2,1)S(1)} %get-tuple-element.34), channel_id=1, source_target_pairs={{0,1},{1,0},{2,3},{3,2},{4,5},{5,4},{6,7},{7,6},{8,9},{9,8},{10,11... | collective-permute-start | bytes 49160 | tf_op jit(solution)/shard_map/ppermute | solution.py:48
  54.4 2.2 %collective-permute-start.21 = (bf16[4,32,128]{2,1,0:T(8,128)(2,1)S(1)}, bf16[4,32,128]{2,1,0:T(8,128)(2,1)S(1)}, u32[]{:S(2)}, u32[]{:S(2)}) collective-permute-start(bf16[4,32,128]{2,1,0:T(8,128)(2,1)S(1)} %lower_half.1), channel_id=1, source_target_pairs={{0,4},{1,5},{2,6},{3,7},{4,0},{5,1},{6,2},{7,3},{8,12},{9,13},{10,... | collective-permute-start | bytes 98312 | tf_op jit(solution)/shard_map/ppermute | solution.py:48
  54.4 3.4 %collective-permute-start.20 = (bf16[4,32,128]{2,1,0:T(8,128)(2,1)S(1)}, bf16[4,32,128]{2,1,0:T(8,128)(2,1)S(1)}, u32[]{:S(2)}, u32[]{:S(2)}) collective-permute-start(bf16[4,32,128]{2,1,0:T(8,128)(2,1)S(1)} %lower_half.1), channel_id=1, source_target_pairs={{0,12},{1,13},{2,14},{3,15},{4,8},{5,9},{6,10},{7,11},{8,4},{9,5},... | collective-permute-start | bytes 98312 | tf_op jit(solution)/shard_map/ppermute | solution.py:48
  54.9 4.0 %collective-permute-start.19 = (bf16[4,32,128]{2,1,0:T(8,128)(2,1)S(1)}, bf16[4,32,128]{2,1,0:T(8,128)(2,1)S(1)}, u32[]{:S(2)}, u32[]{:S(2)}) collective-permute-start(bf16[4,32,128]{2,1,0:T(8,128)(2,1)S(1)} %lower_half.1), channel_id=1, source_target_pairs={{0,8},{1,9},{2,10},{3,11},{4,12},{5,13},{6,14},{7,15},{8,0},{9,1},... | collective-permute-start | bytes 98312 | tf_op jit(solution)/shard_map/ppermute | solution.py:48

commit v6 on v5

--- a/solution.py
+++ b/solution.py
@@ -350,11 +350,11 @@
     sent = total.astype(jnp.bfloat16)
     total = total + across_z(sent, plan, plan.zs - 1).astype(jnp.float32)
     cross = jnp.stack([cross, other_core(cross, plan)])
-    upper = after(total[plan.upper].astype(jnp.bfloat16), cross, got[1], got[2 % plan.cols])
+    upper = after(total[plan.upper].astype(jnp.bfloat16), cross, got[1])
     values = jnp.stack(direct(upper, plan))
 
     split = plan.counts[0]
-    early, late = jnp.stack(got[:-1]), after(got[-1], values)[None]
+    early, late = jnp.stack(got[:-1]), got[-1][None]
     high = [jnp.concatenate([early[:, :split], late[:, :split]])]
     high.append(
         jnp.concatenate([other_core(piece[:, :split], plan) for piece in (early, late)])

time: 59.8 us -> 59.4 us (level)
  transfers between devices with their start and end apart: 23 -> 23, of which waited for: 14 -> 12; matrix products, arithmetic and copies ran while one was open for 1% -> 1% of each run, Pallas kernels for 7% -> 7%
where the time goes in v6:
time: 59.4 us; the launch traced here: 59.1 us
  starting transfers between devices  27.4 us (46%)
  waiting for transfers between devices  19.9 us (34%)
  Pallas kernels  9.39 us (16%)
  other arithmetic  1.4 us (2%)
  local copies, waits for them, and re-layouts  0.82 us (1%)
    ppermute x22, starting transfers between devices, send(): return lax.ppermute(array, AXES, flat)  23.6 us
    ppermute x22, waiting for transfers between devices, send(): return lax.ppermute(array, AXES, flat)  19.8 us
    pallas_call x1, Pallas kernels, segment_sums(): pl.pallas_call(functools.partial(segment_kernel, chunk), in_specs=[pl.Blo...  4.25 us
    all_to_all x1, starting transfers between devices, body(): known_all = lax.all_to_all(known, 'col', 0, 0)  3.72 us
    pallas_call x1, Pallas kernels, fold_panel(): pl.pallas_call(functools.partial(fold_kernel, slots), in_specs=[pl.BlockS...  2.03 us
    pallas_call x2, Pallas kernels, call_half(): pl.pallas_call(functools.partial(kernel, plan), out_shape=[jax.ShapeDtype...  1.95 us
  transfers between devices with their start and end apart: 23, of which 12 were waited for; matrix products, arithmetic and copies ran while one was open for 1% of the time, Pallas kernels for 7%

profile of v6, /device:TPU:0, one launch (start us, length us, event | category | flops | bytes accessed | tf_op | source)
XLA Modules:
  0.0 59.1 jit_solution(3998841251883117956)
XLA Ops:
  0.0 2.0 %fold_panel.1 = (bf16[6,128,128]{2,1,0:T(8,128)(2,1)}, bf16[4,2,64,128]{3,2,1,0:T(8,128)(2,1)}) custom-call(bf16[2,4,128,128]{3,2,1,0:T(8,128)(2,1)} %panel_hbm.1, f32[4,128,128]{2,1,0:T(8,128)} %inverse_ref.1, bf16[2,64,128]{2,1,0:T(8,128)(2,1)} %known_hbm.1), custom_call_target="tpu_custom_call" | custom-call | tf_op jit(solution)/shard_map/fold_panel/pallas_call | solution.py:130
  2.0 4.1 %collective-permute-start.2 = (bf16[6,128,128]{2,1,0:T(8,128)(2,1)}, bf16[6,128,128]{2,1,0:T(8,128)(2,1)S(1)}, u32[]{:S(2)}, u32[]{:S(2)}) collective-permute-start(bf16[6,128,128]{2,1,0:T(8,128)(2,1)} %get-tuple-element.25.refs_3_), channel_id=1, source_target_pairs={{0,16},{1,17},{2,18},{3,19},{4,20},{5,21},{6,22},{7,23},{8,0},{9,1... | collective-permute-start | bytes 589832 | tf_op jit(solution)/shard_map/ppermute | solution.py:48
  6.1 0.0 collective-permute-start.1
  6.1 1.6 %collective-permute-start = (bf16[6,128,128]{2,1,0:T(8,128)(2,1)}, bf16[6,128,128]{2,1,0:T(8,128)(2,1)S(1)}, u32[]{:S(2)}, u32[]{:S(2)}) collective-permute-start(bf16[6,128,128]{2,1,0:T(8,128)(2,1)} %get-tuple-element.25.refs_3_), channel_id=1, source_target_pairs={{0,0},{1,1},{2,2},{3,3},{4,4},{5,5},{6,6},{7,7},{8,16},{9,17},{10,... | collective-permute-start | bytes 589832 | tf_op jit(solution)/shard_map/ppermute | solution.py:48
  7.7 3.7 %all-to-all-start = ((bf16[4,2,64,128]{3,2,1,0:T(8,128)(2,1)}), bf16[4,2,64,128]{3,2,1,0:T(8,128)(2,1)S(1)}, u32[]{:S(2)}, u32[]{:S(2)}) async-start(bf16[4,2,64,128]{3,2,1,0:T(8,128)(2,1)} %get-tuple-element.20), calls=%async_computation | async-start | bytes 262144 | tf_op jit(solution)/shard_map/all_to_all | solution.py:339
  11.4 0.7 %copy-done.3 = s32[64]{0:T(128)S(1)} copy-done((s32[64]{0:T(128)S(1)}, s32[64]{0:T(128)}, u32[]{:S(2)}) %copy-start.3) | copy-done | bytes 280
  12.1 4.3 %segment_sums.1.sums_ref = bf16[8,4,128,128]{3,2,1,0:T(8,128)(2,1)S(1)} custom-call(s32[64]{0:T(128)S(1)} %copy-done.3, bf16[64,4,128,128]{3,2,1,0:T(8,128)(2,1)} %tiles_hbm.1), custom_call_target="tpu_custom_call" | custom-call | flops 4194304 | bytes 8388608 | tf_op jit(solution)/shard_map/segment_sums/pallas_call | solution.py:172
  16.3 0.1 all-to-all-done.known_ref
  16.4 0.0 collective-permute-done.2.refs_2_
  16.4 0.0 collective-permute-done.1.refs_1_
  16.5 0.0 collective-permute-done.refs_0_
  16.5 0.0 copy-done.1
  16.5 0.4 pack.1
  16.9 0.0 copy-done
  16.9 0.7 %local_update.1 = (f32[4,32,128]{2,1,0:T(8,128)S(1)}, bf16[4,32,128]{2,1,0:T(8,128)(2,1)S(1)}) custom-call(bf16[4,2,64,128]{3,2,1,0:T(8,128)(2,1)S(1)} %all-to-all-done.known_ref, bf16[8,4,128,128]{3,2,1,0:T(8,128)(2,1)S(1)} %segment_sums.1.sums_ref, f32[4,64,128]{2,1,0:T(8,128)S(1)} %copy-done.2, f32[4,128,128]{2,1,0:T(8,128)S(1)} %copy-done), custom_call_target="tpu_custom_call" | custom-call | tf_op jit(solution)/shard_map/local_update/pallas_call | solution.py:217
  17.7 0.1 collective-permute-start.3
  17.7 1.2 %collective-permute-done.3 = bf16[4,32,128]{2,1,0:T(8,128)(2,1)S(1)} collective-permute-done((bf16[4,32,128]{2,1,0:T(8,128)(2,1)S(1)}, bf16[4,32,128]{2,1,0:T(8,128)(2,1)S(1)}, u32[]{:S(2)}, u32[]{:S(2)}) %collective-permute-start.3) | collective-permute-done | bytes 32800 | tf_op jit(solution)/shard_map/ppermute | solution.py:48
  18.9 2.9 %collective-permute-start.4 = (bf16[4,32,128]{2,1,0:T(8,128)(2,1)S(1)}, bf16[4,32,128]{2,1,0:T(8,128)(2,1)S(1)}, u32[]{:S(2)}, u32[]{:S(2)}) collective-permute-start(bf16[4,32,128]{2,1,0:T(8,128)(2,1)S(1)} %fusion), channel_id=1, source_target_pairs={{0,8},{1,9},{2,10},{3,11},{4,12},{5,13},{6,14},{7,15},{8,0},{9,1},... | collective-permute-start | bytes 98312 | tf_op jit(solution)/shard_map/ppermute | solution.py:48
  21.8 2.0 %collective-permute-start.11 = (bf16[12,128,128]{2,1,0:T(8,128)(2,1)S(1)}, bf16[12,128,128]{2,1,0:T(8,128)(2,1)S(1)}, u32[]{:S(2)}, u32[]{:S(2)}) collective-permute-start(bf16[12,128,128]{2,1,0:T(8,128)(2,1)S(1)} %get-tuple-element.30), channel_id=1, source_target_pairs={{0,2},{1,3},{2,0},{3,1},{4,6},{5,7},{6,4},{7,5},{8,10},{9,11},{10,... | collective-permute-start | bytes 1179656 | tf_op jit(solution)/shard_map/ppermute | solution.py:48
  23.8 1.5 %collective-permute-start.7 = (bf16[12,128,128]{2,1,0:T(8,128)(2,1)S(1)}, bf16[12,128,128]{2,1,0:T(8,128)(2,1)S(1)}, u32[]{:S(2)}, u32[]{:S(2)}) collective-permute-start(bf16[12,128,128]{2,1,0:T(8,128)(2,1)S(1)} %get-tuple-element.30), channel_id=1, source_target_pairs={{0,1},{1,0},{2,3},{3,2},{4,5},{5,4},{6,7},{7,6},{8,9},{9,8},{10,11... | collective-permute-start | bytes 1179656 | tf_op jit(solution)/shard_map/ppermute | solution.py:48
  25.2 0.0 collective-permute-done.4
  25.3 0.7 %collective-permute-start.5 = (bf16[4,32,128]{2,1,0:T(8,128)(2,1)S(1)}, bf16[4,32,128]{2,1,0:T(8,128)(2,1)S(1)}, u32[]{:S(2)}, u32[]{:S(2)}) collective-permute-start(bf16[4,32,128]{2,1,0:T(8,128)(2,1)S(1)} %fusion.1), channel_id=1, source_target_pairs={{0,0},{1,1},{2,2},{3,3},{4,4},{5,5},{6,6},{7,7},{8,16},{9,17},{10,... | collective-permute-start | bytes 98312 | tf_op jit(solution)/shard_map/ppermute | solution.py:48
  25.9 0.1 collective-permute-start.6
  26.0 1.4 %collective-permute-start.12 = (bf16[12,128,128]{2,1,0:T(8,128)(2,1)S(1)}, bf16[12,128,128]{2,1,0:T(8,128)(2,1)S(1)}, u32[]{:S(2)}, u32[]{:S(2)}) collective-permute-start(bf16[12,128,128]{2,1,0:T(8,128)(2,1)S(1)} %get-tuple-element.30), channel_id=1, source_target_pairs={{0,3},{1,2},{2,1},{3,0},{4,7},{5,6},{6,5},{7,4},{8,11},{9,10},{10,... | collective-permute-start | bytes 1179656 | tf_op jit(solution)/shard_map/ppermute | solution.py:48
  27.4 0.0 collective-permute-done.5
  27.5 0.1 collective-permute-done.6
  27.5 0.1 pad_maximum_fusion.4.cross_ref
  27.6 8.2 %collective-permute-done.7 = bf16[12,128,128]{2,1,0:T(8,128)(2,1)S(1)} collective-permute-done((bf16[12,128,128]{2,1,0:T(8,128)(2,1)S(1)}, bf16[12,128,128]{2,1,0:T(8,128)(2,1)S(1)}, u32[]{:S(2)}, u32[]{:S(2)}) %collective-permute-start.7) | collective-permute-done | bytes 393248 | tf_op jit(solution)/shard_map/ppermute | solution.py:48
  35.8 1.5 %collective-permute-start.10 = (bf16[2,32,128]{2,1,0:T(8,128)(2,1)S(1)}, bf16[2,32,128]{2,1,0:T(8,128)(2,1)S(1)}, u32[]{:S(2)}, u32[]{:S(2)}) collective-permute-start(bf16[2,32,128]{2,1,0:T(8,128)(2,1)S(1)} %slice.34), channel_id=1, source_target_pairs={{0,3},{1,2},{2,1},{3,0},{4,7},{5,6},{6,5},{7,4},{8,11},{9,10},{10,... | collective-permute-start | bytes 49160 | tf_op jit(solution)/shard_map/ppermute | solution.py:48
  37.3 1.5 %collective-permute-start.9 = (bf16[2,32,128]{2,1,0:T(8,128)(2,1)S(1)}, bf16[2,32,128]{2,1,0:T(8,128)(2,1)S(1)}, u32[]{:S(2)}, u32[]{:S(2)}) collective-permute-start(bf16[2,32,128]{2,1,0:T(8,128)(2,1)S(1)} %slice.34), channel_id=1, source_target_pairs={{0,2},{1,3},{2,0},{3,1},{4,6},{5,7},{6,4},{7,5},{8,10},{9,11},{10,... | collective-permute-start | bytes 49160 | tf_op jit(solution)/shard_map/ppermute | solution.py:48
  38.7 0.6 collective-permute-start.8
  39.3 0.0 collective-permute-done.11
  39.3 0.1 pad_maximum_fusion.2
  39.4 0.1 fusion.2
  39.6 0.1 collective-permute-start.13
  39.7 3.3 %collective-permute-done.12 = bf16[12,128,128]{2,1,0:T(8,128)(2,1)S(1)} collective-permute-done((bf16[12,128,128]{2,1,0:T(8,128)(2,1)S(1)}, bf16[12,128,128]{2,1,0:T(8,128)(2,1)S(1)}, u32[]{:S(2)}, u32[]{:S(2)}) %collective-permute-start.12) | collective-permute-done | bytes 393248 | tf_op jit(solution)/shard_map/ppermute | solution.py:48
  43.0 0.1 collective-permute-start.14
  43.1 0.1 maximum_bitcast_fusion
  43.2 0.1 pad_maximum_fusion.3
  43.3 0.0 collective-permute-done.10
  43.3 0.0 collective-permute-done.9
  43.3 0.3 collective-permute-done.8
  43.6 0.9 %collective-permute-done.14 = bf16[1,6,128,128]{3,2,1,0:T(8,128)(2,1)S(1)} collective-permute-done((bf16[1,6,128,128]{3,2,1,0:T(8,128)(2,1)S(1)}, bf16[1,6,128,128]{3,2,1,0:T(8,128)(2,1)S(1)}, u32[]{:S(2)}, u32[]{:S(2)}) %collective-permute-start.14) | collective-permute-done | bytes 196640 | tf_op jit(solution)/shard_map/ppermute | solution.py:48
  44.5 0.0 collective-permute-done.13
  44.5 0.1 maximum_bitcast_fusion.1
  44.6 0.1 pad_maximum_fusion.tiles_ref
  44.8 1.1 %upper_half.1 = (bf16[8,32,128]{2,1,0:T(8,128)(2,1)S(1)}, bf16[2,32,128]{2,1,0:T(8,128)(2,1)S(1)}) custom-call(bf16[4,2,32,128]{3,2,1,0:T(8,128)(2,1)S(1)} %pad_maximum_fusion.5.value_ref, f32[2,32,128]{2,1,0:T(8,128)S(1)} %slice.28.own_ref, bf16[2,4,6,128,128]{4,3,2,1,0:T(8,128)(2,1)S(1)} %pad_maximum_fusion.tiles_ref, ...), custom_call_target="tpu_custom_call" | custom-call | tf_op jit(solution)/shard_map/upper_half/pallas_call | solution.py:316
  45.9 0.2 collective-permute-start.18
  46.1 2.7 %collective-permute-start.17 = (bf16[2,32,128]{2,1,0:T(8,128)(2,1)S(1)}, bf16[2,32,128]{2,1,0:T(8,128)(2,1)S(1)}, u32[]{:S(2)}, u32[]{:S(2)}) collective-permute-start(bf16[2,32,128]{2,1,0:T(8,128)(2,1)S(1)} %get-tuple-element.32), channel_id=1, source_target_pairs={{0,3},{1,2},{2,1},{3,0},{4,7},{5,6},{6,5},{7,4},{8,11},{9,10},{10,... | collective-permute-start | bytes 49160 | tf_op jit(solution)/shard_map/ppermute | solution.py:48
  48.7 0.6 collective-permute-start.16
  49.3 0.3 collective-permute-start.15
  49.6 1.1 %collective-permute-done.17 = bf16[2,32,128]{2,1,0:T(8,128)(2,1)S(1)} collective-permute-done((bf16[2,32,128]{2,1,0:T(8,128)(2,1)S(1)}, bf16[2,32,128]{2,1,0:T(8,128)(2,1)S(1)}, u32[]{:S(2)}, u32[]{:S(2)}) %collective-permute-start.17) | collective-permute-done | bytes 16416 | tf_op jit(solution)/shard_map/ppermute | solution.py:48
  50.7 1.7 %collective-permute-done.16 = bf16[2,32,128]{2,1,0:T(8,128)(2,1)S(1)} collective-permute-done((bf16[2,32,128]{2,1,0:T(8,128)(2,1)S(1)}, bf16[2,32,128]{2,1,0:T(8,128)(2,1)S(1)}, u32[]{:S(2)}, u32[]{:S(2)}) %collective-permute-start.16) | collective-permute-done | bytes 16416 | tf_op jit(solution)/shard_map/ppermute | solution.py:48
  52.5 0.6 collective-permute-done.15
  53.0 0.0 collective-permute-done.18
  53.0 0.1 pad_maximum_fusion.1.tiles_ref
  53.2 0.9 %lower_half.1 = bf16[4,32,128]{2,1,0:T(8,128)(2,1)S(1)} custom-call(bf16[4,2,32,128]{3,2,1,0:T(8,128)(2,1)S(1)} %pad_maximum_fusion.6.value_ref, bf16[8,32,128]{2,1,0:T(8,128)(2,1)S(1)} %get-tuple-element.33.upper_ref, bf16[2,4,6,128,128]{4,3,2,1,0:T(8,128)(2,1)S(1)} %pad_maximum_fusion.1.tiles_ref), custom_call_target="tpu_custom_call" | custom-call | tf_op jit(solution)/shard_map/lower_half/pallas_call | solution.py:316
  54.0 0.0 collective-permute-start.21
  54.0 0.5 collective-permute-start.20
  54.5 1.7 %collective-permute-start.19 = (bf16[4,32,128]{2,1,0:T(8,128)(2,1)S(1)}, bf16[4,32,128]{2,1,0:T(8,128)(2,1)S(1)}, u32[]{:S(2)}, u32[]{:S(2)}) collective-permute-start(bf16[4,32,128]{2,1,0:T(8,128)(2,1)S(1)} %lower_half.1), channel_id=1, source_target_pairs={{0,8},{1,9},{2,10},{3,11},{4,12},{5,13},{6,14},{7,15},{8,0},{9,1},... | collective-permute-start | bytes 98312 | tf_op jit(solution)/shard_map/ppermute | solution.py:48
  56.2 0.0 collective-permute-done.21
  56.2 1.2 %collective-permute-done.20 = bf16[4,32,128]{2,1,0:T(8,128)(2,1)S(1)} collective-permute-done((bf16[4,32,128]{2,1,0:T(8,128)(2,1)S(1)}, bf16[4,32,128]{2,1,0:T(8,128)(2,1)S(1)}, u32[]{:S(2)}, u32[]{:S(2)}) %collective-permute-start.20) | collective-permute-done | bytes 32800 | tf_op jit(solution)/shard_map/ppermute | solution.py:48
  57.4 1.1 %collective-permute-done.19 = bf16[4,32,128]{2,1,0:T(8,128)(2,1)S(1)} collective-permute-done((bf16[4,32,128]{2,1,0:T(8,128)(2,1)S(1)}, bf16[4,32,128]{2,1,0:T(8,128)(2,1)S(1)}, u32[]{:S(2)}, u32[]{:S(2)}) %collective-permute-start.19) | collective-permute-done | bytes 32800 | tf_op jit(solution)/shard_map/ppermute | solution.py:48
  58.5 0.6 %pad_maximum_fusion.7 = bf16[4,64,128]{2,1,0:T(8,128)(2,1)} fusion(bf16[4,32,128]{2,1,0:T(8,128)(2,1)S(1)} %get-tuple-element.40, bf16[4,32,128]{2,1,0:T(8,128)(2,1)S(1)} %get-tuple-element.39), kind=kLoop, calls=%fused_computation.9 | loop fusion | flops 131072 | bytes 131072 | tf_op jit(solution)/shard_map/concatenate | solution.py:375
  (14 shorter events, 0.1 us)
Async XLA Ops:
  2.0 14.4 %collective-permute-start.2 = (bf16[6,128,128]{2,1,0:T(8,128)(2,1)}, bf16[6,128,128]{2,1,0:T(8,128)(2,1)S(1)}, u32[]{:S(2)}, u32[]{:S(2)}) collective-permute-start(bf16[6,128,128]{2,1,0:T(8,128)(2,1)} %get-tuple-element.25.refs_3_), channel_id=1, source_target_pairs={{0,16},{1,17},{2,18},{3,19},{4,20},{5,21},{6,22},{7,23},{8,0},{9,1... | collective-permute-start | bytes 589832 | tf_op jit(solution)/shard_map/ppermute | solution.py:48
  6.1 10.3 %collective-permute-start.1 = (bf16[6,128,128]{2,1,0:T(8,128)(2,1)}, bf16[6,128,128]{2,1,0:T(8,128)(2,1)S(1)}, u32[]{:S(2)}, u32[]{:S(2)}) collective-permute-start(bf16[6,128,128]{2,1,0:T(8,128)(2,1)} %get-tuple-element.25.refs_3_), channel_id=1, source_target_pairs={{0,8},{1,9},{2,10},{3,11},{4,12},{5,13},{6,14},{7,15},{8,0},{9,1},... | collective-permute-start | bytes 589832 | tf_op jit(solution)/shard_map/ppermute | solution.py:48
  6.1 10.3 %collective-permute-start = (bf16[6,128,128]{2,1,0:T(8,128)(2,1)}, bf16[6,128,128]{2,1,0:T(8,128)(2,1)S(1)}, u32[]{:S(2)}, u32[]{:S(2)}) collective-permute-start(bf16[6,128,128]{2,1,0:T(8,128)(2,1)} %get-tuple-element.25.refs_3_), channel_id=1, source_target_pairs={{0,0},{1,1},{2,2},{3,3},{4,4},{5,5},{6,6},{7,7},{8,16},{9,17},{10,... | collective-permute-start | bytes 589832 | tf_op jit(solution)/shard_map/ppermute | solution.py:48
  7.7 8.7 %all-to-all-start = ((bf16[4,2,64,128]{3,2,1,0:T(8,128)(2,1)}), bf16[4,2,64,128]{3,2,1,0:T(8,128)(2,1)S(1)}, u32[]{:S(2)}, u32[]{:S(2)}) async-start(bf16[4,2,64,128]{3,2,1,0:T(8,128)(2,1)} %get-tuple-element.20), calls=%async_computation | async-start | bytes 262144 | tf_op jit(solution)/shard_map/all_to_all | solution.py:339
  11.4 0.7 %copy-start.3 = (s32[64]{0:T(128)S(1)}, s32[64]{0:T(128)}, u32[]{:S(2)}) copy-start(s32[64]{0:T(128)} %index_ref.1) | copy-start | bytes 772
  12.1 4.4 %copy-start.1 = (bf16[6,128,128]{2,1,0:T(8,128)(2,1)S(1)}, bf16[6,128,128]{2,1,0:T(8,128)(2,1)}, u32[]{:S(2)}) copy-start(bf16[6,128,128]{2,1,0:T(8,128)(2,1)} %get-tuple-element.25.refs_3_) | copy-start | bytes 589828
  12.1 4.8 %copy-start = (f32[4,128,128]{2,1,0:T(8,128)S(1)}, f32[4,128,128]{2,1,0:T(8,128)}, u32[]{:S(2)}) copy-start(f32[4,128,128]{2,1,0:T(8,128)} %inverse_ref.1) | copy-start | bytes 786436
  12.1 4.8 %copy-start.2 = (f32[4,64,128]{2,1,0:T(8,128)S(1)}, f32[4,64,128]{2,1,0:T(8,128)}, u32[]{:S(2)}) copy-start(f32[4,64,128]{2,1,0:T(8,128)} %rhs_ref.1) | copy-start | bytes 393220
  17.7 1.3 %collective-permute-start.3 = (bf16[4,32,128]{2,1,0:T(8,128)(2,1)S(1)}, bf16[4,32,128]{2,1,0:T(8,128)(2,1)S(1)}, u32[]{:S(2)}, u32[]{:S(2)}) collective-permute-start(bf16[4,32,128]{2,1,0:T(8,128)(2,1)S(1)} %get-tuple-element.29), channel_id=1, source_target_pairs={{0,4},{1,5},{2,6},{3,7},{4,0},{5,1},{6,2},{7,3},{8,12},{9,13},{10,... | collective-permute-start | bytes 98312 | tf_op jit(solution)/shard_map/ppermute | solution.py:48
  18.9 6.3 %collective-permute-start.4 = (bf16[4,32,128]{2,1,0:T(8,128)(2,1)S(1)}, bf16[4,32,128]{2,1,0:T(8,128)(2,1)S(1)}, u32[]{:S(2)}, u32[]{:S(2)}) collective-permute-start(bf16[4,32,128]{2,1,0:T(8,128)(2,1)S(1)} %fusion), channel_id=1, source_target_pairs={{0,8},{1,9},{2,10},{3,11},{4,12},{5,13},{6,14},{7,15},{8,0},{9,1},... | collective-permute-start | bytes 98312 | tf_op jit(solution)/shard_map/ppermute | solution.py:48
  21.8 17.5 %collective-permute-start.11 = (bf16[12,128,128]{2,1,0:T(8,128)(2,1)S(1)}, bf16[12,128,128]{2,1,0:T(8,128)(2,1)S(1)}, u32[]{:S(2)}, u32[]{:S(2)}) collective-permute-start(bf16[12,128,128]{2,1,0:T(8,128)(2,1)S(1)} %get-tuple-element.30), channel_id=1, source_target_pairs={{0,2},{1,3},{2,0},{3,1},{4,6},{5,7},{6,4},{7,5},{8,10},{9,11},{10,... | collective-permute-start | bytes 1179656 | tf_op jit(solution)/shard_map/ppermute | solution.py:48
  23.8 12.0 %collective-permute-start.7 = (bf16[12,128,128]{2,1,0:T(8,128)(2,1)S(1)}, bf16[12,128,128]{2,1,0:T(8,128)(2,1)S(1)}, u32[]{:S(2)}, u32[]{:S(2)}) collective-permute-start(bf16[12,128,128]{2,1,0:T(8,128)(2,1)S(1)} %get-tuple-element.30), channel_id=1, source_target_pairs={{0,1},{1,0},{2,3},{3,2},{4,5},{5,4},{6,7},{7,6},{8,9},{9,8},{10,11... | collective-permute-start | bytes 1179656 | tf_op jit(solution)/shard_map/ppermute | solution.py:48
  25.3 2.1 %collective-permute-start.5 = (bf16[4,32,128]{2,1,0:T(8,128)(2,1)S(1)}, bf16[4,32,128]{2,1,0:T(8,128)(2,1)S(1)}, u32[]{:S(2)}, u32[]{:S(2)}) collective-permute-start(bf16[4,32,128]{2,1,0:T(8,128)(2,1)S(1)} %fusion.1), channel_id=1, source_target_pairs={{0,0},{1,1},{2,2},{3,3},{4,4},{5,5},{6,6},{7,7},{8,16},{9,17},{10,... | collective-permute-start | bytes 98312 | tf_op jit(solution)/shard_map/ppermute | solution.py:48
  25.9 1.6 %collective-permute-start.6 = (bf16[8,128,128]{2,1,0:T(8,128)(2,1)S(1)}, bf16[8,128,128]{2,1,0:T(8,128)(2,1)S(1)}, u32[]{:S(2)}, u32[]{:S(2)}) collective-permute-start(bf16[8,128,128]{2,1,0:T(8,128)(2,1)S(1)} %get-tuple-element.26), channel_id=1, source_target_pairs={{0,4},{1,5},{2,6},{3,7},{4,0},{5,1},{6,2},{7,3},{8,12},{9,13},{10,... | collective-permute-start | bytes 786440 | tf_op jit(solution)/shard_map/ppermute | solution.py:48
  26.0 17.0 %collective-permute-start.12 = (bf16[12,128,128]{2,1,0:T(8,128)(2,1)S(1)}, bf16[12,128,128]{2,1,0:T(8,128)(2,1)S(1)}, u32[]{:S(2)}, u32[]{:S(2)}) collective-permute-start(bf16[12,128,128]{2,1,0:T(8,128)(2,1)S(1)} %get-tuple-element.30), channel_id=1, source_target_pairs={{0,3},{1,2},{2,1},{3,0},{4,7},{5,6},{6,5},{7,4},{8,11},{9,10},{10,... | collective-permute-start | bytes 1179656 | tf_op jit(solution)/shard_map/ppermute | solution.py:48
  35.8 7.4 %collective-permute-start.10 = (bf16[2,32,128]{2,1,0:T(8,128)(2,1)S(1)}, bf16[2,32,128]{2,1,0:T(8,128)(2,1)S(1)}, u32[]{:S(2)}, u32[]{:S(2)}) collective-permute-start(bf16[2,32,128]{2,1,0:T(8,128)(2,1)S(1)} %slice.34), channel_id=1, source_target_pairs={{0,3},{1,2},{2,1},{3,0},{4,7},{5,6},{6,5},{7,4},{8,11},{9,10},{10,... | collective-permute-start | bytes 49160 | tf_op jit(solution)/shard_map/ppermute | solution.py:48
  37.3 6.0 %collective-permute-start.9 = (bf16[2,32,128]{2,1,0:T(8,128)(2,1)S(1)}, bf16[2,32,128]{2,1,0:T(8,128)(2,1)S(1)}, u32[]{:S(2)}, u32[]{:S(2)}) collective-permute-start(bf16[2,32,128]{2,1,0:T(8,128)(2,1)S(1)} %slice.34), channel_id=1, source_target_pairs={{0,2},{1,3},{2,0},{3,1},{4,6},{5,7},{6,4},{7,5},{8,10},{9,11},{10,... | collective-permute-start | bytes 49160 | tf_op jit(solution)/shard_map/ppermute | solution.py:48
  38.7 4.8 %collective-permute-start.8 = (bf16[2,32,128]{2,1,0:T(8,128)(2,1)S(1)}, bf16[2,32,128]{2,1,0:T(8,128)(2,1)S(1)}, u32[]{:S(2)}, u32[]{:S(2)}) collective-permute-start(bf16[2,32,128]{2,1,0:T(8,128)(2,1)S(1)} %slice.34), channel_id=1, source_target_pairs={{0,1},{1,0},{2,3},{3,2},{4,5},{5,4},{6,7},{7,6},{8,9},{9,8},{10,11... | collective-permute-start | bytes 49160 | tf_op jit(solution)/shard_map/ppermute | solution.py:48
  39.6 5.0 %collective-permute-start.13 = (bf16[3,6,128,128]{3,2,1,0:T(8,128)(2,1)S(1)}, bf16[3,6,128,128]{3,2,1,0:T(8,128)(2,1)S(1)}, u32[]{:S(2)}, u32[]{:S(2)}) collective-permute-start(bf16[3,6,128,128]{3,2,1,0:T(8,128)(2,1)S(1)} %get-tuple-element.36), channel_id=1, source_target_pairs={{0,4},{1,5},{2,6},{3,7},{4,0},{5,1},{6,2},{7,3},{8,12},{9,13},{10,... | collective-permute-start | bytes 1769480 | tf_op jit(solution)/shard_map/ppermute | solution.py:48
  43.0 1.5 %collective-permute-start.14 = (bf16[1,6,128,128]{3,2,1,0:T(8,128)(2,1)S(1)}, bf16[1,6,128,128]{3,2,1,0:T(8,128)(2,1)S(1)}, u32[]{:S(2)}, u32[]{:S(2)}) collective-permute-start(bf16[1,6,128,128]{3,2,1,0:T(8,128)(2,1)S(1)} %get-tuple-element.38), channel_id=1, source_target_pairs={{0,4},{1,5},{2,6},{3,7},{4,0},{5,1},{6,2},{7,3},{8,12},{9,13},{10,... | collective-permute-start | bytes 589832 | tf_op jit(solution)/shard_map/ppermute | solution.py:48
  45.9 7.2 %collective-permute-start.18 = (bf16[4,6,128,128]{3,2,1,0:T(8,128)(2,1)S(1)}, bf16[4,6,128,128]{3,2,1,0:T(8,128)(2,1)S(1)}, u32[]{:S(2)}, u32[]{:S(2)}) collective-permute-start(bf16[4,6,128,128]{3,2,1,0:T(8,128)(2,1)S(1)} %pad_maximum_fusion.3), channel_id=1, source_target_pairs={{0,4},{1,5},{2,6},{3,7},{4,0},{5,1},{6,2},{7,3},{8,12},{9,13},{10,... | collective-permute-start | bytes 2359304 | tf_op jit(solution)/shard_map/ppermute | solution.py:48
  46.1 4.7 %collective-permute-start.17 = (bf16[2,32,128]{2,1,0:T(8,128)(2,1)S(1)}, bf16[2,32,128]{2,1,0:T(8,128)(2,1)S(1)}, u32[]{:S(2)}, u32[]{:S(2)}) collective-permute-start(bf16[2,32,128]{2,1,0:T(8,128)(2,1)S(1)} %get-tuple-element.32), channel_id=1, source_target_pairs={{0,3},{1,2},{2,1},{3,0},{4,7},{5,6},{6,5},{7,4},{8,11},{9,10},{10,... | collective-permute-start | bytes 49160 | tf_op jit(solution)/shard_map/ppermute | solution.py:48
  48.7 3.7 %collective-permute-start.16 = (bf16[2,32,128]{2,1,0:T(8,128)(2,1)S(1)}, bf16[2,32,128]{2,1,0:T(8,128)(2,1)S(1)}, u32[]{:S(2)}, u32[]{:S(2)}) collective-permute-start(bf16[2,32,128]{2,1,0:T(8,128)(2,1)S(1)} %get-tuple-element.32), channel_id=1, source_target_pairs={{0,2},{1,3},{2,0},{3,1},{4,6},{5,7},{6,4},{7,5},{8,10},{9,11},{10,... | collective-permute-start | bytes 49160 | tf_op jit(solution)/shard_map/ppermute | solution.py:48
  49.3 3.7 %collective-permute-start.15 = (bf16[2,32,128]{2,1,0:T(8,128)(2,1)S(1)}, bf16[2,32,128]{2,1,0:T(8,128)(2,1)S(1)}, u32[]{:S(2)}, u32[]{:S(2)}) collective-permute-start(bf16[2,32,128]{2,1,0:T(8,128)(2,1)S(1)} %get-tuple-element.32), channel_id=1, source_target_pairs={{0,1},{1,0},{2,3},{3,2},{4,5},{5,4},{6,7},{7,6},{8,9},{9,8},{10,11... | collective-permute-start | bytes 49160 | tf_op jit(solution)/shard_map/ppermute | solution.py:48
  54.0 2.2 %collective-permute-start.21 = (bf16[4,32,128]{2,1,0:T(8,128)(2,1)S(1)}, bf16[4,32,128]{2,1,0:T(8,128)(2,1)S(1)}, u32[]{:S(2)}, u32[]{:S(2)}) collective-permute-start(bf16[4,32,128]{2,1,0:T(8,128)(2,1)S(1)} %lower_half.1), channel_id=1, source_target_pairs={{0,4},{1,5},{2,6},{3,7},{4,0},{5,1},{6,2},{7,3},{8,12},{9,13},{10,... | collective-permute-start | bytes 98312 | tf_op jit(solution)/shard_map/ppermute | solution.py:48
  54.0 3.4 %collective-permute-start.20 = (bf16[4,32,128]{2,1,0:T(8,128)(2,1)S(1)}, bf16[4,32,128]{2,1,0:T(8,128)(2,1)S(1)}, u32[]{:S(2)}, u32[]{:S(2)}) collective-permute-start(bf16[4,32,128]{2,1,0:T(8,128)(2,1)S(1)} %lower_half.1), channel_id=1, source_target_pairs={{0,12},{1,13},{2,14},{3,15},{4,8},{5,9},{6,10},{7,11},{8,4},{9,5},... | collective-permute-start | bytes 98312 | tf_op jit(solution)/shard_map/ppermute | solution.py:48
  54.5 4.0 %collective-permute-start.19 = (bf16[4,32,128]{2,1,0:T(8,128)(2,1)S(1)}, bf16[4,32,128]{2,1,0:T(8,128)(2,1)S(1)}, u32[]{:S(2)}, u32[]{:S(2)}) collective-permute-start(bf16[4,32,128]{2,1,0:T(8,128)(2,1)S(1)} %lower_half.1), channel_id=1, source_target_pairs={{0,8},{1,9},{2,10},{3,11},{4,12},{5,13},{6,14},{7,15},{8,0},{9,1},... | collective-permute-start | bytes 98312 | tf_op jit(solution)/shard_map/ppermute | solution.py:48

commit v7 on v6

--- a/solution.py
+++ b/solution.py
@@ -102,27 +102,27 @@
 
 
 def fold_kernel(slots, panel_hbm, inverse_hbm, known_hbm, out_ref, known_ref, panel_ref, inverse_ref, sems):
-    copies = [
-        pltpu.make_async_copy(inverse_hbm, inverse_ref, sems.at[0]),
-        pltpu.make_async_copy(panel_hbm, panel_ref, sems.at[1]),
-    ]
-    copies += [
-        pltpu.make_async_copy(known_hbm, known_ref.at[c], sems.at[2 + c])
-        for c in range(known_ref.shape[0])
-    ]
+    blocks, cols = inverse_ref.shape[0], known_ref.shape[0]
+    pairs = [(inverse_hbm.at[b], inverse_ref.at[b]) for b in range(blocks)]
+    pairs += [(panel_hbm.at[a, b], panel_ref.at[at]) for at, (a, b) in enumerate(slots)]
+    pairs += [(known_hbm, known_ref.at[c]) for c in range(cols)]
+    copies = [pltpu.make_async_copy(x, y, sems.at[i]) for i, (x, y) in enumerate(pairs)]
     for copy in copies:
         copy.start()
-    for copy in copies:
+    for copy in copies[:blocks]:
         copy.wait()
-    for at, (a, b) in enumerate(slots):
+    for at, (_, b) in enumerate(slots):
+        copies[blocks + at].wait()
         inverse = inverse_ref[b]
         high = inverse.astype(jnp.bfloat16)
         low = (inverse - high.astype(jnp.float32)).astype(jnp.bfloat16)
-        tile = panel_ref[a, b]
+        tile = panel_ref[at]
         out_ref[at] = (
             jnp.dot(tile, high, preferred_element_type=jnp.float32)
             + jnp.dot(tile, low, preferred_element_type=jnp.float32)
         ).astype(jnp.bfloat16)
+    for copy in copies[blocks + len(slots) :]:
+        copy.wait()
 
 
 def fold_panel(panel, inverse, known, slots, cols):
@@ -135,9 +135,9 @@
             jax.ShapeDtypeStruct((cols, *known.shape), known.dtype),
         ),
         scratch_shapes=[
-            pltpu.VMEM(panel.shape, panel.dtype),
+            pltpu.VMEM((len(slots), bs, bs), panel.dtype),
             pltpu.VMEM(inverse.shape, inverse.dtype),
-            pltpu.SemaphoreType.DMA((2 + cols,)),
+            pltpu.SemaphoreType.DMA((inverse.shape[0] + len(slots) + cols,)),
         ],
         compiler_params=pltpu.CompilerParams(vmem_limit_bytes=62 * 1024 * 1024),
         cost_estimate=NO_COST,

time: 59.4 us -> 60.2 us (1.013)
  Pallas kernels: 9.39 us -> 10.2 us
    pallas_call x1, Pallas kernels: 2.03 us -> 2.81 us  [fold_panel(): pl.pallas_call(functools.partial(fold_kernel, slots), in_specs=[pl.BlockS...]
where the time goes in v7:
time: 60.2 us; the launch traced here: 59.9 us
  starting transfers between devices  27.4 us (46%)
  waiting for transfers between devices  19.9 us (33%)
  Pallas kernels  10.2 us (17%)
  other arithmetic  1.4 us (2%)
  local copies, waits for them, and re-layouts  0.82 us (1%)
    ppermute x22, starting transfers between devices, send(): return lax.ppermute(array, AXES, flat)  23.6 us
    ppermute x22, waiting for transfers between devices, send(): return lax.ppermute(array, AXES, flat)  19.8 us
    pallas_call x1, Pallas kernels, segment_sums(): pl.pallas_call(functools.partial(segment_kernel, chunk), in_specs=[pl.Blo...  4.25 us
    all_to_all x1, starting transfers between devices, body(): known_all = lax.all_to_all(known, 'col', 0, 0)  3.71 us
    pallas_call x1, Pallas kernels, fold_panel(): pl.pallas_call(functools.partial(fold_kernel, slots), in_specs=[pl.BlockS...  2.81 us
    pallas_call x2, Pallas kernels, call_half(): pl.pallas_call(functools.partial(kernel, plan), out_shape=[jax.ShapeDtype...  1.95 us
  transfers between devices with their start and end apart: 23, of which 12 were waited for; matrix products, arithmetic and copies ran while one was open for 1% of the time, Pallas kernels for 7%

profile of v7, /device:TPU:0, one launch (start us, length us, event | category | flops | bytes accessed | tf_op | source)
XLA Modules:
  0.0 59.9 jit_solution(1650952236891493410)
XLA Ops:
  0.0 2.8 %fold_panel.1 = (bf16[6,128,128]{2,1,0:T(8,128)(2,1)}, bf16[4,2,64,128]{3,2,1,0:T(8,128)(2,1)}) custom-call(bf16[2,4,128,128]{3,2,1,0:T(8,128)(2,1)} %panel_hbm.1, f32[4,128,128]{2,1,0:T(8,128)} %inverse_ref.1, bf16[2,64,128]{2,1,0:T(8,128)(2,1)} %known_hbm.1), custom_call_target="tpu_custom_call" | custom-call | tf_op jit(solution)/shard_map/fold_panel/pallas_call | solution.py:130
  2.8 4.1 %collective-permute-start.2 = (bf16[6,128,128]{2,1,0:T(8,128)(2,1)}, bf16[6,128,128]{2,1,0:T(8,128)(2,1)S(1)}, u32[]{:S(2)}, u32[]{:S(2)}) collective-permute-start(bf16[6,128,128]{2,1,0:T(8,128)(2,1)} %get-tuple-element.25.refs_3_), channel_id=1, source_target_pairs={{0,16},{1,17},{2,18},{3,19},{4,20},{5,21},{6,22},{7,23},{8,0},{9,1... | collective-permute-start | bytes 589832 | tf_op jit(solution)/shard_map/ppermute | solution.py:48
  6.9 0.0 collective-permute-start.1
  6.9 1.6 %collective-permute-start = (bf16[6,128,128]{2,1,0:T(8,128)(2,1)}, bf16[6,128,128]{2,1,0:T(8,128)(2,1)S(1)}, u32[]{:S(2)}, u32[]{:S(2)}) collective-permute-start(bf16[6,128,128]{2,1,0:T(8,128)(2,1)} %get-tuple-element.25.refs_3_), channel_id=1, source_target_pairs={{0,0},{1,1},{2,2},{3,3},{4,4},{5,5},{6,6},{7,7},{8,16},{9,17},{10,... | collective-permute-start | bytes 589832 | tf_op jit(solution)/shard_map/ppermute | solution.py:48
  8.5 3.7 %all-to-all-start = ((bf16[4,2,64,128]{3,2,1,0:T(8,128)(2,1)}), bf16[4,2,64,128]{3,2,1,0:T(8,128)(2,1)S(1)}, u32[]{:S(2)}, u32[]{:S(2)}) async-start(bf16[4,2,64,128]{3,2,1,0:T(8,128)(2,1)} %get-tuple-element.20), calls=%async_computation | async-start | bytes 262144 | tf_op jit(solution)/shard_map/all_to_all | solution.py:339
  12.2 0.7 %copy-done.3 = s32[64]{0:T(128)S(1)} copy-done((s32[64]{0:T(128)S(1)}, s32[64]{0:T(128)}, u32[]{:S(2)}) %copy-start.3) | copy-done | bytes 280
  12.9 4.3 %segment_sums.1.sums_ref = bf16[8,4,128,128]{3,2,1,0:T(8,128)(2,1)S(1)} custom-call(s32[64]{0:T(128)S(1)} %copy-done.3, bf16[64,4,128,128]{3,2,1,0:T(8,128)(2,1)} %tiles_hbm.1), custom_call_target="tpu_custom_call" | custom-call | flops 4194304 | bytes 8388608 | tf_op jit(solution)/shard_map/segment_sums/pallas_call | solution.py:172
  17.1 0.1 all-to-all-done.known_ref
  17.2 0.0 collective-permute-done.2.refs_2_
  17.2 0.0 collective-permute-done.1.refs_1_
  17.2 0.0 collective-permute-done.refs_0_
  17.2 0.0 copy-done.1
  17.2 0.4 pack.1
  17.7 0.0 copy-done
  17.7 0.7 %local_update.1 = (f32[4,32,128]{2,1,0:T(8,128)S(1)}, bf16[4,32,128]{2,1,0:T(8,128)(2,1)S(1)}) custom-call(bf16[4,2,64,128]{3,2,1,0:T(8,128)(2,1)S(1)} %all-to-all-done.known_ref, bf16[8,4,128,128]{3,2,1,0:T(8,128)(2,1)S(1)} %segment_sums.1.sums_ref, f32[4,64,128]{2,1,0:T(8,128)S(1)} %copy-done.2, f32[4,128,128]{2,1,0:T(8,128)S(1)} %copy-done), custom_call_target="tpu_custom_call" | custom-call | tf_op jit(solution)/shard_map/local_update/pallas_call | solution.py:217
  18.4 0.1 collective-permute-start.3
  18.5 1.2 %collective-permute-done.3 = bf16[4,32,128]{2,1,0:T(8,128)(2,1)S(1)} collective-permute-done((bf16[4,32,128]{2,1,0:T(8,128)(2,1)S(1)}, bf16[4,32,128]{2,1,0:T(8,128)(2,1)S(1)}, u32[]{:S(2)}, u32[]{:S(2)}) %collective-permute-start.3) | collective-permute-done | bytes 32800 | tf_op jit(solution)/shard_map/ppermute | solution.py:48
  19.7 2.9 %collective-permute-start.4 = (bf16[4,32,128]{2,1,0:T(8,128)(2,1)S(1)}, bf16[4,32,128]{2,1,0:T(8,128)(2,1)S(1)}, u32[]{:S(2)}, u32[]{:S(2)}) collective-permute-start(bf16[4,32,128]{2,1,0:T(8,128)(2,1)S(1)} %fusion), channel_id=1, source_target_pairs={{0,8},{1,9},{2,10},{3,11},{4,12},{5,13},{6,14},{7,15},{8,0},{9,1},... | collective-permute-start | bytes 98312 | tf_op jit(solution)/shard_map/ppermute | solution.py:48
  22.6 2.0 %collective-permute-start.11 = (bf16[12,128,128]{2,1,0:T(8,128)(2,1)S(1)}, bf16[12,128,128]{2,1,0:T(8,128)(2,1)S(1)}, u32[]{:S(2)}, u32[]{:S(2)}) collective-permute-start(bf16[12,128,128]{2,1,0:T(8,128)(2,1)S(1)} %get-tuple-element.30), channel_id=1, source_target_pairs={{0,2},{1,3},{2,0},{3,1},{4,6},{5,7},{6,4},{7,5},{8,10},{9,11},{10,... | collective-permute-start | bytes 1179656 | tf_op jit(solution)/shard_map/ppermute | solution.py:48
  24.6 1.5 %collective-permute-start.7 = (bf16[12,128,128]{2,1,0:T(8,128)(2,1)S(1)}, bf16[12,128,128]{2,1,0:T(8,128)(2,1)S(1)}, u32[]{:S(2)}, u32[]{:S(2)}) collective-permute-start(bf16[12,128,128]{2,1,0:T(8,128)(2,1)S(1)} %get-tuple-element.30), channel_id=1, source_target_pairs={{0,1},{1,0},{2,3},{3,2},{4,5},{5,4},{6,7},{7,6},{8,9},{9,8},{10,11... | collective-permute-start | bytes 1179656 | tf_op jit(solution)/shard_map/ppermute | solution.py:48
  26.0 0.0 collective-permute-done.4
  26.0 0.7 %collective-permute-start.5 = (bf16[4,32,128]{2,1,0:T(8,128)(2,1)S(1)}, bf16[4,32,128]{2,1,0:T(8,128)(2,1)S(1)}, u32[]{:S(2)}, u32[]{:S(2)}) collective-permute-start(bf16[4,32,128]{2,1,0:T(8,128)(2,1)S(1)} %fusion.1), channel_id=1, source_target_pairs={{0,0},{1,1},{2,2},{3,3},{4,4},{5,5},{6,6},{7,7},{8,16},{9,17},{10,... | collective-permute-start | bytes 98312 | tf_op jit(solution)/shard_map/ppermute | solution.py:48
  26.7 0.1 collective-permute-start.6
  26.8 1.4 %collective-permute-start.12 = (bf16[12,128,128]{2,1,0:T(8,128)(2,1)S(1)}, bf16[12,128,128]{2,1,0:T(8,128)(2,1)S(1)}, u32[]{:S(2)}, u32[]{:S(2)}) collective-permute-start(bf16[12,128,128]{2,1,0:T(8,128)(2,1)S(1)} %get-tuple-element.30), channel_id=1, source_target_pairs={{0,3},{1,2},{2,1},{3,0},{4,7},{5,6},{6,5},{7,4},{8,11},{9,10},{10,... | collective-permute-start | bytes 1179656 | tf_op jit(solution)/shard_map/ppermute | solution.py:48
  28.2 0.0 collective-permute-done.5
  28.2 0.1 collective-permute-done.6
  28.3 0.1 pad_maximum_fusion.4.cross_ref
  28.4 8.2 %collective-permute-done.7 = bf16[12,128,128]{2,1,0:T(8,128)(2,1)S(1)} collective-permute-done((bf16[12,128,128]{2,1,0:T(8,128)(2,1)S(1)}, bf16[12,128,128]{2,1,0:T(8,128)(2,1)S(1)}, u32[]{:S(2)}, u32[]{:S(2)}) %collective-permute-start.7) | collective-permute-done | bytes 393248 | tf_op jit(solution)/shard_map/ppermute | solution.py:48
  36.6 1.5 %collective-permute-start.10 = (bf16[2,32,128]{2,1,0:T(8,128)(2,1)S(1)}, bf16[2,32,128]{2,1,0:T(8,128)(2,1)S(1)}, u32[]{:S(2)}, u32[]{:S(2)}) collective-permute-start(bf16[2,32,128]{2,1,0:T(8,128)(2,1)S(1)} %slice.34), channel_id=1, source_target_pairs={{0,3},{1,2},{2,1},{3,0},{4,7},{5,6},{6,5},{7,4},{8,11},{9,10},{10,... | collective-permute-start | bytes 49160 | tf_op jit(solution)/shard_map/ppermute | solution.py:48
  38.1 1.5 %collective-permute-start.9 = (bf16[2,32,128]{2,1,0:T(8,128)(2,1)S(1)}, bf16[2,32,128]{2,1,0:T(8,128)(2,1)S(1)}, u32[]{:S(2)}, u32[]{:S(2)}) collective-permute-start(bf16[2,32,128]{2,1,0:T(8,128)(2,1)S(1)} %slice.34), channel_id=1, source_target_pairs={{0,2},{1,3},{2,0},{3,1},{4,6},{5,7},{6,4},{7,5},{8,10},{9,11},{10,... | collective-permute-start | bytes 49160 | tf_op jit(solution)/shard_map/ppermute | solution.py:48
  39.5 0.6 collective-permute-start.8
  40.1 0.0 collective-permute-done.11
  40.1 0.1 pad_maximum_fusion.2
  40.2 0.1 fusion.2
  40.4 0.1 collective-permute-start.13
  40.4 3.3 %collective-permute-done.12 = bf16[12,128,128]{2,1,0:T(8,128)(2,1)S(1)} collective-permute-done((bf16[12,128,128]{2,1,0:T(8,128)(2,1)S(1)}, bf16[12,128,128]{2,1,0:T(8,128)(2,1)S(1)}, u32[]{:S(2)}, u32[]{:S(2)}) %collective-permute-start.12) | collective-permute-done | bytes 393248 | tf_op jit(solution)/shard_map/ppermute | solution.py:48
  43.8 0.1 collective-permute-start.14
  43.9 0.1 maximum_bitcast_fusion
  44.0 0.1 pad_maximum_fusion.3
  44.0 0.0 collective-permute-done.10
  44.1 0.0 collective-permute-done.9
  44.1 0.3 collective-permute-done.8
  44.4 0.9 %collective-permute-done.14 = bf16[1,6,128,128]{3,2,1,0:T(8,128)(2,1)S(1)} collective-permute-done((bf16[1,6,128,128]{3,2,1,0:T(8,128)(2,1)S(1)}, bf16[1,6,128,128]{3,2,1,0:T(8,128)(2,1)S(1)}, u32[]{:S(2)}, u32[]{:S(2)}) %collective-permute-start.14) | collective-permute-done | bytes 196640 | tf_op jit(solution)/shard_map/ppermute | solution.py:48
  45.3 0.0 collective-permute-done.13
  45.3 0.1 maximum_bitcast_fusion.1
  45.4 0.1 pad_maximum_fusion.tiles_ref
  45.5 1.1 %upper_half.1 = (bf16[8,32,128]{2,1,0:T(8,128)(2,1)S(1)}, bf16[2,32,128]{2,1,0:T(8,128)(2,1)S(1)}) custom-call(bf16[4,2,32,128]{3,2,1,0:T(8,128)(2,1)S(1)} %pad_maximum_fusion.5.value_ref, f32[2,32,128]{2,1,0:T(8,128)S(1)} %slice.28.own_ref, bf16[2,4,6,128,128]{4,3,2,1,0:T(8,128)(2,1)S(1)} %pad_maximum_fusion.tiles_ref, ...), custom_call_target="tpu_custom_call" | custom-call | tf_op jit(solution)/shard_map/upper_half/pallas_call | solution.py:316
  46.6 0.2 collective-permute-start.18
  46.8 2.7 %collective-permute-start.17 = (bf16[2,32,128]{2,1,0:T(8,128)(2,1)S(1)}, bf16[2,32,128]{2,1,0:T(8,128)(2,1)S(1)}, u32[]{:S(2)}, u32[]{:S(2)}) collective-permute-start(bf16[2,32,128]{2,1,0:T(8,128)(2,1)S(1)} %get-tuple-element.32), channel_id=1, source_target_pairs={{0,3},{1,2},{2,1},{3,0},{4,7},{5,6},{6,5},{7,4},{8,11},{9,10},{10,... | collective-permute-start | bytes 49160 | tf_op jit(solution)/shard_map/ppermute | solution.py:48
  49.5 0.6 collective-permute-start.16
  50.0 0.3 collective-permute-start.15
  50.3 1.1 %collective-permute-done.17 = bf16[2,32,128]{2,1,0:T(8,128)(2,1)S(1)} collective-permute-done((bf16[2,32,128]{2,1,0:T(8,128)(2,1)S(1)}, bf16[2,32,128]{2,1,0:T(8,128)(2,1)S(1)}, u32[]{:S(2)}, u32[]{:S(2)}) %collective-permute-start.17) | collective-permute-done | bytes 16416 | tf_op jit(solution)/shard_map/ppermute | solution.py:48
  51.5 1.7 %collective-permute-done.16 = bf16[2,32,128]{2,1,0:T(8,128)(2,1)S(1)} collective-permute-done((bf16[2,32,128]{2,1,0:T(8,128)(2,1)S(1)}, bf16[2,32,128]{2,1,0:T(8,128)(2,1)S(1)}, u32[]{:S(2)}, u32[]{:S(2)}) %collective-permute-start.16) | collective-permute-done | bytes 16416 | tf_op jit(solution)/shard_map/ppermute | solution.py:48
  53.2 0.6 collective-permute-done.15
  53.8 0.0 collective-permute-done.18
  53.8 0.1 pad_maximum_fusion.1.tiles_ref
  54.0 0.9 %lower_half.1 = bf16[4,32,128]{2,1,0:T(8,128)(2,1)S(1)} custom-call(bf16[4,2,32,128]{3,2,1,0:T(8,128)(2,1)S(1)} %pad_maximum_fusion.6.value_ref, bf16[8,32,128]{2,1,0:T(8,128)(2,1)S(1)} %get-tuple-element.33.upper_ref, bf16[2,4,6,128,128]{4,3,2,1,0:T(8,128)(2,1)S(1)} %pad_maximum_fusion.1.tiles_ref), custom_call_target="tpu_custom_call" | custom-call | tf_op jit(solution)/shard_map/lower_half/pallas_call | solution.py:316
  54.8 0.0 collective-permute-start.21
  54.8 0.5 collective-permute-start.20
  55.3 1.7 %collective-permute-start.19 = (bf16[4,32,128]{2,1,0:T(8,128)(2,1)S(1)}, bf16[4,32,128]{2,1,0:T(8,128)(2,1)S(1)}, u32[]{:S(2)}, u32[]{:S(2)}) collective-permute-start(bf16[4,32,128]{2,1,0:T(8,128)(2,1)S(1)} %lower_half.1), channel_id=1, source_target_pairs={{0,8},{1,9},{2,10},{3,11},{4,12},{5,13},{6,14},{7,15},{8,0},{9,1},... | collective-permute-start | bytes 98312 | tf_op jit(solution)/shard_map/ppermute | solution.py:48
  57.0 0.0 collective-permute-done.21
  57.0 1.2 %collective-permute-done.20 = bf16[4,32,128]{2,1,0:T(8,128)(2,1)S(1)} collective-permute-done((bf16[4,32,128]{2,1,0:T(8,128)(2,1)S(1)}, bf16[4,32,128]{2,1,0:T(8,128)(2,1)S(1)}, u32[]{:S(2)}, u32[]{:S(2)}) %collective-permute-start.20) | collective-permute-done | bytes 32800 | tf_op jit(solution)/shard_map/ppermute | solution.py:48
  58.2 1.1 %collective-permute-done.19 = bf16[4,32,128]{2,1,0:T(8,128)(2,1)S(1)} collective-permute-done((bf16[4,32,128]{2,1,0:T(8,128)(2,1)S(1)}, bf16[4,32,128]{2,1,0:T(8,128)(2,1)S(1)}, u32[]{:S(2)}, u32[]{:S(2)}) %collective-permute-start.19) | collective-permute-done | bytes 32800 | tf_op jit(solution)/shard_map/ppermute | solution.py:48
  59.3 0.6 %pad_maximum_fusion.7 = bf16[4,64,128]{2,1,0:T(8,128)(2,1)} fusion(bf16[4,32,128]{2,1,0:T(8,128)(2,1)S(1)} %get-tuple-element.40, bf16[4,32,128]{2,1,0:T(8,128)(2,1)S(1)} %get-tuple-element.39), kind=kLoop, calls=%fused_computation.9 | loop fusion | flops 131072 | bytes 131072 | tf_op jit(solution)/shard_map/concatenate | solution.py:375
  (14 shorter events, 0.1 us)
Async XLA Ops:
  2.8 14.4 %collective-permute-start.2 = (bf16[6,128,128]{2,1,0:T(8,128)(2,1)}, bf16[6,128,128]{2,1,0:T(8,128)(2,1)S(1)}, u32[]{:S(2)}, u32[]{:S(2)}) collective-permute-start(bf16[6,128,128]{2,1,0:T(8,128)(2,1)} %get-tuple-element.25.refs_3_), channel_id=1, source_target_pairs={{0,16},{1,17},{2,18},{3,19},{4,20},{5,21},{6,22},{7,23},{8,0},{9,1... | collective-permute-start | bytes 589832 | tf_op jit(solution)/shard_map/ppermute | solution.py:48
  6.9 10.3 %collective-permute-start.1 = (bf16[6,128,128]{2,1,0:T(8,128)(2,1)}, bf16[6,128,128]{2,1,0:T(8,128)(2,1)S(1)}, u32[]{:S(2)}, u32[]{:S(2)}) collective-permute-start(bf16[6,128,128]{2,1,0:T(8,128)(2,1)} %get-tuple-element.25.refs_3_), channel_id=1, source_target_pairs={{0,8},{1,9},{2,10},{3,11},{4,12},{5,13},{6,14},{7,15},{8,0},{9,1},... | collective-permute-start | bytes 589832 | tf_op jit(solution)/shard_map/ppermute | solution.py:48
  6.9 10.3 %collective-permute-start = (bf16[6,128,128]{2,1,0:T(8,128)(2,1)}, bf16[6,128,128]{2,1,0:T(8,128)(2,1)S(1)}, u32[]{:S(2)}, u32[]{:S(2)}) collective-permute-start(bf16[6,128,128]{2,1,0:T(8,128)(2,1)} %get-tuple-element.25.refs_3_), channel_id=1, source_target_pairs={{0,0},{1,1},{2,2},{3,3},{4,4},{5,5},{6,6},{7,7},{8,16},{9,17},{10,... | collective-permute-start | bytes 589832 | tf_op jit(solution)/shard_map/ppermute | solution.py:48
  8.5 8.7 %all-to-all-start = ((bf16[4,2,64,128]{3,2,1,0:T(8,128)(2,1)}), bf16[4,2,64,128]{3,2,1,0:T(8,128)(2,1)S(1)}, u32[]{:S(2)}, u32[]{:S(2)}) async-start(bf16[4,2,64,128]{3,2,1,0:T(8,128)(2,1)} %get-tuple-element.20), calls=%async_computation | async-start | bytes 262144 | tf_op jit(solution)/shard_map/all_to_all | solution.py:339
  12.2 0.7 %copy-start.3 = (s32[64]{0:T(128)S(1)}, s32[64]{0:T(128)}, u32[]{:S(2)}) copy-start(s32[64]{0:T(128)} %index_ref.1) | copy-start | bytes 772
  12.9 4.4 %copy-start.1 = (bf16[6,128,128]{2,1,0:T(8,128)(2,1)S(1)}, bf16[6,128,128]{2,1,0:T(8,128)(2,1)}, u32[]{:S(2)}) copy-start(bf16[6,128,128]{2,1,0:T(8,128)(2,1)} %get-tuple-element.25.refs_3_) | copy-start | bytes 589828
  12.9 4.8 %copy-start = (f32[4,128,128]{2,1,0:T(8,128)S(1)}, f32[4,128,128]{2,1,0:T(8,128)}, u32[]{:S(2)}) copy-start(f32[4,128,128]{2,1,0:T(8,128)} %inverse_ref.1) | copy-start | bytes 786436
  12.9 4.8 %copy-start.2 = (f32[4,64,128]{2,1,0:T(8,128)S(1)}, f32[4,64,128]{2,1,0:T(8,128)}, u32[]{:S(2)}) copy-start(f32[4,64,128]{2,1,0:T(8,128)} %rhs_ref.1) | copy-start | bytes 393220
  18.4 1.3 %collective-permute-start.3 = (bf16[4,32,128]{2,1,0:T(8,128)(2,1)S(1)}, bf16[4,32,128]{2,1,0:T(8,128)(2,1)S(1)}, u32[]{:S(2)}, u32[]{:S(2)}) collective-permute-start(bf16[4,32,128]{2,1,0:T(8,128)(2,1)S(1)} %get-tuple-element.29), channel_id=1, source_target_pairs={{0,4},{1,5},{2,6},{3,7},{4,0},{5,1},{6,2},{7,3},{8,12},{9,13},{10,... | collective-permute-start | bytes 98312 | tf_op jit(solution)/shard_map/ppermute | solution.py:48
  19.7 6.3 %collective-permute-start.4 = (bf16[4,32,128]{2,1,0:T(8,128)(2,1)S(1)}, bf16[4,32,128]{2,1,0:T(8,128)(2,1)S(1)}, u32[]{:S(2)}, u32[]{:S(2)}) collective-permute-start(bf16[4,32,128]{2,1,0:T(8,128)(2,1)S(1)} %fusion), channel_id=1, source_target_pairs={{0,8},{1,9},{2,10},{3,11},{4,12},{5,13},{6,14},{7,15},{8,0},{9,1},... | collective-permute-start | bytes 98312 | tf_op jit(solution)/shard_map/ppermute | solution.py:48
  22.6 17.5 %collective-permute-start.11 = (bf16[12,128,128]{2,1,0:T(8,128)(2,1)S(1)}, bf16[12,128,128]{2,1,0:T(8,128)(2,1)S(1)}, u32[]{:S(2)}, u32[]{:S(2)}) collective-permute-start(bf16[12,128,128]{2,1,0:T(8,128)(2,1)S(1)} %get-tuple-element.30), channel_id=1, source_target_pairs={{0,2},{1,3},{2,0},{3,1},{4,6},{5,7},{6,4},{7,5},{8,10},{9,11},{10,... | collective-permute-start | bytes 1179656 | tf_op jit(solution)/shard_map/ppermute | solution.py:48
  24.6 12.0 %collective-permute-start.7 = (bf16[12,128,128]{2,1,0:T(8,128)(2,1)S(1)}, bf16[12,128,128]{2,1,0:T(8,128)(2,1)S(1)}, u32[]{:S(2)}, u32[]{:S(2)}) collective-permute-start(bf16[12,128,128]{2,1,0:T(8,128)(2,1)S(1)} %get-tuple-element.30), channel_id=1, source_target_pairs={{0,1},{1,0},{2,3},{3,2},{4,5},{5,4},{6,7},{7,6},{8,9},{9,8},{10,11... | collective-permute-start | bytes 1179656 | tf_op jit(solution)/shard_map/ppermute | solution.py:48
  26.0 2.1 %collective-permute-start.5 = (bf16[4,32,128]{2,1,0:T(8,128)(2,1)S(1)}, bf16[4,32,128]{2,1,0:T(8,128)(2,1)S(1)}, u32[]{:S(2)}, u32[]{:S(2)}) collective-permute-start(bf16[4,32,128]{2,1,0:T(8,128)(2,1)S(1)} %fusion.1), channel_id=1, source_target_pairs={{0,0},{1,1},{2,2},{3,3},{4,4},{5,5},{6,6},{7,7},{8,16},{9,17},{10,... | collective-permute-start | bytes 98312 | tf_op jit(solution)/shard_map/ppermute | solution.py:48
  26.7 1.6 %collective-permute-start.6 = (bf16[8,128,128]{2,1,0:T(8,128)(2,1)S(1)}, bf16[8,128,128]{2,1,0:T(8,128)(2,1)S(1)}, u32[]{:S(2)}, u32[]{:S(2)}) collective-permute-start(bf16[8,128,128]{2,1,0:T(8,128)(2,1)S(1)} %get-tuple-element.26), channel_id=1, source_target_pairs={{0,4},{1,5},{2,6},{3,7},{4,0},{5,1},{6,2},{7,3},{8,12},{9,13},{10,... | collective-permute-start | bytes 786440 | tf_op jit(solution)/shard_map/ppermute | solution.py:48
  26.8 17.0 %collective-permute-start.12 = (bf16[12,128,128]{2,1,0:T(8,128)(2,1)S(1)}, bf16[12,128,128]{2,1,0:T(8,128)(2,1)S(1)}, u32[]{:S(2)}, u32[]{:S(2)}) collective-permute-start(bf16[12,128,128]{2,1,0:T(8,128)(2,1)S(1)} %get-tuple-element.30), channel_id=1, source_target_pairs={{0,3},{1,2},{2,1},{3,0},{4,7},{5,6},{6,5},{7,4},{8,11},{9,10},{10,... | collective-permute-start | bytes 1179656 | tf_op jit(solution)/shard_map/ppermute | solution.py:48
  36.6 7.4 %collective-permute-start.10 = (bf16[2,32,128]{2,1,0:T(8,128)(2,1)S(1)}, bf16[2,32,128]{2,1,0:T(8,128)(2,1)S(1)}, u32[]{:S(2)}, u32[]{:S(2)}) collective-permute-start(bf16[2,32,128]{2,1,0:T(8,128)(2,1)S(1)} %slice.34), channel_id=1, source_target_pairs={{0,3},{1,2},{2,1},{3,0},{4,7},{5,6},{6,5},{7,4},{8,11},{9,10},{10,... | collective-permute-start | bytes 49160 | tf_op jit(solution)/shard_map/ppermute | solution.py:48
  38.1 6.0 %collective-permute-start.9 = (bf16[2,32,128]{2,1,0:T(8,128)(2,1)S(1)}, bf16[2,32,128]{2,1,0:T(8,128)(2,1)S(1)}, u32[]{:S(2)}, u32[]{:S(2)}) collective-permute-start(bf16[2,32,128]{2,1,0:T(8,128)(2,1)S(1)} %slice.34), channel_id=1, source_target_pairs={{0,2},{1,3},{2,0},{3,1},{4,6},{5,7},{6,4},{7,5},{8,10},{9,11},{10,... | collective-permute-start | bytes 49160 | tf_op jit(solution)/shard_map/ppermute | solution.py:48
  39.5 4.8 %collective-permute-start.8 = (bf16[2,32,128]{2,1,0:T(8,128)(2,1)S(1)}, bf16[2,32,128]{2,1,0:T(8,128)(2,1)S(1)}, u32[]{:S(2)}, u32[]{:S(2)}) collective-permute-start(bf16[2,32,128]{2,1,0:T(8,128)(2,1)S(1)} %slice.34), channel_id=1, source_target_pairs={{0,1},{1,0},{2,3},{3,2},{4,5},{5,4},{6,7},{7,6},{8,9},{9,8},{10,11... | collective-permute-start | bytes 49160 | tf_op jit(solution)/shard_map/ppermute | solution.py:48
  40.4 5.0 %collective-permute-start.13 = (bf16[3,6,128,128]{3,2,1,0:T(8,128)(2,1)S(1)}, bf16[3,6,128,128]{3,2,1,0:T(8,128)(2,1)S(1)}, u32[]{:S(2)}, u32[]{:S(2)}) collective-permute-start(bf16[3,6,128,128]{3,2,1,0:T(8,128)(2,1)S(1)} %get-tuple-element.36), channel_id=1, source_target_pairs={{0,4},{1,5},{2,6},{3,7},{4,0},{5,1},{6,2},{7,3},{8,12},{9,13},{10,... | collective-permute-start | bytes 1769480 | tf_op jit(solution)/shard_map/ppermute | solution.py:48
  43.8 1.5 %collective-permute-start.14 = (bf16[1,6,128,128]{3,2,1,0:T(8,128)(2,1)S(1)}, bf16[1,6,128,128]{3,2,1,0:T(8,128)(2,1)S(1)}, u32[]{:S(2)}, u32[]{:S(2)}) collective-permute-start(bf16[1,6,128,128]{3,2,1,0:T(8,128)(2,1)S(1)} %get-tuple-element.38), channel_id=1, source_target_pairs={{0,4},{1,5},{2,6},{3,7},{4,0},{5,1},{6,2},{7,3},{8,12},{9,13},{10,... | collective-permute-start | bytes 589832 | tf_op jit(solution)/shard_map/ppermute | solution.py:48
  46.6 7.2 %collective-permute-start.18 = (bf16[4,6,128,128]{3,2,1,0:T(8,128)(2,1)S(1)}, bf16[4,6,128,128]{3,2,1,0:T(8,128)(2,1)S(1)}, u32[]{:S(2)}, u32[]{:S(2)}) collective-permute-start(bf16[4,6,128,128]{3,2,1,0:T(8,128)(2,1)S(1)} %pad_maximum_fusion.3), channel_id=1, source_target_pairs={{0,4},{1,5},{2,6},{3,7},{4,0},{5,1},{6,2},{7,3},{8,12},{9,13},{10,... | collective-permute-start | bytes 2359304 | tf_op jit(solution)/shard_map/ppermute | solution.py:48
  46.8 4.7 %collective-permute-start.17 = (bf16[2,32,128]{2,1,0:T(8,128)(2,1)S(1)}, bf16[2,32,128]{2,1,0:T(8,128)(2,1)S(1)}, u32[]{:S(2)}, u32[]{:S(2)}) collective-permute-start(bf16[2,32,128]{2,1,0:T(8,128)(2,1)S(1)} %get-tuple-element.32), channel_id=1, source_target_pairs={{0,3},{1,2},{2,1},{3,0},{4,7},{5,6},{6,5},{7,4},{8,11},{9,10},{10,... | collective-permute-start | bytes 49160 | tf_op jit(solution)/shard_map/ppermute | solution.py:48
  49.5 3.7 %collective-permute-start.16 = (bf16[2,32,128]{2,1,0:T(8,128)(2,1)S(1)}, bf16[2,32,128]{2,1,0:T(8,128)(2,1)S(1)}, u32[]{:S(2)}, u32[]{:S(2)}) collective-permute-start(bf16[2,32,128]{2,1,0:T(8,128)(2,1)S(1)} %get-tuple-element.32), channel_id=1, source_target_pairs={{0,2},{1,3},{2,0},{3,1},{4,6},{5,7},{6,4},{7,5},{8,10},{9,11},{10,... | collective-permute-start | bytes 49160 | tf_op jit(solution)/shard_map/ppermute | solution.py:48
  50.0 3.7 %collective-permute-start.15 = (bf16[2,32,128]{2,1,0:T(8,128)(2,1)S(1)}, bf16[2,32,128]{2,1,0:T(8,128)(2,1)S(1)}, u32[]{:S(2)}, u32[]{:S(2)}) collective-permute-start(bf16[2,32,128]{2,1,0:T(8,128)(2,1)S(1)} %get-tuple-element.32), channel_id=1, source_target_pairs={{0,1},{1,0},{2,3},{3,2},{4,5},{5,4},{6,7},{7,6},{8,9},{9,8},{10,11... | collective-permute-start | bytes 49160 | tf_op jit(solution)/shard_map/ppermute | solution.py:48
  54.8 2.2 %collective-permute-start.21 = (bf16[4,32,128]{2,1,0:T(8,128)(2,1)S(1)}, bf16[4,32,128]{2,1,0:T(8,128)(2,1)S(1)}, u32[]{:S(2)}, u32[]{:S(2)}) collective-permute-start(bf16[4,32,128]{2,1,0:T(8,128)(2,1)S(1)} %lower_half.1), channel_id=1, source_target_pairs={{0,4},{1,5},{2,6},{3,7},{4,0},{5,1},{6,2},{7,3},{8,12},{9,13},{10,... | collective-permute-start | bytes 98312 | tf_op jit(solution)/shard_map/ppermute | solution.py:48
  54.8 3.4 %collective-permute-start.20 = (bf16[4,32,128]{2,1,0:T(8,128)(2,1)S(1)}, bf16[4,32,128]{2,1,0:T(8,128)(2,1)S(1)}, u32[]{:S(2)}, u32[]{:S(2)}) collective-permute-start(bf16[4,32,128]{2,1,0:T(8,128)(2,1)S(1)} %lower_half.1), channel_id=1, source_target_pairs={{0,12},{1,13},{2,14},{3,15},{4,8},{5,9},{6,10},{7,11},{8,4},{9,5},... | collective-permute-start | bytes 98312 | tf_op jit(solution)/shard_map/ppermute | solution.py:48
  55.3 4.0 %collective-permute-start.19 = (bf16[4,32,128]{2,1,0:T(8,128)(2,1)S(1)}, bf16[4,32,128]{2,1,0:T(8,128)(2,1)S(1)}, u32[]{:S(2)}, u32[]{:S(2)}) collective-permute-start(bf16[4,32,128]{2,1,0:T(8,128)(2,1)S(1)} %lower_half.1), channel_id=1, source_target_pairs={{0,8},{1,9},{2,10},{3,11},{4,12},{5,13},{6,14},{7,15},{8,0},{9,1},... | collective-permute-start | bytes 98312 | tf_op jit(solution)/shard_map/ppermute | solution.py:48

commit v8 on v6

--- a/solution.py
+++ b/solution.py
@@ -338,7 +338,7 @@
     line = [folded] + [across_z(folded, plan, m) for m in range(1, plan.zs)]
     known_all = lax.all_to_all(known, "col", 0, 0)
     sums = segment_sums(offdiag, row_index, known.shape[0] * known.shape[1])
-    within, cross = pack(plan, [after(piece, sums, known_all) for piece in line])
+    within, cross = pack(plan, [after(piece, known_all) for piece in line])
 
     got = direct(within, plan)
 

time: 59.4 us -> 59.2 us (level)
  waiting for transfers between devices: 19.9 us -> 18.4 us
  starting transfers between devices: 27.4 us -> 28.6 us
    ppermute x22, waiting for transfers between devices: 19.8 us -> 18.3 us  [send(): return lax.ppermute(array, AXES, flat)]
    ppermute x22, starting transfers between devices: 23.6 us -> 24.9 us  [send(): return lax.ppermute(array, AXES, flat)]
  transfers between devices with their start and end apart: 23 -> 23, of which waited for: 12 -> 10; matrix products, arithmetic and copies ran while one was open for 1% -> 1% of each run, Pallas kernels for 7% -> 7%
where the time goes in v8:
time: 59.2 us; the launch traced here: 58.9 us
  starting transfers between devices  28.6 us (48%)
  waiting for transfers between devices  18.4 us (31%)
  Pallas kernels  9.39 us (16%)
  other arithmetic  1.4 us (2%)
  local copies, waits for them, and re-layouts  0.82 us (1%)
    ppermute x22, starting transfers between devices, send(): return lax.ppermute(array, AXES, flat)  24.9 us
    ppermute x22, waiting for transfers between devices, send(): return lax.ppermute(array, AXES, flat)  18.3 us
    pallas_call x1, Pallas kernels, segment_sums(): pl.pallas_call(functools.partial(segment_kernel, chunk), in_specs=[pl.Blo...  4.25 us
    all_to_all x1, starting transfers between devices, body(): known_all = lax.all_to_all(known, 'col', 0, 0)  3.72 us
    pallas_call x1, Pallas kernels, fold_panel(): pl.pallas_call(functools.partial(fold_kernel, slots), in_specs=[pl.BlockS...  2.03 us
    pallas_call x2, Pallas kernels, call_half(): pl.pallas_call(functools.partial(kernel, plan), out_shape=[jax.ShapeDtype...  1.95 us
  transfers between devices with their start and end apart: 23, of which 10 were waited for; matrix products, arithmetic and copies ran while one was open for 1% of the time, Pallas kernels for 7%

profile of v8, /device:TPU:0, one launch (start us, length us, event | category | flops | bytes accessed | tf_op | source)
XLA Modules:
  0.0 58.9 jit_solution(15567168778942637987)
XLA Ops:
  0.0 2.0 %fold_panel.1 = (bf16[6,128,128]{2,1,0:T(8,128)(2,1)}, bf16[4,2,64,128]{3,2,1,0:T(8,128)(2,1)}) custom-call(bf16[2,4,128,128]{3,2,1,0:T(8,128)(2,1)} %panel_hbm.1, f32[4,128,128]{2,1,0:T(8,128)} %inverse_ref.1, bf16[2,64,128]{2,1,0:T(8,128)(2,1)} %known_hbm.1), custom_call_target="tpu_custom_call" | custom-call | tf_op jit(solution)/shard_map/fold_panel/pallas_call | solution.py:130
  2.0 1.6 %collective-permute-start = (bf16[6,128,128]{2,1,0:T(8,128)(2,1)}, bf16[6,128,128]{2,1,0:T(8,128)(2,1)S(1)}, u32[]{:S(2)}, u32[]{:S(2)}) collective-permute-start(bf16[6,128,128]{2,1,0:T(8,128)(2,1)} %get-tuple-element.25.refs_3_), channel_id=1, source_target_pairs={{0,0},{1,1},{2,2},{3,3},{4,4},{5,5},{6,6},{7,7},{8,16},{9,17},{10,... | collective-permute-start | bytes 589832 | tf_op jit(solution)/shard_map/ppermute | solution.py:48
  3.6 5.0 %collective-permute-start.1 = (bf16[6,128,128]{2,1,0:T(8,128)(2,1)}, bf16[6,128,128]{2,1,0:T(8,128)(2,1)S(1)}, u32[]{:S(2)}, u32[]{:S(2)}) collective-permute-start(bf16[6,128,128]{2,1,0:T(8,128)(2,1)} %get-tuple-element.25.refs_3_), channel_id=1, source_target_pairs={{0,8},{1,9},{2,10},{3,11},{4,12},{5,13},{6,14},{7,15},{8,0},{9,1},... | collective-permute-start | bytes 589832 | tf_op jit(solution)/shard_map/ppermute | solution.py:48
  8.6 0.6 %collective-permute-start.2 = (bf16[6,128,128]{2,1,0:T(8,128)(2,1)}, bf16[6,128,128]{2,1,0:T(8,128)(2,1)S(1)}, u32[]{:S(2)}, u32[]{:S(2)}) collective-permute-start(bf16[6,128,128]{2,1,0:T(8,128)(2,1)} %get-tuple-element.25.refs_3_), channel_id=1, source_target_pairs={{0,16},{1,17},{2,18},{3,19},{4,20},{5,21},{6,22},{7,23},{8,0},{9,1... | collective-permute-start | bytes 589832 | tf_op jit(solution)/shard_map/ppermute | solution.py:48
  9.2 3.7 %all-to-all-start = ((bf16[4,2,64,128]{3,2,1,0:T(8,128)(2,1)}), bf16[4,2,64,128]{3,2,1,0:T(8,128)(2,1)S(1)}, u32[]{:S(2)}, u32[]{:S(2)}) async-start(bf16[4,2,64,128]{3,2,1,0:T(8,128)(2,1)} %get-tuple-element.20), calls=%async_computation | async-start | bytes 262144 | tf_op jit(solution)/shard_map/all_to_all | solution.py:339
  13.0 0.7 %copy-done.3 = s32[64]{0:T(128)S(1)} copy-done((s32[64]{0:T(128)S(1)}, s32[64]{0:T(128)}, u32[]{:S(2)}) %copy-start.3) | copy-done | bytes 280
  13.6 4.3 %segment_sums.1.sums_ref = bf16[8,4,128,128]{3,2,1,0:T(8,128)(2,1)S(1)} custom-call(s32[64]{0:T(128)S(1)} %copy-done.3, bf16[64,4,128,128]{3,2,1,0:T(8,128)(2,1)} %tiles_hbm.1), custom_call_target="tpu_custom_call" | custom-call | flops 4194304 | bytes 8388608 | tf_op jit(solution)/shard_map/segment_sums/pallas_call | solution.py:172
  17.9 0.1 all-to-all-done.known_ref
  18.0 0.0 collective-permute-done.refs_0_
  18.0 0.0 collective-permute-done.1.refs_1_
  18.0 0.0 collective-permute-done.2.refs_2_
  18.0 0.0 copy-done.1
  18.0 0.4 pack.1
  18.4 0.0 copy-done
  18.5 0.7 %local_update.1 = (f32[4,32,128]{2,1,0:T(8,128)S(1)}, bf16[4,32,128]{2,1,0:T(8,128)(2,1)S(1)}) custom-call(bf16[4,2,64,128]{3,2,1,0:T(8,128)(2,1)S(1)} %all-to-all-done.known_ref, bf16[8,4,128,128]{3,2,1,0:T(8,128)(2,1)S(1)} %segment_sums.1.sums_ref, f32[4,64,128]{2,1,0:T(8,128)S(1)} %copy-done.2, f32[4,128,128]{2,1,0:T(8,128)S(1)} %copy-done), custom_call_target="tpu_custom_call" | custom-call | tf_op jit(solution)/shard_map/local_update/pallas_call | solution.py:217
  19.2 0.1 collective-permute-start.3
  19.3 1.2 %collective-permute-done.3 = bf16[4,32,128]{2,1,0:T(8,128)(2,1)S(1)} collective-permute-done((bf16[4,32,128]{2,1,0:T(8,128)(2,1)S(1)}, bf16[4,32,128]{2,1,0:T(8,128)(2,1)S(1)}, u32[]{:S(2)}, u32[]{:S(2)}) %collective-permute-start.3) | collective-permute-done | bytes 32800 | tf_op jit(solution)/shard_map/ppermute | solution.py:48
  20.5 1.5 %collective-permute-start.4 = (bf16[4,32,128]{2,1,0:T(8,128)(2,1)S(1)}, bf16[4,32,128]{2,1,0:T(8,128)(2,1)S(1)}, u32[]{:S(2)}, u32[]{:S(2)}) collective-permute-start(bf16[4,32,128]{2,1,0:T(8,128)(2,1)S(1)} %fusion), channel_id=1, source_target_pairs={{0,8},{1,9},{2,10},{3,11},{4,12},{5,13},{6,14},{7,15},{8,0},{9,1},... | collective-permute-start | bytes 98312 | tf_op jit(solution)/shard_map/ppermute | solution.py:48
  21.9 2.0 %collective-permute-start.7 = (bf16[12,128,128]{2,1,0:T(8,128)(2,1)S(1)}, bf16[12,128,128]{2,1,0:T(8,128)(2,1)S(1)}, u32[]{:S(2)}, u32[]{:S(2)}) collective-permute-start(bf16[12,128,128]{2,1,0:T(8,128)(2,1)S(1)} %get-tuple-element.30), channel_id=1, source_target_pairs={{0,1},{1,0},{2,3},{3,2},{4,5},{5,4},{6,7},{7,6},{8,9},{9,8},{10,11... | collective-permute-start | bytes 1179656 | tf_op jit(solution)/shard_map/ppermute | solution.py:48
  23.9 1.5 %collective-permute-start.11 = (bf16[12,128,128]{2,1,0:T(8,128)(2,1)S(1)}, bf16[12,128,128]{2,1,0:T(8,128)(2,1)S(1)}, u32[]{:S(2)}, u32[]{:S(2)}) collective-permute-start(bf16[12,128,128]{2,1,0:T(8,128)(2,1)S(1)} %get-tuple-element.30), channel_id=1, source_target_pairs={{0,2},{1,3},{2,0},{3,1},{4,6},{5,7},{6,4},{7,5},{8,10},{9,11},{10,... | collective-permute-start | bytes 1179656 | tf_op jit(solution)/shard_map/ppermute | solution.py:48
  25.4 0.0 collective-permute-done.4
  25.4 0.7 %collective-permute-start.5 = (bf16[4,32,128]{2,1,0:T(8,128)(2,1)S(1)}, bf16[4,32,128]{2,1,0:T(8,128)(2,1)S(1)}, u32[]{:S(2)}, u32[]{:S(2)}) collective-permute-start(bf16[4,32,128]{2,1,0:T(8,128)(2,1)S(1)} %fusion.1), channel_id=1, source_target_pairs={{0,0},{1,1},{2,2},{3,3},{4,4},{5,5},{6,6},{7,7},{8,16},{9,17},{10,... | collective-permute-start | bytes 98312 | tf_op jit(solution)/shard_map/ppermute | solution.py:48
  26.1 0.1 collective-permute-start.6
  26.1 2.0 %collective-permute-start.12 = (bf16[12,128,128]{2,1,0:T(8,128)(2,1)S(1)}, bf16[12,128,128]{2,1,0:T(8,128)(2,1)S(1)}, u32[]{:S(2)}, u32[]{:S(2)}) collective-permute-start(bf16[12,128,128]{2,1,0:T(8,128)(2,1)S(1)} %get-tuple-element.30), channel_id=1, source_target_pairs={{0,3},{1,2},{2,1},{3,0},{4,7},{5,6},{6,5},{7,4},{8,11},{9,10},{10,... | collective-permute-start | bytes 1179656 | tf_op jit(solution)/shard_map/ppermute | solution.py:48
  28.2 0.0 collective-permute-done.5
  28.2 0.0 collective-permute-done.6
  28.2 0.1 pad_maximum_fusion.4.cross_ref
  28.3 5.6 %collective-permute-done.7 = bf16[12,128,128]{2,1,0:T(8,128)(2,1)S(1)} collective-permute-done((bf16[12,128,128]{2,1,0:T(8,128)(2,1)S(1)}, bf16[12,128,128]{2,1,0:T(8,128)(2,1)S(1)}, u32[]{:S(2)}, u32[]{:S(2)}) %collective-permute-start.7) | collective-permute-done | bytes 393248 | tf_op jit(solution)/shard_map/ppermute | solution.py:48
  33.9 2.9 %collective-permute-start.10 = (bf16[2,32,128]{2,1,0:T(8,128)(2,1)S(1)}, bf16[2,32,128]{2,1,0:T(8,128)(2,1)S(1)}, u32[]{:S(2)}, u32[]{:S(2)}) collective-permute-start(bf16[2,32,128]{2,1,0:T(8,128)(2,1)S(1)} %slice.34), channel_id=1, source_target_pairs={{0,3},{1,2},{2,1},{3,0},{4,7},{5,6},{6,5},{7,4},{8,11},{9,10},{10,... | collective-permute-start | bytes 49160 | tf_op jit(solution)/shard_map/ppermute | solution.py:48
  36.8 0.6 collective-permute-start.9
  37.4 0.0 collective-permute-start.8
  37.4 6.0 %collective-permute-done.11 = bf16[12,128,128]{2,1,0:T(8,128)(2,1)S(1)} collective-permute-done((bf16[12,128,128]{2,1,0:T(8,128)(2,1)S(1)}, bf16[12,128,128]{2,1,0:T(8,128)(2,1)S(1)}, u32[]{:S(2)}, u32[]{:S(2)}) %collective-permute-start.11) | collective-permute-done | bytes 393248 | tf_op jit(solution)/shard_map/ppermute | solution.py:48
  43.4 0.1 pad_maximum_fusion.2
  43.5 0.1 fusion.2
  43.7 0.1 collective-permute-start.13
  43.7 0.0 collective-permute-done.12
  43.8 0.5 collective-permute-start.14
  44.3 0.1 maximum_bitcast_fusion
  44.4 0.1 pad_maximum_fusion.3
  44.5 0.0 collective-permute-done.10
  44.5 0.0 collective-permute-done.9
  44.5 0.0 collective-permute-done.8
  44.5 1.5 %collective-permute-done.14 = bf16[1,6,128,128]{3,2,1,0:T(8,128)(2,1)S(1)} collective-permute-done((bf16[1,6,128,128]{3,2,1,0:T(8,128)(2,1)S(1)}, bf16[1,6,128,128]{3,2,1,0:T(8,128)(2,1)S(1)}, u32[]{:S(2)}, u32[]{:S(2)}) %collective-permute-start.14) | collective-permute-done | bytes 196640 | tf_op jit(solution)/shard_map/ppermute | solution.py:48
  46.0 0.0 collective-permute-done.13
  46.0 0.1 maximum_bitcast_fusion.1
  46.1 0.1 pad_maximum_fusion.tiles_ref
  46.3 1.1 %upper_half.1 = (bf16[8,32,128]{2,1,0:T(8,128)(2,1)S(1)}, bf16[2,32,128]{2,1,0:T(8,128)(2,1)S(1)}) custom-call(bf16[4,2,32,128]{3,2,1,0:T(8,128)(2,1)S(1)} %pad_maximum_fusion.5.value_ref, f32[2,32,128]{2,1,0:T(8,128)S(1)} %slice.28.own_ref, bf16[2,4,6,128,128]{4,3,2,1,0:T(8,128)(2,1)S(1)} %pad_maximum_fusion.tiles_ref, ...), custom_call_target="tpu_custom_call" | custom-call | tf_op jit(solution)/shard_map/upper_half/pallas_call | solution.py:316
  47.4 0.2 collective-permute-start.18
  47.5 1.5 %collective-permute-start.17 = (bf16[2,32,128]{2,1,0:T(8,128)(2,1)S(1)}, bf16[2,32,128]{2,1,0:T(8,128)(2,1)S(1)}, u32[]{:S(2)}, u32[]{:S(2)}) collective-permute-start(bf16[2,32,128]{2,1,0:T(8,128)(2,1)S(1)} %get-tuple-element.32), channel_id=1, source_target_pairs={{0,3},{1,2},{2,1},{3,0},{4,7},{5,6},{6,5},{7,4},{8,11},{9,10},{10,... | collective-permute-start | bytes 49160 | tf_op jit(solution)/shard_map/ppermute | solution.py:48
  49.0 0.1 collective-permute-start.16
  49.1 1.9 %collective-permute-start.15 = (bf16[2,32,128]{2,1,0:T(8,128)(2,1)S(1)}, bf16[2,32,128]{2,1,0:T(8,128)(2,1)S(1)}, u32[]{:S(2)}, u32[]{:S(2)}) collective-permute-start(bf16[2,32,128]{2,1,0:T(8,128)(2,1)S(1)} %get-tuple-element.32), channel_id=1, source_target_pairs={{0,1},{1,0},{2,3},{3,2},{4,5},{5,4},{6,7},{7,6},{8,9},{9,8},{10,11... | collective-permute-start | bytes 49160 | tf_op jit(solution)/shard_map/ppermute | solution.py:48
  51.0 1.1 %collective-permute-done.17 = bf16[2,32,128]{2,1,0:T(8,128)(2,1)S(1)} collective-permute-done((bf16[2,32,128]{2,1,0:T(8,128)(2,1)S(1)}, bf16[2,32,128]{2,1,0:T(8,128)(2,1)S(1)}, u32[]{:S(2)}, u32[]{:S(2)}) %collective-permute-start.17) | collective-permute-done | bytes 16416 | tf_op jit(solution)/shard_map/ppermute | solution.py:48
  52.2 0.6 collective-permute-done.16
  52.8 0.1 collective-permute-done.15
  52.9 0.0 collective-permute-done.18
  52.9 0.1 pad_maximum_fusion.1.tiles_ref
  53.0 0.9 %lower_half.1 = bf16[4,32,128]{2,1,0:T(8,128)(2,1)S(1)} custom-call(bf16[4,2,32,128]{3,2,1,0:T(8,128)(2,1)S(1)} %pad_maximum_fusion.6.value_ref, bf16[8,32,128]{2,1,0:T(8,128)(2,1)S(1)} %get-tuple-element.33.upper_ref, bf16[2,4,6,128,128]{4,3,2,1,0:T(8,128)(2,1)S(1)} %pad_maximum_fusion.1.tiles_ref), custom_call_target="tpu_custom_call" | custom-call | tf_op jit(solution)/shard_map/lower_half/pallas_call | solution.py:316
  53.9 0.6 %collective-permute-start.19 = (bf16[4,32,128]{2,1,0:T(8,128)(2,1)S(1)}, bf16[4,32,128]{2,1,0:T(8,128)(2,1)S(1)}, u32[]{:S(2)}, u32[]{:S(2)}) collective-permute-start(bf16[4,32,128]{2,1,0:T(8,128)(2,1)S(1)} %lower_half.1), channel_id=1, source_target_pairs={{0,8},{1,9},{2,10},{3,11},{4,12},{5,13},{6,14},{7,15},{8,0},{9,1},... | collective-permute-start | bytes 98312 | tf_op jit(solution)/shard_map/ppermute | solution.py:48
  54.5 0.0 collective-permute-start.20
  54.5 1.5 %collective-permute-start.21 = (bf16[4,32,128]{2,1,0:T(8,128)(2,1)S(1)}, bf16[4,32,128]{2,1,0:T(8,128)(2,1)S(1)}, u32[]{:S(2)}, u32[]{:S(2)}) collective-permute-start(bf16[4,32,128]{2,1,0:T(8,128)(2,1)S(1)} %lower_half.1), channel_id=1, source_target_pairs={{0,4},{1,5},{2,6},{3,7},{4,0},{5,1},{6,2},{7,3},{8,12},{9,13},{10,... | collective-permute-start | bytes 98312 | tf_op jit(solution)/shard_map/ppermute | solution.py:48
  56.0 2.1 %collective-permute-done.19 = bf16[4,32,128]{2,1,0:T(8,128)(2,1)S(1)} collective-permute-done((bf16[4,32,128]{2,1,0:T(8,128)(2,1)S(1)}, bf16[4,32,128]{2,1,0:T(8,128)(2,1)S(1)}, u32[]{:S(2)}, u32[]{:S(2)}) %collective-permute-start.19) | collective-permute-done | bytes 32800 | tf_op jit(solution)/shard_map/ppermute | solution.py:48
  58.1 0.1 collective-permute-done.20
  58.2 0.0 collective-permute-done.21
  58.2 0.6 %pad_maximum_fusion.7 = bf16[4,64,128]{2,1,0:T(8,128)(2,1)} fusion(bf16[4,32,128]{2,1,0:T(8,128)(2,1)S(1)} %get-tuple-element.40, bf16[4,32,128]{2,1,0:T(8,128)(2,1)S(1)} %get-tuple-element.39), kind=kLoop, calls=%fused_computation.9 | loop fusion | flops 131072 | bytes 131072 | tf_op jit(solution)/shard_map/concatenate | solution.py:375
  (14 shorter events, 0.1 us)
Async XLA Ops:
  2.0 15.9 %collective-permute-start = (bf16[6,128,128]{2,1,0:T(8,128)(2,1)}, bf16[6,128,128]{2,1,0:T(8,128)(2,1)S(1)}, u32[]{:S(2)}, u32[]{:S(2)}) collective-permute-start(bf16[6,128,128]{2,1,0:T(8,128)(2,1)} %get-tuple-element.25.refs_3_), channel_id=1, source_target_pairs={{0,0},{1,1},{2,2},{3,3},{4,4},{5,5},{6,6},{7,7},{8,16},{9,17},{10,... | collective-permute-start | bytes 589832 | tf_op jit(solution)/shard_map/ppermute | solution.py:48
  3.6 14.4 %collective-permute-start.1 = (bf16[6,128,128]{2,1,0:T(8,128)(2,1)}, bf16[6,128,128]{2,1,0:T(8,128)(2,1)S(1)}, u32[]{:S(2)}, u32[]{:S(2)}) collective-permute-start(bf16[6,128,128]{2,1,0:T(8,128)(2,1)} %get-tuple-element.25.refs_3_), channel_id=1, source_target_pairs={{0,8},{1,9},{2,10},{3,11},{4,12},{5,13},{6,14},{7,15},{8,0},{9,1},... | collective-permute-start | bytes 589832 | tf_op jit(solution)/shard_map/ppermute | solution.py:48
  8.6 9.4 %collective-permute-start.2 = (bf16[6,128,128]{2,1,0:T(8,128)(2,1)}, bf16[6,128,128]{2,1,0:T(8,128)(2,1)S(1)}, u32[]{:S(2)}, u32[]{:S(2)}) collective-permute-start(bf16[6,128,128]{2,1,0:T(8,128)(2,1)} %get-tuple-element.25.refs_3_), channel_id=1, source_target_pairs={{0,16},{1,17},{2,18},{3,19},{4,20},{5,21},{6,22},{7,23},{8,0},{9,1... | collective-permute-start | bytes 589832 | tf_op jit(solution)/shard_map/ppermute | solution.py:48
  9.2 8.7 %all-to-all-start = ((bf16[4,2,64,128]{3,2,1,0:T(8,128)(2,1)}), bf16[4,2,64,128]{3,2,1,0:T(8,128)(2,1)S(1)}, u32[]{:S(2)}, u32[]{:S(2)}) async-start(bf16[4,2,64,128]{3,2,1,0:T(8,128)(2,1)} %get-tuple-element.20), calls=%async_computation | async-start | bytes 262144 | tf_op jit(solution)/shard_map/all_to_all | solution.py:339
  13.0 0.7 %copy-start.3 = (s32[64]{0:T(128)S(1)}, s32[64]{0:T(128)}, u32[]{:S(2)}) copy-start(s32[64]{0:T(128)} %index_ref.1) | copy-start | bytes 772
  13.6 4.4 %copy-start.1 = (bf16[6,128,128]{2,1,0:T(8,128)(2,1)S(1)}, bf16[6,128,128]{2,1,0:T(8,128)(2,1)}, u32[]{:S(2)}) copy-start(bf16[6,128,128]{2,1,0:T(8,128)(2,1)} %get-tuple-element.25.refs_3_) | copy-start | bytes 589828
  13.6 4.8 %copy-start = (f32[4,128,128]{2,1,0:T(8,128)S(1)}, f32[4,128,128]{2,1,0:T(8,128)}, u32[]{:S(2)}) copy-start(f32[4,128,128]{2,1,0:T(8,128)} %inverse_ref.1) | copy-start | bytes 786436
  13.6 4.8 %copy-start.2 = (f32[4,64,128]{2,1,0:T(8,128)S(1)}, f32[4,64,128]{2,1,0:T(8,128)}, u32[]{:S(2)}) copy-start(f32[4,64,128]{2,1,0:T(8,128)} %rhs_ref.1) | copy-start | bytes 393220
  19.2 1.3 %collective-permute-start.3 = (bf16[4,32,128]{2,1,0:T(8,128)(2,1)S(1)}, bf16[4,32,128]{2,1,0:T(8,128)(2,1)S(1)}, u32[]{:S(2)}, u32[]{:S(2)}) collective-permute-start(bf16[4,32,128]{2,1,0:T(8,128)(2,1)S(1)} %get-tuple-element.29), channel_id=1, source_target_pairs={{0,4},{1,5},{2,6},{3,7},{4,0},{5,1},{6,2},{7,3},{8,12},{9,13},{10,... | collective-permute-start | bytes 98312 | tf_op jit(solution)/shard_map/ppermute | solution.py:48
  20.5 4.9 %collective-permute-start.4 = (bf16[4,32,128]{2,1,0:T(8,128)(2,1)S(1)}, bf16[4,32,128]{2,1,0:T(8,128)(2,1)S(1)}, u32[]{:S(2)}, u32[]{:S(2)}) collective-permute-start(bf16[4,32,128]{2,1,0:T(8,128)(2,1)S(1)} %fusion), channel_id=1, source_target_pairs={{0,8},{1,9},{2,10},{3,11},{4,12},{5,13},{6,14},{7,15},{8,0},{9,1},... | collective-permute-start | bytes 98312 | tf_op jit(solution)/shard_map/ppermute | solution.py:48
  21.9 12.0 %collective-permute-start.7 = (bf16[12,128,128]{2,1,0:T(8,128)(2,1)S(1)}, bf16[12,128,128]{2,1,0:T(8,128)(2,1)S(1)}, u32[]{:S(2)}, u32[]{:S(2)}) collective-permute-start(bf16[12,128,128]{2,1,0:T(8,128)(2,1)S(1)} %get-tuple-element.30), channel_id=1, source_target_pairs={{0,1},{1,0},{2,3},{3,2},{4,5},{5,4},{6,7},{7,6},{8,9},{9,8},{10,11... | collective-permute-start | bytes 1179656 | tf_op jit(solution)/shard_map/ppermute | solution.py:48
  23.9 19.5 %collective-permute-start.11 = (bf16[12,128,128]{2,1,0:T(8,128)(2,1)S(1)}, bf16[12,128,128]{2,1,0:T(8,128)(2,1)S(1)}, u32[]{:S(2)}, u32[]{:S(2)}) collective-permute-start(bf16[12,128,128]{2,1,0:T(8,128)(2,1)S(1)} %get-tuple-element.30), channel_id=1, source_target_pairs={{0,2},{1,3},{2,0},{3,1},{4,6},{5,7},{6,4},{7,5},{8,10},{9,11},{10,... | collective-permute-start | bytes 1179656 | tf_op jit(solution)/shard_map/ppermute | solution.py:48
  25.4 2.8 %collective-permute-start.5 = (bf16[4,32,128]{2,1,0:T(8,128)(2,1)S(1)}, bf16[4,32,128]{2,1,0:T(8,128)(2,1)S(1)}, u32[]{:S(2)}, u32[]{:S(2)}) collective-permute-start(bf16[4,32,128]{2,1,0:T(8,128)(2,1)S(1)} %fusion.1), channel_id=1, source_target_pairs={{0,0},{1,1},{2,2},{3,3},{4,4},{5,5},{6,6},{7,7},{8,16},{9,17},{10,... | collective-permute-start | bytes 98312 | tf_op jit(solution)/shard_map/ppermute | solution.py:48
  26.1 2.1 %collective-permute-start.6 = (bf16[8,128,128]{2,1,0:T(8,128)(2,1)S(1)}, bf16[8,128,128]{2,1,0:T(8,128)(2,1)S(1)}, u32[]{:S(2)}, u32[]{:S(2)}) collective-permute-start(bf16[8,128,128]{2,1,0:T(8,128)(2,1)S(1)} %get-tuple-element.26), channel_id=1, source_target_pairs={{0,4},{1,5},{2,6},{3,7},{4,0},{5,1},{6,2},{7,3},{8,12},{9,13},{10,... | collective-permute-start | bytes 786440 | tf_op jit(solution)/shard_map/ppermute | solution.py:48
  26.1 17.6 %collective-permute-start.12 = (bf16[12,128,128]{2,1,0:T(8,128)(2,1)S(1)}, bf16[12,128,128]{2,1,0:T(8,128)(2,1)S(1)}, u32[]{:S(2)}, u32[]{:S(2)}) collective-permute-start(bf16[12,128,128]{2,1,0:T(8,128)(2,1)S(1)} %get-tuple-element.30), channel_id=1, source_target_pairs={{0,3},{1,2},{2,1},{3,0},{4,7},{5,6},{6,5},{7,4},{8,11},{9,10},{10,... | collective-permute-start | bytes 1179656 | tf_op jit(solution)/shard_map/ppermute | solution.py:48
  33.9 10.6 %collective-permute-start.10 = (bf16[2,32,128]{2,1,0:T(8,128)(2,1)S(1)}, bf16[2,32,128]{2,1,0:T(8,128)(2,1)S(1)}, u32[]{:S(2)}, u32[]{:S(2)}) collective-permute-start(bf16[2,32,128]{2,1,0:T(8,128)(2,1)S(1)} %slice.34), channel_id=1, source_target_pairs={{0,3},{1,2},{2,1},{3,0},{4,7},{5,6},{6,5},{7,4},{8,11},{9,10},{10,... | collective-permute-start | bytes 49160 | tf_op jit(solution)/shard_map/ppermute | solution.py:48
  36.8 7.7 %collective-permute-start.9 = (bf16[2,32,128]{2,1,0:T(8,128)(2,1)S(1)}, bf16[2,32,128]{2,1,0:T(8,128)(2,1)S(1)}, u32[]{:S(2)}, u32[]{:S(2)}) collective-permute-start(bf16[2,32,128]{2,1,0:T(8,128)(2,1)S(1)} %slice.34), channel_id=1, source_target_pairs={{0,2},{1,3},{2,0},{3,1},{4,6},{5,7},{6,4},{7,5},{8,10},{9,11},{10,... | collective-permute-start | bytes 49160 | tf_op jit(solution)/shard_map/ppermute | solution.py:48
  37.4 7.2 %collective-permute-start.8 = (bf16[2,32,128]{2,1,0:T(8,128)(2,1)S(1)}, bf16[2,32,128]{2,1,0:T(8,128)(2,1)S(1)}, u32[]{:S(2)}, u32[]{:S(2)}) collective-permute-start(bf16[2,32,128]{2,1,0:T(8,128)(2,1)S(1)} %slice.34), channel_id=1, source_target_pairs={{0,1},{1,0},{2,3},{3,2},{4,5},{5,4},{6,7},{7,6},{8,9},{9,8},{10,11... | collective-permute-start | bytes 49160 | tf_op jit(solution)/shard_map/ppermute | solution.py:48
  43.7 2.4 %collective-permute-start.13 = (bf16[3,6,128,128]{3,2,1,0:T(8,128)(2,1)S(1)}, bf16[3,6,128,128]{3,2,1,0:T(8,128)(2,1)S(1)}, u32[]{:S(2)}, u32[]{:S(2)}) collective-permute-start(bf16[3,6,128,128]{3,2,1,0:T(8,128)(2,1)S(1)} %get-tuple-element.36), channel_id=1, source_target_pairs={{0,4},{1,5},{2,6},{3,7},{4,0},{5,1},{6,2},{7,3},{8,12},{9,13},{10,... | collective-permute-start | bytes 1769480 | tf_op jit(solution)/shard_map/ppermute | solution.py:48
  43.8 2.2 %collective-permute-start.14 = (bf16[1,6,128,128]{3,2,1,0:T(8,128)(2,1)S(1)}, bf16[1,6,128,128]{3,2,1,0:T(8,128)(2,1)S(1)}, u32[]{:S(2)}, u32[]{:S(2)}) collective-permute-start(bf16[1,6,128,128]{3,2,1,0:T(8,128)(2,1)S(1)} %get-tuple-element.38), channel_id=1, source_target_pairs={{0,4},{1,5},{2,6},{3,7},{4,0},{5,1},{6,2},{7,3},{8,12},{9,13},{10,... | collective-permute-start | bytes 589832 | tf_op jit(solution)/shard_map/ppermute | solution.py:48
  47.4 5.5 %collective-permute-start.18 = (bf16[4,6,128,128]{3,2,1,0:T(8,128)(2,1)S(1)}, bf16[4,6,128,128]{3,2,1,0:T(8,128)(2,1)S(1)}, u32[]{:S(2)}, u32[]{:S(2)}) collective-permute-start(bf16[4,6,128,128]{3,2,1,0:T(8,128)(2,1)S(1)} %pad_maximum_fusion.3), channel_id=1, source_target_pairs={{0,4},{1,5},{2,6},{3,7},{4,0},{5,1},{6,2},{7,3},{8,12},{9,13},{10,... | collective-permute-start | bytes 2359304 | tf_op jit(solution)/shard_map/ppermute | solution.py:48
  47.5 4.7 %collective-permute-start.17 = (bf16[2,32,128]{2,1,0:T(8,128)(2,1)S(1)}, bf16[2,32,128]{2,1,0:T(8,128)(2,1)S(1)}, u32[]{:S(2)}, u32[]{:S(2)}) collective-permute-start(bf16[2,32,128]{2,1,0:T(8,128)(2,1)S(1)} %get-tuple-element.32), channel_id=1, source_target_pairs={{0,3},{1,2},{2,1},{3,0},{4,7},{5,6},{6,5},{7,4},{8,11},{9,10},{10,... | collective-permute-start | bytes 49160 | tf_op jit(solution)/shard_map/ppermute | solution.py:48
  49.0 3.7 %collective-permute-start.16 = (bf16[2,32,128]{2,1,0:T(8,128)(2,1)S(1)}, bf16[2,32,128]{2,1,0:T(8,128)(2,1)S(1)}, u32[]{:S(2)}, u32[]{:S(2)}) collective-permute-start(bf16[2,32,128]{2,1,0:T(8,128)(2,1)S(1)} %get-tuple-element.32), channel_id=1, source_target_pairs={{0,2},{1,3},{2,0},{3,1},{4,6},{5,7},{6,4},{7,5},{8,10},{9,11},{10,... | collective-permute-start | bytes 49160 | tf_op jit(solution)/shard_map/ppermute | solution.py:48
  49.1 3.7 %collective-permute-start.15 = (bf16[2,32,128]{2,1,0:T(8,128)(2,1)S(1)}, bf16[2,32,128]{2,1,0:T(8,128)(2,1)S(1)}, u32[]{:S(2)}, u32[]{:S(2)}) collective-permute-start(bf16[2,32,128]{2,1,0:T(8,128)(2,1)S(1)} %get-tuple-element.32), channel_id=1, source_target_pairs={{0,1},{1,0},{2,3},{3,2},{4,5},{5,4},{6,7},{7,6},{8,9},{9,8},{10,11... | collective-permute-start | bytes 49160 | tf_op jit(solution)/shard_map/ppermute | solution.py:48
  53.9 4.2 %collective-permute-start.19 = (bf16[4,32,128]{2,1,0:T(8,128)(2,1)S(1)}, bf16[4,32,128]{2,1,0:T(8,128)(2,1)S(1)}, u32[]{:S(2)}, u32[]{:S(2)}) collective-permute-start(bf16[4,32,128]{2,1,0:T(8,128)(2,1)S(1)} %lower_half.1), channel_id=1, source_target_pairs={{0,8},{1,9},{2,10},{3,11},{4,12},{5,13},{6,14},{7,15},{8,0},{9,1},... | collective-permute-start | bytes 98312 | tf_op jit(solution)/shard_map/ppermute | solution.py:48
  54.5 3.7 %collective-permute-start.20 = (bf16[4,32,128]{2,1,0:T(8,128)(2,1)S(1)}, bf16[4,32,128]{2,1,0:T(8,128)(2,1)S(1)}, u32[]{:S(2)}, u32[]{:S(2)}) collective-permute-start(bf16[4,32,128]{2,1,0:T(8,128)(2,1)S(1)} %lower_half.1), channel_id=1, source_target_pairs={{0,12},{1,13},{2,14},{3,15},{4,8},{5,9},{6,10},{7,11},{8,4},{9,5},... | collective-permute-start | bytes 98312 | tf_op jit(solution)/shard_map/ppermute | solution.py:48
  54.5 3.7 %collective-permute-start.21 = (bf16[4,32,128]{2,1,0:T(8,128)(2,1)S(1)}, bf16[4,32,128]{2,1,0:T(8,128)(2,1)S(1)}, u32[]{:S(2)}, u32[]{:S(2)}) collective-permute-start(bf16[4,32,128]{2,1,0:T(8,128)(2,1)S(1)} %lower_half.1), channel_id=1, source_target_pairs={{0,4},{1,5},{2,6},{3,7},{4,0},{5,1},{6,2},{7,3},{8,12},{9,13},{10,... | collective-permute-start | bytes 98312 | tf_op jit(solution)/shard_map/ppermute | solution.py:48
